TPU v7x, 32 devices: a whole 2x2x4 slice. The times are simulated.
32 devices in a mesh: rep: 4 (over x, core), shard: 8 (over z, y).
Axes of the slice: x: 2, y: 2, z: 4, core: 2. Of those that a mesh axis runs over, the one named last changes fastest.
Arguments:
- latents: bfloat16 [128, 16, 256], P(('rep', 'shard')), may hold values from -6 to 6
- target_noise: bfloat16 [128, 16, 256], P(('rep', 'shard')), may hold values from -6 to 6
- labels: int32 [128], P(('rep', 'shard')), may hold values from 0 to 15
- timesteps: int32 [128], P(('rep', 'shard')), may hold values from 0 to 999
- loss_weight: int32 [128], P(('rep', 'shard')), may hold values from 0 to 6, as said below
- layer_mats: float32 [2, 512, 4096], P(None, 'shard'), may hold values from -0.53033009 to 0.53033009
- layer_mats_first: float32 [2, 512, 4096], P(None, 'shard'), may hold values from -0.0024414062 to 0.0024414062
- layer_mats_second: float32 [2, 512, 4096], P(None, 'shard'), may hold values from 5.2083333e-09 to 8.333333e-08
- down_mats: float32 [2, 2048, 512], P(None, 'shard'), may hold values from -0.125 to 0.125
- down_first: float32 [2, 2048, 512], P(None, 'shard'), may hold values from -0.0024414062 to 0.0024414062
- down_second: float32 [2, 2048, 512], P(None, 'shard'), may hold values from 5.2083333e-09 to 8.333333e-08
- skip_mat: float32 [1024, 512], P('shard'), may hold values from -0.1875 to 0.1875
- skip_first: float32 [1024, 512], P('shard'), may hold values from -0.0024414062 to 0.0024414062
- skip_second: float32 [1024, 512], P('shard'), may hold values from 5.2083333e-09 to 8.333333e-08
- tables: float32 [306, 512], P(None, 'shard'), may hold values from -2 to 2
- tables_first: float32 [306, 512], P(None, 'shard'), may hold values from -0.0024414062 to 0.0024414062
- tables_second: float32 [306, 512], P(None, 'shard'), may hold values from 5.2083333e-09 to 8.333333e-08
- vectors: float32 [24, 512], P(None, 'shard'), may hold values from -1.2 to 1.3
- vectors_first: float32 [24, 512], P(None, 'shard'), may hold values from -0.0024414062 to 0.0024414062
- vectors_second: float32 [24, 512], P(None, 'shard'), may hold values from 5.2083333e-09 to 8.333333e-08
Outputs:
- loss_sum: float32 [], replicated
- weight_total: float32 [], replicated
- new_layer_first: float32 [2, 512, 4096], P(None, 'shard')
- new_layer_second: float32 [2, 512, 4096], P(None, 'shard')
- new_layer_mats: float32 [2, 512, 4096], P(None, 'shard')
- low_layer_mats: bfloat16 [2, 512, 4096], P(None, 'shard')
- new_down_first: float32 [2, 2048, 512], P(None, 'shard')
- new_down_second: float32 [2, 2048, 512], P(None, 'shard')
- new_down_mats: float32 [2, 2048, 512], P(None, 'shard')
- low_down_mats: bfloat16 [2, 2048, 512], P(None, 'shard')
- new_skip_first: float32 [1024, 512], P('shard')
- new_skip_second: float32 [1024, 512], P('shard')
- new_skip_mat: float32 [1024, 512], P('shard')
- low_skip_mat: bfloat16 [1024, 512], P('shard')
- new_tables_first: float32 [306, 512], P(None, 'shard')
- new_tables_second: float32 [306, 512], P(None, 'shard')
- new_tables: float32 [306, 512], P(None, 'shard')
- low_tables: bfloat16 [306, 512], P(None, 'shard')
- new_vectors_first: float32 [24, 512], P(None, 'shard')
- new_vectors_second: float32 [24, 512], P(None, 'shard')
- new_vectors: float32 [24, 512], P(None, 'shard')
- low_vectors: bfloat16 [24, 512], P(None, 'shard')
Inputs may be any that keep to these rules, and one draw needn't show every extreme that they name: `loss_weight`: zero marks a dummy sequence; some sequence has weight 6 in every draw.
All inputs are finite; a program needn't handle non-finite values.
Results may differ from a plain program's by a relative error of at most 0.018.
The roundings to bfloat16 on the way count: a program that leaves them out, or rounds other values in their place, can miss the bound.
Values may be sent and summed in bfloat16 or wider, within the bound.
No kernel may reach another device: no remote copies, remote signals or barrier semaphores. Data moves between devices by JAX's collectives and lax.ppermute only.
A program may use at most 256 MiB of HBM per device.

v0:
```python
import math

import jax
import jax.numpy as jnp
from jax import lax
from jax.sharding import PartitionSpec as P

D = 512
HEADS = 8
HD = 64
FF = 2048
CH = 16
NP = 256
CLASSES = 16
LAYERS = 2
STEP = 10
SEQ_LEN = 258


beta_one = 0.5
beta_two = 0.75
epsilon = 1e-08
weight_decay = 0.05
step_rates = (0.05, 0.03, 0.03, 0.05, 0.3)
HIGHEST_PREC = lax.Precision.HIGHEST


def norm_forward(stream, gain, shift):
    center = jnp.mean(stream, -1, keepdims=True)
    offset = stream - center
    spread = jnp.mean(offset * offset, -1, keepdims=True)
    return offset * lax.rsqrt(spread + 1e-05) * gain + shift


def norm_backward(stream, gain, shift, grad_out):
    _, pull_back = jax.vjp(norm_forward, stream, gain, shift)
    return pull_back(grad_out)


def time_token(timesteps):
    half_width = D // 2
    freqs_row = jnp.exp(-math.log(10000.0) * jnp.arange(half_width, dtype=jnp.float32) / half_width)
    angles = timesteps.astype(jnp.float32)[:, None] * freqs_row[None, :]
    return jnp.concatenate([jnp.cos(angles), jnp.sin(angles)], -1)


def layer_vectors(vectors, layer_id):
    per_layer = 6 + FF // D
    start = layer_id * per_layer
    return (vectors[start : start + 6], vectors[start + 6 : start + per_layer].reshape(FF))


def split_heads(packed):
    shaped = packed.reshape(packed.shape[0], packed.shape[1], 3, HEADS, HD)
    return (shaped[:, :, 0], shaped[:, :, 1], shaped[:, :, 2])


def layer_forward(stream, matrix, down_mat, layer_vec, fc1_bias):
    batch_seqs = stream.shape[0]
    normed = norm_forward(stream, layer_vec[0], layer_vec[1]).astype(jnp.bfloat16)
    packed = jnp.dot(normed, matrix[:, : 3 * D], preferred_element_type=jnp.float32).astype(
        jnp.bfloat16
    )
    queries, key_rows, values = split_heads(packed)
    scores = jnp.einsum(
        "bqhe,bkhe->bhqk", queries, key_rows, preferred_element_type=jnp.float32
    ) * HD ** (-0.5)
    row_max = jnp.max(scores, -1, keepdims=True)
    expon_rows = jnp.exp(scores - row_max)
    row_total = jnp.sum(expon_rows, -1, keepdims=True)
    log_total = row_max + jnp.log(row_total)
    attend_w = (expon_rows / row_total).astype(jnp.bfloat16)
    attended = jnp.einsum("bhqk,bkhe->bqhe", attend_w, values, preferred_element_type=jnp.float32)
    attended = attended.reshape(batch_seqs, SEQ_LEN, D).astype(jnp.bfloat16)
    middle = (
        stream
        + jnp.dot(attended, matrix[:, 3 * D : 4 * D], preferred_element_type=jnp.float32)
        + layer_vec[4]
    )
    normed_two = norm_forward(middle, layer_vec[2], layer_vec[3]).astype(jnp.bfloat16)
    hidden_pre = (
        jnp.dot(normed_two, matrix[:, 4 * D :], preferred_element_type=jnp.float32) + fc1_bias
    )
    hidden_act = jax.nn.gelu(hidden_pre).astype(jnp.bfloat16)
    result = (
        middle + jnp.dot(hidden_act, down_mat, preferred_element_type=jnp.float32) + layer_vec[5]
    )
    return (
        result,
        (stream, normed, packed, log_total, attended, middle, normed_two, hidden_pre, hidden_act),
    )


def layer_backward(grad_out, saved, matrix, down_mat, layer_vec):
    stream, normed, packed, log_total, attended, middle, normed_two, hidden_pre, hidden_act = saved
    batch_seqs = stream.shape[0]
    out_low = grad_out.astype(jnp.bfloat16)
    grad_down = jnp.einsum("bsf,bsd->fd", hidden_act, out_low, preferred_element_type=jnp.float32)
    grad_fc2b = jnp.sum(grad_out, (0, 1))
    grad_act = jnp.dot(out_low, down_mat.T, preferred_element_type=jnp.float32)
    _, gelu_pull = jax.vjp(jax.nn.gelu, hidden_pre)
    grad_pre = gelu_pull(grad_act)[0]
    grad_fc1b = jnp.sum(grad_pre, (0, 1))
    pre_low = grad_pre.astype(jnp.bfloat16)
    grad_fc1 = jnp.einsum("bsd,bsf->df", normed_two, pre_low, preferred_element_type=jnp.float32)
    grad_normed_two = jnp.dot(pre_low, matrix[:, 4 * D :].T, preferred_element_type=jnp.float32)
    grad_mid, grad_gain_two, grad_shift_two = norm_backward(
        middle, layer_vec[2], layer_vec[3], grad_normed_two
    )
    grad_mid = grad_mid + grad_out
    grad_projb = jnp.sum(grad_mid, (0, 1))
    mid_low = grad_mid.astype(jnp.bfloat16)
    grad_proj = jnp.einsum("bsd,bse->de", attended, mid_low, preferred_element_type=jnp.float32)
    grad_att = jnp.dot(mid_low, matrix[:, 3 * D : 4 * D].T, preferred_element_type=jnp.float32)
    grad_att = grad_att.astype(jnp.bfloat16).reshape(batch_seqs, SEQ_LEN, HEADS, HD)
    queries, key_rows, values = split_heads(packed)
    head_scale = HD ** (-0.5)
    scores = (
        jnp.einsum("bqhe,bkhe->bhqk", queries, key_rows, preferred_element_type=jnp.float32)
        * head_scale
    )
    attend_f = jnp.exp(scores - log_total)
    grad_values = jnp.einsum(
        "bhqk,bqhe->bkhe",
        attend_f.astype(jnp.bfloat16),
        grad_att,
        preferred_element_type=jnp.float32,
    )
    grad_attend = jnp.einsum(
        "bqhe,bkhe->bhqk", grad_att, values, preferred_element_type=jnp.float32
    )
    inner_sum = jnp.sum(attend_f * grad_attend, -1, keepdims=True)
    grad_scores = (attend_f * (grad_attend - inner_sum)).astype(jnp.bfloat16)
    grad_queries = (
        jnp.einsum("bhqk,bkhe->bqhe", grad_scores, key_rows, preferred_element_type=jnp.float32)
        * head_scale
    )
    grad_keys = (
        jnp.einsum("bhqk,bqhe->bkhe", grad_scores, queries, preferred_element_type=jnp.float32)
        * head_scale
    )
    grad_packed = jnp.concatenate(
        [
            grad_queries.reshape(batch_seqs, SEQ_LEN, D),
            grad_keys.reshape(batch_seqs, SEQ_LEN, D),
            grad_values.reshape(batch_seqs, SEQ_LEN, D),
        ],
        -1,
    ).astype(jnp.bfloat16)
    grad_qkv = jnp.einsum("bsd,bse->de", normed, grad_packed, preferred_element_type=jnp.float32)
    grad_normed = jnp.dot(grad_packed, matrix[:, : 3 * D].T, preferred_element_type=jnp.float32)
    grad_in, grad_gain_one, grad_shift_one = norm_backward(
        stream, layer_vec[0], layer_vec[1], grad_normed
    )
    grad_in = grad_in + grad_mid
    grad_matrix = jnp.concatenate([grad_qkv, grad_proj, grad_fc1], 1)
    grad_vec = jnp.stack(
        [grad_gain_one, grad_shift_one, grad_gain_two, grad_shift_two, grad_projb, grad_fc2b]
    )
    grad_vec = jnp.concatenate([grad_vec, grad_fc1b.reshape(FF // D, D)], 0)
    return (grad_in, grad_matrix, grad_down, grad_vec)


def unpack_weights(gathered):
    layer_mats, down_mats, skip_mat, tables, vectors = gathered
    vectors_f = vectors.astype(jnp.float32)
    tail_rows = vectors_f[LAYERS * (6 + FF // D) :]
    return (layer_mats, down_mats, skip_mat, tables, vectors_f, tail_rows)


def network_forward(gathered, latents, labels, timesteps):
    layer_mats, down_mats, skip_mat, tables, vectors_f, tail_rows = unpack_weights(gathered)
    patch_rows = (
        jnp.einsum("bcp,cd->bpd", latents, tables[:CH], preferred_element_type=jnp.float32)
        + tail_rows[3]
    )
    choose = (labels[:, None] == jnp.arange(CLASSES)[None, :]).astype(jnp.bfloat16)
    class_rows = jnp.dot(choose, tables[CH : CH + CLASSES], preferred_element_type=jnp.float32)
    stream = jnp.concatenate([time_token(timesteps)[:, None], class_rows[:, None], patch_rows], 1)
    stream = stream + tables[CH + CLASSES : CH + CLASSES + SEQ_LEN].astype(jnp.float32)
    embedded = stream
    joined = None
    saved_layers = []
    for layer_id in range(LAYERS):
        if layer_id == LAYERS // 2:
            joined = jnp.concatenate([stream, embedded], -1).astype(jnp.bfloat16)
            stream = jnp.dot(joined, skip_mat, preferred_element_type=jnp.float32) + tail_rows[2]
        layer_vec, fc1_bias = layer_vectors(vectors_f, layer_id)
        stream, saved_one = layer_forward(
            stream, layer_mats[layer_id], down_mats[layer_id], layer_vec, fc1_bias
        )
        saved_layers.append(saved_one)
    final_in = stream[:, 2:]
    final_norm = norm_forward(final_in, tail_rows[0], tail_rows[1]).astype(jnp.bfloat16)
    head_rows = tables[CH + CLASSES + SEQ_LEN :]
    prediction = jnp.einsum(
        "cd,bpd->bcp", head_rows, final_norm, preferred_element_type=jnp.float32
    )
    return (prediction, (saved_layers, joined, final_in, final_norm))


def network_backward(gathered, saved, grad_pred, latents, labels, finish_layer):
    layer_mats, down_mats, skip_mat, tables, vectors_f, tail_rows = unpack_weights(gathered)
    saved_layers, joined, final_in, final_norm = saved
    pred_low = grad_pred.astype(jnp.bfloat16)
    head_rows = tables[CH + CLASSES + SEQ_LEN :]
    grad_head = jnp.einsum("bcp,bpd->cd", pred_low, final_norm, preferred_element_type=jnp.float32)
    grad_final = jnp.einsum("bcp,cd->bpd", pred_low, head_rows, preferred_element_type=jnp.float32)
    grad_top, grad_final_gain, grad_final_shift = norm_backward(
        final_in, tail_rows[0], tail_rows[1], grad_final
    )
    grad_stream = jnp.pad(grad_top, ((0, 0), (2, 0), (0, 0)))
    grad_embed = jnp.zeros_like(grad_stream)
    grad_skip = None
    grad_skipb = None
    matrix_list = [None] * LAYERS
    down_list = [None] * LAYERS
    vec_list = [None] * LAYERS
    for layer_id in reversed(range(LAYERS)):
        layer_vec, fc1_bias = layer_vectors(vectors_f, layer_id)
        grad_stream, grad_matrix, grad_down, vec_list[layer_id] = layer_backward(
            grad_stream,
            saved_layers[layer_id],
            layer_mats[layer_id],
            down_mats[layer_id],
            layer_vec,
        )
        matrix_list[layer_id], down_list[layer_id] = finish_layer(grad_matrix, grad_down)
        if layer_id == LAYERS // 2:
            grad_skipb = jnp.sum(grad_stream, (0, 1))
            skip_low = grad_stream.astype(jnp.bfloat16)
            grad_skip = jnp.einsum(
                "bse,bsd->ed", joined, skip_low, preferred_element_type=jnp.float32
            )
            grad_joined = jnp.dot(skip_low, skip_mat.T, preferred_element_type=jnp.float32)
            grad_stream = grad_joined[..., :D]
            grad_embed = grad_joined[..., D:]
    grad_stream = grad_stream + grad_embed
    grad_pos = jnp.sum(grad_stream, 0)
    choose = (labels[:, None] == jnp.arange(CLASSES)[None, :]).astype(jnp.float32)
    grad_class = jnp.dot(choose.T, grad_stream[:, 1], precision=HIGHEST_PREC)
    grad_patch_rows = grad_stream[:, 2:]
    grad_patchb = jnp.sum(grad_patch_rows, (0, 1))
    grad_patch = jnp.einsum(
        "bcp,bpd->cd",
        latents,
        grad_patch_rows.astype(jnp.bfloat16),
        preferred_element_type=jnp.float32,
    )
    grad_tables = jnp.concatenate([grad_patch, grad_class, grad_pos, grad_head], 0)
    grad_tail = jnp.stack([grad_final_gain, grad_final_shift, grad_skipb, grad_patchb])
    grad_vectors = jnp.concatenate(vec_list + [grad_tail], 0)
    return (jnp.stack(matrix_list), jnp.stack(down_list), grad_skip, grad_tables, grad_vectors)


def keep_pair(grad_matrix, grad_down):
    return (grad_matrix, grad_down)


def adam_update(weight, grad, moment_one, moment_two, step_rate):
    moment_one = beta_one * moment_one + (1.0 - beta_one) * grad
    moment_two = beta_two * moment_two + (1.0 - beta_two) * grad * grad
    first_hat = moment_one / (1.0 - beta_one**STEP)
    second_hat = moment_two / (1.0 - beta_two**STEP)
    weight = weight - step_rate * (
        first_hat / (jnp.sqrt(second_hat) + epsilon) + weight_decay * weight
    )
    return (moment_one, moment_two, weight, weight.astype(jnp.bfloat16))


def local(
    latents,
    target_noise,
    labels,
    timesteps,
    loss_weight,
    layer_mats,
    layer_mats_first,
    layer_mats_second,
    down_mats,
    down_first,
    down_second,
    skip_mat,
    skip_first,
    skip_second,
    tables,
    tables_first,
    tables_second,
    vectors,
    vectors_first,
    vectors_second,
):
    mats_low = layer_mats.astype(jnp.bfloat16)
    down_low = down_mats.astype(jnp.bfloat16)
    skip_low = skip_mat.astype(jnp.bfloat16)
    tables_low = tables.astype(jnp.bfloat16)
    vectors_low = vectors.astype(jnp.bfloat16)
    gathered = (
        lax.all_gather(mats_low, "shard", axis=1, tiled=True),
        lax.all_gather(down_low, "shard", axis=1, tiled=True),
        lax.all_gather(skip_low, "shard", axis=0, tiled=True),
        lax.all_gather(tables_low, "shard", axis=1, tiled=True),
        lax.all_gather(vectors_low, "shard", axis=1, tiled=True),
    )
    prediction, saved = network_forward(gathered, latents, labels, timesteps)
    errors = prediction - target_noise.astype(jnp.float32)
    per_seq = jnp.mean(errors * errors, axis=(1, 2))
    seq_weight = loss_weight.astype(jnp.float32)
    loss_sum, weight_total = lax.psum(
        (jnp.sum(seq_weight * per_seq), jnp.sum(seq_weight)), ("rep", "shard")
    )
    inverse = 1.0 / weight_total
    grad_pred = (inverse * seq_weight)[:, None, None] * (2.0 / (CH * NP)) * errors
    back_weights = (
        lax.all_gather(mats_low, "shard", axis=1, tiled=True),
        lax.all_gather(down_low, "shard", axis=1, tiled=True),
        lax.all_gather(skip_low, "shard", axis=0, tiled=True),
        lax.all_gather(tables_low, "shard", axis=1, tiled=True),
        lax.all_gather(vectors_low, "shard", axis=1, tiled=True),
    )
    grads = network_backward(back_weights, saved, grad_pred, latents, labels, keep_pair)
    owned = (
        lax.psum_scatter(grads[0], "shard", scatter_dimension=1, tiled=True),
        lax.psum_scatter(grads[1], "shard", scatter_dimension=1, tiled=True),
        lax.psum_scatter(grads[2], "shard", scatter_dimension=0, tiled=True),
        lax.psum_scatter(grads[3], "shard", scatter_dimension=1, tiled=True),
        lax.psum_scatter(grads[4], "shard", scatter_dimension=1, tiled=True),
    )
    summed = (
        lax.psum(owned[0].astype(jnp.bfloat16), "rep").astype(jnp.float32),
        lax.psum(owned[1].astype(jnp.bfloat16), "rep").astype(jnp.float32),
        lax.psum(owned[2].astype(jnp.bfloat16), "rep").astype(jnp.float32),
        lax.psum(owned[3].astype(jnp.bfloat16), "rep").astype(jnp.float32),
        lax.psum(owned[4].astype(jnp.bfloat16), "rep").astype(jnp.float32),
    )
    masters = (layer_mats, down_mats, skip_mat, tables, vectors)
    firsts = (layer_mats_first, down_first, skip_first, tables_first, vectors_first)
    seconds = (layer_mats_second, down_second, skip_second, tables_second, vectors_second)
    results = [
        adam_update(masters[index], summed[index], firsts[index], seconds[index], step_rates[index])
        for index in range(5)
    ]
    return (
        loss_sum,
        weight_total,
        results[0][0],
        results[0][1],
        results[0][2],
        results[0][3],
        results[1][0],
        results[1][1],
        results[1][2],
        results[1][3],
        results[2][0],
        results[2][1],
        results[2][2],
        results[2][3],
        results[3][0],
        results[3][1],
        results[3][2],
        results[3][3],
        results[4][0],
        results[4][1],
        results[4][2],
        results[4][3],
    )


def solution(mesh):
    placed = (
        P(("rep", "shard"), None, None),
        P(("rep", "shard"), None, None),
        P(("rep", "shard")),
        P(("rep", "shard")),
        P(("rep", "shard")),
        P(None, "shard", None),
        P(None, "shard", None),
        P(None, "shard", None),
        P(None, "shard", None),
        P(None, "shard", None),
        P(None, "shard", None),
        P("shard", None),
        P("shard", None),
        P("shard", None),
        P(None, "shard"),
        P(None, "shard"),
        P(None, "shard"),
        P(None, "shard"),
        P(None, "shard"),
        P(None, "shard"),
    )
    return jax.shard_map(
        local,
        mesh=mesh,
        in_specs=placed,
        out_specs=(
            P(),
            P(),
            P(None, "shard", None),
            P(None, "shard", None),
            P(None, "shard", None),
            P(None, "shard", None),
            P(None, "shard", None),
            P(None, "shard", None),
            P(None, "shard", None),
            P(None, "shard", None),
            P("shard", None),
            P("shard", None),
            P("shard", None),
            P("shard", None),
            P(None, "shard"),
            P(None, "shard"),
            P(None, "shard"),
            P(None, "shard"),
            P(None, "shard"),
            P(None, "shard"),
            P(None, "shard"),
            P(None, "shard"),
        ),
        check_vma=False,
    )
```

profile of v0, /device:TPU:0, one launch (start us, length us, event | category | flops | bytes accessed | tf_op | source)
XLA Modules:
  0.0 1118.0 jit_solution(1226734070333204097)
XLA Ops:
  11.9 32.8 %all-gather = bf16[8,64,24]{1,2,0:T(8,128)(2,1)S(1)} all-gather(bf16[1,64,24]{1,2,0:T(8,128)(2,1)S(1)} %convert_bitcast_fusion), channel_id=1, replica_groups=mesh['rep'=4,'shard'=8] {'shard'}, dimensions={0}, use_global_device_ids=true | all-gather | bytes 27648 | tf_op jit(solution)/shard_map/all_gather | solution.py:303
  45.2 32.0 %all_gather.20 = bf16[306,512]{0,1:T(8,128)(2,1)S(1)} all-gather(bf16[306,64]{0,1:T(8,128)(2,1)S(1)} %convert_element_type.181), channel_id=1, replica_groups=mesh['rep'=4,'shard'=8] {'shard'}, dimensions={1}, use_global_device_ids=true | all-gather | bytes 352512 | tf_op jit(solution)/shard_map/all_gather | solution.py:302
  80.5 61.8 %all-gather.5.cloned.1.call-done = bf16[2,512,4096]{2,1,0:T(8,128)(2,1)} async-done(((bf16[2,64,4096]{2,1,0:T(8,128)(2,1)}), bf16[2,512,4096]{2,1,0:T(8,128)(2,1)}) %all-gather.5.cloned.1.call-update) | async-done | bytes 8388624 | tf_op jit(solution)/shard_map/all_gather | solution.py:299
  142.3 5.3 slice_bitcast_fusion.1
  149.6 3.8 convolution_convert_fusion.1
  153.4 6.3 copy.203
  159.8 4.4 multiply_reduce_fusion.3
  169.0 4.6 fusion.37
  176.3 6.0 fusion.44
  182.2 34.6 %all-gather.7.cloned.1.call-done = bf16[2,2048,512]{2,1,0:T(8,128)(2,1)} async-done(((bf16[2,256,512]{2,1,0:T(8,128)(2,1)}), bf16[2,2048,512]{2,1,0:T(8,128)(2,1)}) %all-gather.7.cloned.1.call-update) | async-done | bytes 4194320 | tf_op jit(solution)/shard_map/all_gather | solution.py:300
  216.8 9.5 add_convert_fusion.2
  226.3 31.7 %all-gather.9.cloned.1.call-done = bf16[1024,512]{1,0:T(8,128)(2,1)} async-done(((bf16[128,512]{1,0:T(8,128)(2,1)}), bf16[1024,512]{1,0:T(8,128)(2,1)}) %all-gather.9.cloned.1.call-update) | async-done | bytes 1048592 | tf_op jit(solution)/shard_map/all_gather | solution.py:301
  261.9 5.4 convolution_convert_fusion
  267.3 6.2 copy.209
  273.4 4.3 multiply_reduce_fusion.2
  282.5 4.6 fusion.36
  291.4 3.5 fusion.35
  297.4 38.5 %all-reduce.1 = (f32[]{:T(128)}, f32[]{:T(128)}) all-reduce(f32[]{:T(128)} %get-tuple-element.88, f32[]{:T(128)} %get-tuple-element.87), channel_id=1, replica_groups=mesh['rep'=4,'shard'=8] {'rep','shard'}, use_global_device_ids=true, to_apply=%region_16.0 | all-reduce | flops 2 | bytes 16 | tf_op jit(solution)/shard_map/psum | solution.py:309
  342.0 9.2 fusion.124
  351.2 3.3 fusion.100
  360.9 8.6 fusion.41
  369.6 9.6 multiply_reduce_fusion.1
  379.2 9.7 multiply_convert_fusion.1
  388.9 6.7 multiply_convert_fusion.6
  405.0 5.1 multiply_reduce_fusion.5
  419.0 9.8 convolution_bitcast_fusion.2
  428.9 4.8 convolution_bitcast_fusion.3
  433.8 4.2 pad_maximum_fusion.1
  438.1 11.3 %fusion.123 = (f32[2048]{0:T(1024)S(1)}, bf16[4,258,2048]{2,1,0:T(8,128)(2,1)S(1)}) fusion(f32[4,258,2048]{2,1,0:T(8,128)} %fusion.44, f32[2048]{0:T(1024)S(1)} %bitcast.347, bf16[2,2048,512]{2,1,0:T(8,128)(2,1)} %all-gather.7.cloned.1.call-done, f32[4,258,1024]{2,1,0:T(8,128)} %copy-done.25), kind=kOutput, calls=%fused_computation.271 | convolution fusion | flops 2210756608 | bytes 16072704 | tf_op jit(solution)/shard_map/dot_general | solution.py:100
  458.7 8.5 fusion.38
  468.9 14.7 %multiply_reduce_fusion = (f32[4,8,258]{2,1,0:T(8,128)S(1)}, f32[4,8,258,258]{2,3,1,0:T(8,128)}) fusion(f32[4,8,258,258]{2,3,1,0:T(8,128)} %copy-done.1, f32[4,8,258]{2,1,0:T(8,128)S(1)} %log_add_fusion.1, bf16[4,258,8,64]{1,3,2,0:T(8,128)(2,1)S(1)} %bitcast.279, bf16[4,258,3,8,64]{1,4,3,2,0:T(8,128)(2,1)} %bitcast.268), kind=kOutput, calls=%fused_computation.2 | convolution fusion | flops 281158080 | bytes 24192000 | tf_op jit(solution)/shard_map/bqhe,bkhe->bhqk/dot_general | solution.py:129
  483.6 6.9 multiply_convert_fusion
  490.5 4.3 multiply_convert_fusion.5
  496.3 7.0 multiply_convert_fusion.4
  506.4 3.4 convolution_bitcast_fusion.7
  512.5 4.0 convolution_bitcast_fusion.1
  516.7 4.1 convolution_bitcast_fusion
  524.1 4.9 convolution_bitcast_fusion.5
  528.9 9.7 maximum_bitcast_fusion
  538.6 11.7 %pad_maximum_fusion = f32[2,512,4096]{2,1,0:T(8,128)} fusion(f32[1,512,4096]{2,1,0:T(8,128)} %get-tuple-element.180, f32[1,512,4096]{2,1,0:T(8,128)} %get-tuple-element.179), kind=kLoop, calls=%fused_computation | loop fusion | flops 4194304 | bytes 33554432 | tf_op jit(solution)/shard_map/stack | solution.py:253
  551.1 4.4 fusion.102
  567.9 68.4 %reduce-scatter.12.cloned.1.call-done = f32[2,256,512]{2,1,0:T(8,128)} async-done(((f32[2,2048,512]{2,1,0:T(8,128)}), f32[2,256,512]{2,1,0:T(8,128)}) %reduce-scatter.12.cloned.1.call-update) | async-done | bytes 1048592 | tf_op jit(solution)/shard_map/reduce_scatter | solution.py:324
  638.4 283.0 %reduce-scatter.10.cloned.1.call-done = f32[2,64,4096]{2,1,0:T(8,128)} async-done(((f32[2,512,4096]{2,1,0:T(8,128)}), f32[2,64,4096]{2,1,0:T(8,128)}) %reduce-scatter.10.cloned.1.call-update) | async-done | bytes 2097168 | tf_op jit(solution)/shard_map/reduce_scatter | solution.py:323
  924.2 61.5 %reduce-scatter.18.cloned.1.call-done = f32[64,24]{1,0:T(8,128)} async-done(((f32[512,24]{1,0:T(8,128)}), f32[64,24]{1,0:T(8,128)}) %reduce-scatter.18.cloned.1.call-update) | async-done | bytes 6160
  987.1 64.0 %reduce-scatter.16.cloned.1.call-done = f32[64,306]{1,0:T(8,128)} async-done(((f32[512,306]{1,0:T(8,128)}), f32[64,306]{1,0:T(8,128)}) %reduce-scatter.16.cloned.1.call-update) | async-done | bytes 78352
  1052.6 12.4 %all-reduce.2 = (bf16[306,64]{0,1:T(8,128)(2,1)}, bf16[24,64]{1,0:T(8,128)(2,1)}) all-reduce(bf16[306,64]{0,1:T(8,128)(2,1)} %bitcast_convert_fusion, bf16[24,64]{1,0:T(8,128)(2,1)} %copy.254), channel_id=1, replica_groups=mesh['rep'=4,'shard'=8] {'rep'}, use_global_device_ids=true, to_apply=%region_39.40 | all-reduce | flops 21120 | bytes 84480 | tf_op jit(solution)/shard_map/psum | solution.py:333
  1068.2 31.3 %all-reduce.6.cloned.1.call-done = (bf16[2,64,4096]{2,1,0:T(8,128)(2,1)}, bf16[2,256,512]{2,1,0:T(8,128)(2,1)}, bf16[128,512]{1,0:T(8,128)(2,1)}) async-done(((bf16[2,64,4096]{2,1,0:T(8,128)(2,1)}, bf16[2,256,512]{2,1,0:T(8,128)(2,1)}, bf16[128,512]{1,0:T(8,128)(2,1)}), (bf16[2,64,4096]{2,1,0:T(8,128)(2,1)}, bf16[2,256,512]{2,1,0:T(8,128)(2,1)}, bf16[128,512]{1,0:T(8,128)(2,1)})) %all-reduce.6.cloned.1.call-update) | async-done | bytes 1703952 | tf_op jit(solution)/shard_map/psum | solution.py:330
  1106.2 5.1 fusion.114
  (432 shorter events, 114.4 us)
Async XLA Ops:
  7.2 70.7 %copy-start = (bf16[4,16,256]{2,1,0:T(8,128)(2,1)S(1)}, bf16[4,16,256]{2,1,0:T(8,128)(2,1)}, u32[]{:S(2)}) copy-start(bf16[4,16,256]{2,1,0:T(8,128)(2,1)} %param.20) | copy-start | bytes 98308
  7.2 135.1 %all-gather.5.cloned.1.call-start = ((), (), s32[]{:S(2)}) async-start(), calls=%async_computation.5 | async-start | bytes 9437184 | tf_op jit(solution)/shard_map/all_gather | solution.py:299
  10.0 34.8 %copy-start.125 = (s32[4]{0:T(128)S(1)}, s32[4]{0:T(128)}, u32[]{:S(2)}) copy-start(s32[4]{0:T(128)} %param.23) | copy-start | bytes 52
  10.0 35.1 %copy-start.59 = (f32[306,64]{0,1:T(8,128)S(1)}, f32[306,64]{0,1:T(8,128)}, u32[]{:S(2)}) copy-start(f32[306,64]{0,1:T(8,128)} %param.34) | copy-start | bytes 235012
  10.1 67.3 %copy-start.126 = (s32[4]{0:T(128)S(1)}, s32[4]{0:T(128)}, u32[]{:S(2)}) copy-start(s32[4]{0:T(128)} %param.22) | copy-start | bytes 52
  10.1 206.8 %all-gather.7.cloned.1.call-start = ((), (), s32[]{:S(2)}) async-start(), calls=%async_computation.6 | async-start | bytes 4718592 | tf_op jit(solution)/shard_map/all_gather | solution.py:300
  11.0 247.0 %all-gather.9.cloned.1.call-start = ((), (), s32[]{:S(2)}) async-start(), calls=%async_computation.7 | async-start | bytes 1179648 | tf_op jit(solution)/shard_map/all_gather | solution.py:301
  11.8 554.5 %reduce-scatter.14.cloned.1.call-start = ((), (), s32[]{:S(2)}) async-start(), calls=%async_computation.10 | async-start | bytes 2359296 | tf_op jit(solution)/shard_map/reduce_scatter | solution.py:325
  44.8 102.8 %copy-start.96 = (f32[1,512]{1,0:T(1,128)}, f32[1,512]{1,0:T(1,128)S(1)}, u32[]{:S(2)}) copy-start(f32[1,512]{1,0:T(1,128)S(1)} %get-tuple-element.147) | copy-start | bytes 6148
  44.9 102.8 %copy-start.115 = (f32[1,512]{1,0:T(1,128)}, f32[1,512]{1,0:T(1,128)S(1)}, u32[]{:S(2)}) copy-start(f32[1,512]{1,0:T(1,128)S(1)} %get-tuple-element.146) | copy-start | bytes 6148
  44.9 130.5 %copy-start.90 = (f32[1,512]{1,0:T(1,128)}, f32[1,512]{1,0:T(1,128)S(1)}, u32[]{:S(2)}) copy-start(f32[1,512]{1,0:T(1,128)S(1)} %get-tuple-element.144) | copy-start | bytes 6148
  44.9 130.4 %copy-start.109 = (f32[1,512]{1,0:T(1,128)}, f32[1,512]{1,0:T(1,128)S(1)}, u32[]{:S(2)}) copy-start(f32[1,512]{1,0:T(1,128)S(1)} %get-tuple-element.143) | copy-start | bytes 6148
  44.9 217.0 %copy-start.113 = (f32[1,512]{1,0:T(1,128)}, f32[1,512]{1,0:T(1,128)S(1)}, u32[]{:S(2)}) copy-start(f32[1,512]{1,0:T(1,128)S(1)} %get-tuple-element.139) | copy-start | bytes 6148
  44.9 243.9 %copy-start.111 = (f32[1,512]{1,0:T(1,128)}, f32[1,512]{1,0:T(1,128)S(1)}, u32[]{:S(2)}) copy-start(f32[1,512]{1,0:T(1,128)S(1)} %get-tuple-element.136) | copy-start | bytes 6148
  44.9 251.1 %copy-start.94 = (f32[1,512]{1,0:T(1,128)}, f32[1,512]{1,0:T(1,128)S(1)}, u32[]{:S(2)}) copy-start(f32[1,512]{1,0:T(1,128)S(1)} %get-tuple-element.134) | copy-start | bytes 6148
  44.9 294.8 %copy-start.73 = (f32[1,512]{1,0:T(1,128)}, f32[1,512]{1,0:T(1,128)S(1)}, u32[]{:S(2)}) copy-start(f32[1,512]{1,0:T(1,128)S(1)} %get-tuple-element.133) | copy-start | bytes 6148
  44.9 311.4 %copy-start.92 = (f32[1,512]{1,0:T(1,128)}, f32[1,512]{1,0:T(1,128)S(1)}, u32[]{:S(2)}) copy-start(f32[1,512]{1,0:T(1,128)S(1)} %get-tuple-element.137) | copy-start | bytes 6148
  45.1 295.4 %copy-start.106 = (f32[1,4,4,128]{3,1,2,0:T(4,128)}, f32[1,4,4,128]{3,1,2,0:T(4,128)S(1)}, u32[]{:S(2)}) copy-start(f32[1,4,4,128]{3,1,2,0:T(4,128)S(1)} %copy.266) | copy-start | bytes 24580
  45.1 171.7 %copy-start.104 = (f32[1,4,4,128]{3,1,2,0:T(4,128)}, f32[1,4,4,128]{3,1,2,0:T(4,128)S(1)}, u32[]{:S(2)}) copy-start(f32[1,4,4,128]{3,1,2,0:T(4,128)S(1)} %copy.265) | copy-start | bytes 24580
  78.8 94.9 %copy-start.7 = (f32[4,258,512]{2,1,0:T(8,128)}, f32[4,258,512]{2,1,0:T(8,128)S(1)}, u32[]{:S(2)}) copy-start(f32[4,258,512]{2,1,0:T(8,128)S(1)} %get-tuple-element.120) | copy-start | bytes 6340612
  78.8 68.9 %copy-start.67 = (f32[4,258]{1,0:T(4,128)}, f32[4,258]{1,0:T(4,128)S(1)}, u32[]{:S(2)}) copy-start(f32[4,258]{1,0:T(4,128)S(1)} %broadcast_multiply_fusion.3) | copy-start | bytes 12388
  80.5 67.1 %copy-start.81 = (f32[4,258]{1,0:T(4,128)}, f32[4,258]{1,0:T(4,128)S(1)}, u32[]{:S(2)}) copy-start(f32[4,258]{1,0:T(4,128)S(1)} %get-tuple-element.126) | copy-start | bytes 12388
  80.5 67.2 %copy-start.75 = (f32[4,258]{1,0:T(4,128)}, f32[4,258]{1,0:T(4,128)S(1)}, u32[]{:S(2)}) copy-start(f32[4,258]{1,0:T(4,128)S(1)} %fusion.81) | copy-start | bytes 12388
  261.3 25.8 %copy-start.21 = (f32[4,258,512]{2,1,0:T(8,128)}, f32[4,258,512]{2,1,0:T(8,128)S(1)}, u32[]{:S(2)}) copy-start(f32[4,258,512]{2,1,0:T(8,128)S(1)} %get-tuple-element.159) | copy-start | bytes 6340612
  288.3 68.0 %copy-start.71 = (f32[4,258]{1,0:T(4,128)}, f32[4,258]{1,0:T(4,128)S(1)}, u32[]{:S(2)}) copy-start(f32[4,258]{1,0:T(4,128)S(1)} %broadcast_multiply_fusion) | copy-start | bytes 12388
  288.8 67.5 %copy-start.79 = (f32[4,258]{1,0:T(4,128)}, f32[4,258]{1,0:T(4,128)S(1)}, u32[]{:S(2)}) copy-start(f32[4,258]{1,0:T(4,128)S(1)} %fusion.84) | copy-start | bytes 12388
  295.5 44.2 %copy-start.3 = (f32[4,256,512]{2,1,0:T(8,128)}, f32[4,256,512]{2,1,0:T(8,128)S(1)}, u32[]{:S(2)}) copy-start(f32[4,256,512]{2,1,0:T(8,128)S(1)} %get-tuple-element.118) | copy-start | bytes 6291460
  295.5 44.2 %copy-start.61 = (f32[4,256]{1,0:T(4,128)}, f32[4,256]{1,0:T(4,128)S(1)}, u32[]{:S(2)}) copy-start(f32[4,256]{1,0:T(4,128)S(1)} %broadcast_multiply_fusion.4) | copy-start | bytes 12292
  296.0 43.8 %copy-start.65 = (f32[4,256]{1,0:T(4,128)}, f32[4,256]{1,0:T(4,128)S(1)}, u32[]{:S(2)}) copy-start(f32[4,256]{1,0:T(4,128)S(1)} %fusion.85) | copy-start | bytes 12292
  296.8 41.3 %copy-start.54 = (f32[4,16,256]{2,1,0:T(8,128)}, f32[4,16,256]{2,1,0:T(8,128)S(1)}, u32[]{:S(2)}) copy-start(f32[4,16,256]{2,1,0:T(8,128)S(1)} %get-tuple-element.165) | copy-start | bytes 196612
  342.0 14.3 %copy-start.27 = (f32[4,256,512]{2,1,0:T(8,128)}, f32[4,256,512]{2,1,0:T(8,128)S(1)}, u32[]{:S(2)}) copy-start(f32[4,256,512]{2,1,0:T(8,128)S(1)} %broadcast_add_fusion) | copy-start | bytes 6291460
  360.9 18.2 %slice-start.4 = ((s8[12976128]{0:T(1024)(128)(4,1)}), s8[4194304]{0:T(1024)(128)(4,1)S(1)}, s32[]{:S(2)}) async-start(s8[12976128]{0:T(1024)(128)(4,1)} %bitcast.264), calls=%async_computation.18 | async-start | bytes 8388608
  360.9 18.2 %slice-start.5 = ((s8[12976128]{0:T(1024)(128)(4,1)}), s8[4194304]{0:T(1024)(128)(4,1)S(1)}, s32[]{:S(2)}) async-start(s8[12976128]{0:T(1024)(128)(4,1)} %bitcast.264), calls=%async_computation.19 | async-start | bytes 8388608
  416.2 220.1 %reduce-scatter.12.cloned.1.call-start = ((), (), s32[]{:S(2)}) async-start(), calls=%async_computation.9 | async-start | bytes 9437184 | tf_op jit(solution)/shard_map/reduce_scatter | solution.py:324
  438.0 483.4 %reduce-scatter.10.cloned.1.call-start = ((), (), s32[]{:S(2)}) async-start(), calls=%async_computation.8 | async-start | bytes 18874368 | tf_op jit(solution)/shard_map/reduce_scatter | solution.py:323
  467.2 16.4 %slice-start = ((s8[12976128]{0:T(1024)(128)(4,1)}), s8[393216]{0:T(1024)(128)(4,1)S(1)}, s32[]{:S(2)}) async-start(s8[12976128]{0:T(1024)(128)(4,1)} %bitcast.262), calls=%async_computation.14 | async-start | bytes 786432
  468.9 14.7 %slice-start.1 = ((s8[12976128]{0:T(1024)(128)(4,1)}), s8[4194304]{0:T(1024)(128)(4,1)S(1)}, s32[]{:S(2)}) async-start(s8[12976128]{0:T(1024)(128)(4,1)} %bitcast.262), calls=%async_computation.15 | async-start | bytes 8388608
  468.9 14.7 %slice-start.2 = ((s8[12976128]{0:T(1024)(128)(4,1)}), s8[4194304]{0:T(1024)(128)(4,1)S(1)}, s32[]{:S(2)}) async-start(s8[12976128]{0:T(1024)(128)(4,1)} %bitcast.262), calls=%async_computation.16 | async-start | bytes 8388608
  468.9 14.7 %slice-start.3 = ((s8[12976128]{0:T(1024)(128)(4,1)}), s8[4194304]{0:T(1024)(128)(4,1)S(1)}, s32[]{:S(2)}) async-start(s8[12976128]{0:T(1024)(128)(4,1)} %bitcast.262), calls=%async_computation.17 | async-start | bytes 8388608
  550.4 435.3 %reduce-scatter.18.cloned.1.call-start = ((), (), s32[]{:S(2)}) async-start(), calls=%async_computation.12 | async-start | bytes 294912
  564.9 486.2 %reduce-scatter.16.cloned.1.call-start = ((), (), s32[]{:S(2)}) async-start(), calls=%async_computation.11 | async-start | bytes 884736
  566.2 533.3 %all-reduce.6.cloned.1.call-start = ((), (), s32[]{:S(2)}) async-start(), calls=%async_computation.13 | async-start | bytes 3407872 | tf_op jit(solution)/shard_map/psum | solution.py:330
  638.4 426.6 %copy-start.86 = (f32[24,64]{1,0:T(8,128)S(1)}, f32[24,64]{1,0:T(8,128)}, u32[]{:S(2)}) copy-start(f32[24,64]{1,0:T(8,128)} %param.37) | copy-start | bytes 18436
  638.4 428.0 %copy-start.60 = (f32[306,64]{0,1:T(8,128)S(1)}, f32[306,64]{0,1:T(8,128)}, u32[]{:S(2)}) copy-start(f32[306,64]{0,1:T(8,128)} %param.34) | copy-start | bytes 235012
  638.4 461.1 %copy-start.53 = (f32[128,512]{1,0:T(8,128)S(1)}, f32[128,512]{1,0:T(8,128)}, u32[]{:S(2)}) copy-start(f32[128,512]{1,0:T(8,128)} %param.31) | copy-start | bytes 786436
  924.1 177.6 %copy-start.36 = (f32[2,256,512]{2,1,0:T(8,128)S(1)}, f32[2,256,512]{2,1,0:T(8,128)}, u32[]{:S(2)}) copy-start(f32[2,256,512]{2,1,0:T(8,128)} %param.28) | copy-start | bytes 3145732
  924.1 177.6 %copy-start.50 = (f32[2,256,512]{2,1,0:T(8,128)S(1)}, f32[2,256,512]{2,1,0:T(8,128)}, u32[]{:S(2)}) copy-start(f32[2,256,512]{2,1,0:T(8,128)} %param.29) | copy-start | bytes 3145732
  924.1 177.6 %copy-start.51 = (f32[2,256,512]{2,1,0:T(8,128)S(1)}, f32[2,256,512]{2,1,0:T(8,128)}, u32[]{:S(2)}) copy-start(f32[2,256,512]{2,1,0:T(8,128)} %param.30) | copy-start | bytes 3145732
  (111 other events, 464.5 us)
Sparse Core Ops, SparseCore 0:
  10.8 131.4 all-gather.4
  145.1 71.7 all-gather.6
  219.5 38.4 all-gather.8
  416.3 68.5 reduce-scatter.13
  488.4 147.8 reduce-scatter.11
  640.4 280.9 reduce-scatter.9
  925.4 60.2 reduce-scatter.17
  989.5 61.5 reduce-scatter.15
  1055.0 44.4 all-reduce.5
where the time goes:
time: 1120 us
  waiting for transfers between devices  636 us (57%)
  matrix products  201 us (18%)
  blocking collectives  116 us (10%)
  other arithmetic  93.4 us (8%)
  local copies, waits for them, and re-layouts  54.4 us (5%)
  between operations  16.7 us (1%)
    reduce_scatter x1, waiting for transfers between devices, local(): lax.psum_scatter(grads[0], 'shard', scatter_dimension=1, tiled=True)  283 us
    unnamed x11, waiting for transfers between devices  126 us
    reduce_scatter x1, waiting for transfers between devices, local(): lax.psum_scatter(grads[1], 'shard', scatter_dimension=1, tiled=True)  68.4 us
    all_gather x1, waiting for transfers between devices, local(): lax.all_gather(mats_low, 'shard', axis=1, tiled=True)  61.8 us
    psum x1, blocking collectives, local(): lax.psum((jnp.sum(seq_weight * per_seq), jnp.sum(seq_weight)), ('rep', 's...  38.5 us
    all_gather x1, waiting for transfers between devices, local(): lax.all_gather(down_low, 'shard', axis=1, tiled=True)  34.6 us
    all_gather x1, blocking collectives, local(): lax.all_gather(vectors_low, 'shard', axis=1, tiled=True)  32.8 us
    all_gather x1, blocking collectives, local(): lax.all_gather(tables_low, 'shard', axis=1, tiled=True)  32 us
  transfers between devices with their start and end apart: 9, of which 8 were waited for; matrix products, arithmetic and copies ran while one was open for 18% of the time, Pallas kernels for 0%

commit v1 on v0

v1 whole, which is shorter than its diff:
```python
import functools
import math

import jax
import jax.numpy as jnp
from jax import lax
from jax.experimental import pallas as pl
from jax.experimental.pallas import tpu as pltpu
from jax.sharding import PartitionSpec as P

D = 512
HEADS = 8
HD = 64
FF = 2048
CH = 16
NP = 256
CLASSES = 16
LAYERS = 2
STEP = 10
SEQ_LEN = 258

beta_one = 0.5
beta_two = 0.75
epsilon = 1e-08
weight_decay = 0.05
step_rates = (0.05, 0.03, 0.03, 0.05, 0.3)

TAIL = 16
T = NP + TAIL
ROW_PATCH = T
ROW_CLASS = ROW_PATCH + CH
ROW_HEAD = ROW_CLASS + CLASSES
ROW_VEC = ROW_HEAD + CH
N_VEC = LAYERS * (6 + FF // D) + 4
ROWS = D
ROW_WEIGHT = ROWS - 1
ROW_LOSS = 384
bf16 = jnp.bfloat16
f32 = jnp.float32
ALL = ("rep", "shard")
VMEM = pltpu.CompilerParams(vmem_limit_bytes=56 * 1024 * 1024)
ANY = pl.BlockSpec(memory_space=pl.ANY)
SMEM = pl.BlockSpec(memory_space=pltpu.SMEM)
WHOLE = pl.BlockSpec(memory_space=pltpu.VMEM)


class Part:
    def __init__(self, body, inputs, in_specs, outs, out_specs, scratch=()):
        self.body, self.inputs, self.in_specs = body, list(inputs), list(in_specs)
        self.outs, self.out_specs, self.scratch = list(outs), list(out_specs), list(scratch)


class Order:
    def __init__(self):
        self.last = None

    def __call__(self, kernel, inputs, in_specs, outs, out_specs, scratch=(), grid=(1,), name=None, aliases=None):
        part = Part(kernel, inputs, in_specs, outs, out_specs, scratch)
        return self.fuse([part], name, grid=grid, aliases=aliases)[0]

    def fuse(self, parts, name, after=(), grid=(1,), aliases=None):
        extra = list(after) + ([] if self.last is None else [self.last])
        inputs = [value for part in parts for value in part.inputs]
        counts = [(len(p.inputs), len(p.outs), len(p.scratch)) for p in parts]
        ends = [sum(c[i] for c in counts) for i in range(3)]
        skip = len(extra)

        def body(*refs):
            groups = (refs[: ends[0]], refs[ends[0] + skip : ends[0] + skip + ends[1]], refs[ends[0] + skip + ends[1] :])
            at = [0, 0, 0]
            rest = []
            for part, count in zip(parts, counts):
                own = [r for i in range(3) for r in groups[i][at[i] : at[i] + count[i]]]
                at = [i + n for i, n in zip(at, count)]
                more = part.body(*own)
                if more is not None:
                    next(more)
                    rest.append(more)
            for more in rest:
                next(more, None)

        result = pl.pallas_call(
            body,
            grid=grid,
            in_specs=[spec for part in parts for spec in part.in_specs] + [ANY] * skip,
            out_specs=[spec for part in parts for spec in part.out_specs],
            out_shape=[out for part in parts for out in part.outs],
            scratch_shapes=[item for part in parts for item in part.scratch],
            input_output_aliases=aliases or {},
            cost_estimate=pl.CostEstimate(flops=50_000_000_000, bytes_accessed=100_000_000, transcendentals=0),
            compiler_params=VMEM,
            name=name,
        )(*inputs, *extra)
        self.last = result[0]
        split, at = [], 0
        for part in parts:
            split.append(result[at : at + len(part.outs)])
            at += len(part.outs)
        return split


def dot(left, right):
    return jnp.dot(left, right, preferred_element_type=f32)


def dot_t(left, right):
    return lax.dot_general(left, right, (((1,), (1,)), ((), ())), preferred_element_type=f32)


def t_dot(left, right):
    return lax.dot_general(left, right, (((0,), (0,)), ((), ())), preferred_element_type=f32)


def norm_hat(stream):
    center = jnp.mean(stream, -1, keepdims=True)
    offset = stream - center
    spread = jnp.mean(offset * offset, -1, keepdims=True)
    inverse = lax.rsqrt(spread + 1e-05)
    return (offset * inverse, inverse)


def norm_back(hat, inverse, gain, grad):
    scaled = grad * gain
    first = jnp.mean(scaled, -1, keepdims=True)
    second = jnp.mean(scaled * hat, -1, keepdims=True)
    return inverse * (scaled - first - hat * second)


def rows_sum(values):
    return jnp.sum(values, 0, keepdims=True)


LSE = 16


def apart(rows, scale):
    lane = lax.broadcasted_iota(jnp.int32, (1, 2 * HD), 1)
    return jnp.concatenate([rows * jnp.where(lane // HD == e, scale, 0.0).astype(bf16) for e in range(2)], 0)


def block_mask():
    row = lax.broadcasted_iota(jnp.int32, (TAIL, D), 0)
    lane = lax.broadcasted_iota(jnp.int32, (TAIL, D), 1)
    return (row // 2 == lane // HD, row % 2 == 0)


def spread_tail(rows, scale):
    own, first = block_mask()
    wide = rows.astype(f32)
    both = jnp.where(first, wide[0:1], wide[1:2]) * scale
    return jnp.where(own, both, 0.0).astype(bf16)


def gather_tail(values):
    own, first = block_mask()
    kept = jnp.where(own, values, 0.0)
    zero = rows_sum(jnp.where(first, kept, 0.0))
    one = rows_sum(jnp.where(first, 0.0, kept))
    row = lax.broadcasted_iota(jnp.int32, (TAIL, D), 0)
    return jnp.where(row == 0, zero, jnp.where(row == 1, one, 0.0))


def mask_keys(scores):
    tail = scores[NP:]
    row = lax.broadcasted_iota(jnp.int32, tail.shape, 0)
    return jnp.concatenate([scores[:NP], jnp.where(row < SEQ_LEN - NP, tail, -1e30)], 0)


def softmax_rows(scores):
    top = jnp.max(scores, 0, keepdims=True)
    expon = jnp.exp(scores - top)
    total = jnp.sum(expon, 0, keepdims=True)
    return (expon * (1.0 / total)).astype(bf16), top + jnp.log(total)


def pipelined(count, *stages):
    held = {}
    for step in range(count + len(stages) - 1):
        for i, stage in enumerate(stages):
            if 0 <= step - i < count:
                held[step - i] = stage(step - i, held.get(step - i))


def attention_forward(stream, layer_id, vec_ref, wa_ref, h_ref, qkv_ref, lse_ref, o_ref, mid_ref):
    base = layer_id * (6 + FF // D)
    hat, _ = norm_hat(stream)
    normed = (hat * vec_ref[base : base + 1] + vec_ref[base + 1 : base + 2]).astype(bf16)
    h_ref[0] = normed
    qkv_ref[0] = dot(normed, wa_ref[:, : 3 * D]).astype(bf16)
    scale = HD**-0.5

    def cut(part, pair):
        return qkv_ref[0, :, part * D + 128 * pair : part * D + 128 * pair + 128]

    def score(pair, _):
        return dot_t(cut(1, pair), apart(cut(0, pair)[:NP], scale))

    def weigh(pair, scores):
        weights, log_total = softmax_rows(mask_keys(scores))
        lse_ref[0, 2 * pair : 2 * pair + 1] = log_total[:, :NP]
        lse_ref[0, 2 * pair + 1 : 2 * pair + 2] = log_total[:, NP:]
        return weights

    def mix(pair, weights):
        values = apart(cut(2, pair), 1.0)
        out = t_dot(weights[:, :NP], values[:T]) + t_dot(weights[:, NP:], values[T:])
        o_ref[0, :NP, 128 * pair : 128 * pair + 128] = out.astype(bf16)

    tails = spread_tail(qkv_ref[0, NP:, :D], scale)
    weights, log_total = softmax_rows(mask_keys(dot_t(qkv_ref[0, :, D : 2 * D], tails)))
    lse_ref[0, HEADS : HEADS + 1, :TAIL] = log_total
    o_ref[0, NP:] = gather_tail(t_dot(weights, qkv_ref[0, :, 2 * D :])).astype(bf16)
    pipelined(HEADS // 2, score, weigh, mix)
    mid_ref[0] = stream + dot(o_ref[0], wa_ref[:, 3 * D :]) + vec_ref[base + 4 : base + 5]


def embed_attention_kernel(
    label_ref, latent_ref, time_ref, tab_ref, vec_ref, wa_ref, x_ref, h_ref, qkv_ref, lse_ref, o_ref, mid_ref
):
    b = pl.program_id(0)
    patch_rows = t_dot(latent_ref[0], tab_ref[ROW_PATCH:ROW_CLASS]) + vec_ref[N_VEC - 1 : N_VEC]
    row = lax.broadcasted_iota(jnp.int32, (TAIL, CLASSES), 0)
    column = lax.broadcasted_iota(jnp.int32, (TAIL, CLASSES), 1)
    choose = jnp.where((row == 1) & (column == label_ref[b]), 1.0, 0.0).astype(bf16)
    tail_rows = time_ref[0] + dot(choose, tab_ref[ROW_CLASS:ROW_HEAD])
    stream = jnp.concatenate([patch_rows, tail_rows], 0) + tab_ref[:T].astype(f32)
    x_ref[0] = stream
    attention_forward(stream, 0, vec_ref, wa_ref, h_ref, qkv_ref, lse_ref, o_ref, mid_ref)


def skip_attention_kernel(x1_ref, x0_ref, ws_ref, vec_ref, wa_ref, x_ref, h_ref, qkv_ref, lse_ref, o_ref, mid_ref):
    one = x1_ref[0].astype(bf16)
    zero = x0_ref[0].astype(bf16)
    halves = [dot(one, ws_ref[i, :D]) + dot(zero, ws_ref[i, D:]) for i in range(2)]
    stream = jnp.concatenate(halves, 1) + vec_ref[N_VEC - 2 : N_VEC - 1]
    x_ref[0] = stream
    attention_forward(stream, 1, vec_ref, wa_ref, h_ref, qkv_ref, lse_ref, o_ref, mid_ref)


def mlp_forward(layer_id, mid_ref, vec_ref, w1_ref, w2_ref, h_ref, act_ref, slope_ref):
    base = layer_id * (6 + FF // D)
    hat, _ = norm_hat(mid_ref[...])
    normed = (hat * vec_ref[base + 2 : base + 3] + vec_ref[base + 3 : base + 4]).astype(bf16)
    h_ref[...] = normed
    const = math.sqrt(2.0 / math.pi)

    for j in range(FF // D):
        cols = slice(D * j, D * j + D)
        pre = dot(normed, w1_ref[:, cols]) + vec_ref[base + 6 + j : base + 7 + j]
        square = pre * pre
        half = 0.5 + 0.5 * jnp.tanh(pre * (const + (const * 0.044715) * square))
        act = pre * half
        act_ref[:, cols] = act.astype(bf16)
        slope = half + act * (1.0 - half) * (2.0 * const + (6.0 * const * 0.044715) * square)
        slope_ref[:, cols] = slope.astype(bf16)
    total = jnp.concatenate([dot(act_ref[...], w2_ref[i]) for i in range(2)], 1)
    return mid_ref[...] + total + vec_ref[base + 5 : base + 6]


def mlp_kernel(layer_id, mid_ref, vec_ref, w1_ref, w2_ref, h_ref, act_ref, slope_ref, out_ref):
    out_ref[...] = mlp_forward(layer_id, mid_ref, vec_ref, w1_ref, w2_ref, h_ref, act_ref, slope_ref)


def mlp_head_kernel(
    total_ref,
    weight_ref,
    mid_ref,
    vec_ref,
    w1_ref,
    w2_ref,
    noise_ref,
    tab_ref,
    h_ref,
    act_ref,
    slope_ref,
    dx_ref,
    dhead_ref,
    small_ref,
):
    b = pl.program_id(0)

    @pl.when(b == 0)
    def _():
        dhead_ref[...] = jnp.zeros_like(dhead_ref)
        small_ref[...] = jnp.zeros_like(small_ref)

    out = mlp_forward(1, mid_ref, vec_ref, w1_ref, w2_ref, h_ref, act_ref, slope_ref)
    hat, inverse = norm_hat(out[:NP])
    gain = vec_ref[N_VEC - 4 : N_VEC - 3]
    final = (hat * gain + vec_ref[N_VEC - 3 : N_VEC - 2]).astype(bf16)
    head = tab_ref[ROW_HEAD:ROW_VEC]
    errors = dot_t(head, final) - noise_ref[0].astype(f32)
    per_seq = jnp.sum(errors * errors) * (1.0 / (CH * NP))
    weight = weight_ref[b].astype(f32)
    scale = (jnp.ones((1, 1), f32) / total_ref[0, 0]) * weight * (2.0 / (CH * NP))
    grad_pred = (scale * errors).astype(bf16)
    dhead_ref[...] += dot(grad_pred, final)
    grad = t_dot(grad_pred, head)
    small_ref[0:1] += rows_sum(grad * hat)
    small_ref[1:2] += rows_sum(grad)
    small_ref[2:3] += jnp.full((1, D), weight * per_seq, f32)
    dx_ref[:NP] = norm_back(hat, inverse, gain, grad)
    dx_ref[NP:] = jnp.zeros((TAIL, D), f32)


def rows_of(b):
    return pl.ds(pl.multiple_of(T * b, TAIL), T)


def coords(c_ref):
    return tuple(c_ref[i] for i in range(4))


def place_of(c_ref, shard):
    _, _, z, y = coords(c_ref)
    return ((shard % 2) ^ y, (shard // 2 - z) & 3)


def sub_of(c_ref, h, t, g):
    x, c, _, _ = coords(c_ref)
    return 4 * (c ^ h) + 2 * t + (g ^ x)


def scatter_pieces(c_ref, keep_ref, send_ref, at, piece):
    for h, dest in ((0, keep_ref), (1, send_ref)):
        for t in range(2):
            for g in range(2):
                j = sub_of(c_ref, h, t, g)
                for s in range(8):
                    f, k = place_of(c_ref, s)
                    value = piece(j, s)
                    dest[t, g, f, k, at : at + value.shape[0]] = value


def by_columns(ref):
    return lambda j, s: ref[64 * s : 64 * s + 64, pl.ds(pl.multiple_of(256 * j, 256), 256)]


def by_rows(ref):
    return lambda j, s: ref[pl.ds(pl.multiple_of(64 * j, 64), 64), 256 * s : 256 * s + 256]


def mlp_backward_kernel(
    layer_id,
    c_ref,
    dout_ref,
    act_ref,
    slope_ref,
    h_ref,
    mid_ref,
    vec_ref,
    w1_ref,
    w2_ref,
    dmid_ref,
    keep_ref,
    send_ref,
    small_ref,
    dfc1b_ref,
    left_s,
    right_s,
    grads_s,
    acts_s,
    tile_s,
):
    b = pl.program_id(0)
    base = layer_id * (6 + FF // D)
    size = dout_ref.shape[0]

    @pl.when(b == 0)
    def _():
        small_ref[...] = jnp.zeros_like(small_ref)
        dfc1b_ref[...] = jnp.zeros_like(dfc1b_ref)

    dout = dout_ref[...]
    low = dout.astype(bf16)
    rows = pl.ds(pl.multiple_of(size * b, TAIL), size)
    left_s[rows] = h_ref[...]
    right_s[rows] = low
    acts_s[rows] = act_ref[...]

    def enter(j, _):
        block = slice(D * j, D * j + D)
        return dot_t(low[:, :256], w2_ref[0, block]) + dot_t(low[:, 256:], w2_ref[1, block])

    def bend(j, grad_act):
        cols = slice(D * j, D * j + D)
        grad_pre = grad_act * slope_ref[:, cols].astype(f32)
        dfc1b_ref[:, cols] += rows_sum(grad_pre)
        grad = grad_pre.astype(bf16)
        grads_s[rows, cols] = grad
        return grad

    total = []

    def leave(j, grad):
        part = dot_t(grad, w1_ref[:, D * j : D * j + D])
        total.append(part if not total else total[-1] + part)

    pipelined(FF // D, enter, bend, leave)
    grad_normed = total[-1]
    hat, inverse = norm_hat(mid_ref[...])
    small_ref[0:1] += rows_sum(grad_normed * hat)
    small_ref[1:2] += rows_sum(grad_normed)
    small_ref[2:3] += rows_sum(dout)
    dmid_ref[...] = dout + norm_back(hat, inverse, vec_ref[base + 2 : base + 3], grad_normed)

    @pl.when(b == pl.num_programs(0) - 1)
    def _():
        tile_s[...] = t_dot(left_s[...], grads_s[...]).astype(bf16)
        scatter_pieces(c_ref, keep_ref, send_ref, 0, by_columns(tile_s))
        tile_s[...] = t_dot(right_s[...], acts_s[...]).astype(bf16)
        scatter_pieces(c_ref, keep_ref, send_ref, 64, by_rows(tile_s))


def last_backward_kernel(
    layer_id,
    c_ref,
    dmid_ref,
    x_ref,
    h_ref,
    qkv_ref,
    lse_ref,
    o_ref,
    vec_ref,
    wa_ref,
    label_ref,
    d0_ref,
    latent_ref,
    dhead_ref,
    small_m0,
    small_m1,
    small_a1,
    small_head,
    dfc1b0,
    dfc1b1,
    keep_ref,
    send_ref,
    left_s,
    outs_s,
    grads_s,
    lows_s,
    dqkv_s,
    tile_s,
    small_ref,
    table_s,
):
    b = pl.program_id(0)

    @pl.when(b == 0)
    def _():
        table_s[...] = jnp.zeros_like(table_s)

    refs = (dmid_ref, x_ref, h_ref, qkv_ref, lse_ref, o_ref, vec_ref, wa_ref, small_ref, left_s, outs_s, grads_s, lows_s, dqkv_s)
    embed_grads(b, label_ref, attention_backward(layer_id, *refs) + d0_ref[0], latent_ref, table_s)

    @pl.when(b == pl.num_programs(0) - 1)
    def _():
        attention_weights(c_ref, keep_ref, send_ref, left_s, outs_s, grads_s, lows_s, tile_s)
        table_s[ROW_HEAD:ROW_VEC] = dhead_ref[...]
        row = ROW_VEC
        for own, mlp, fc1b in ((small_ref, small_m0, dfc1b0), (small_a1, small_m1, dfc1b1)):
            table_s[row : row + 2] = own[0:2]
            table_s[row + 2 : row + 4] = mlp[0:2]
            table_s[row + 4 : row + 5] = own[2:3]
            table_s[row + 5 : row + 6] = mlp[2:3]
            for i in range(FF // D):
                table_s[row + 6 + i : row + 7 + i] = fc1b[:, D * i : D * i + D]
            row += 6 + FF // D
        table_s[row : row + 2] = small_head[0:2]
        table_s[row + 2 : row + 3] = small_a1[3:4]
        table_pieces(c_ref, small_head[2:3, 0:1], table_s[...], keep_ref, send_ref, 64)


def attention_backward(
    layer_id, dmid_ref, x_ref, h_ref, qkv_ref, lse_ref, o_ref, vec_ref, wa_ref, small_ref, left_s, outs_s, grads_s, lows_s, dqkv_s
):
    b = pl.program_id(0)
    rows = rows_of(b)
    base = layer_id * (6 + FF // D)

    @pl.when(b == 0)
    def _():
        small_ref[...] = jnp.zeros_like(small_ref)

    dmid = dmid_ref[0]
    low = dmid.astype(bf16)
    left_s[rows] = h_ref[0]
    outs_s[rows] = o_ref[0]
    lows_s[rows] = low
    grad_att = dot_t(low, wa_ref[:, 3 * D :]).astype(bf16)
    scale = HD**-0.5

    def cut(part, pair):
        return qkv_ref[0, :, part * D + 128 * pair : part * D + 128 * pair + 128]

    def put(part, pair, value):
        dqkv_s[: value.shape[0], part * D + 128 * pair : part * D + 128 * pair + 128] = value.astype(bf16)

    tails, tail_douts = spread_tail(qkv_ref[0, NP:, :D], scale), spread_tail(grad_att[NP:], 1.0)
    weights = jnp.exp(mask_keys(dot_t(qkv_ref[0, :, D : 2 * D], tails)) - lse_ref[0, HEADS : HEADS + 1, :TAIL])
    grad_w = dot_t(qkv_ref[0, :, 2 * D :], tail_douts)
    grad_s = (weights * (grad_w - rows_sum(weights * grad_w))).astype(bf16)
    tail_dk = dot(grad_s, tails)
    tail_dv = dot(weights.astype(bf16), tail_douts)
    dqkv_s[NP:, :D] = (gather_tail(t_dot(grad_s, qkv_ref[0, :, D : 2 * D])) * scale).astype(bf16)

    def score(pair, _):
        queries = apart(cut(0, pair)[:NP], scale)
        douts = apart(grad_att[:NP, 128 * pair : 128 * pair + 128], 1.0)
        return dot_t(cut(1, pair), queries), dot_t(cut(2, pair), douts), queries, douts

    def weigh(pair, held):
        scores, grad_w, queries, douts = held
        log_total = jnp.concatenate([lse_ref[0, 2 * pair + e : 2 * pair + e + 1] for e in range(2)], 1)
        weights = jnp.exp(mask_keys(scores) - log_total)
        grad_s = weights * (grad_w - rows_sum(weights * grad_w))
        return weights.astype(bf16), grad_s.astype(bf16), queries, douts

    def mix(pair, held):
        weights, grad_s, queries, douts = held
        cols = slice(128 * pair, 128 * pair + 128)
        keys = apart(cut(1, pair), scale)
        put(0, pair, t_dot(grad_s[:, :NP], keys[:T]) + t_dot(grad_s[:, NP:], keys[T:]))
        put(1, pair, dot(grad_s, queries) + tail_dk[:, cols])
        put(2, pair, dot(weights, douts) + tail_dv[:, cols])

    pipelined(HEADS // 2, score, weigh, mix)
    grads_s[rows] = dqkv_s[...]
    grad_normed = dot_t(dqkv_s[...], wa_ref[:, : 3 * D])
    hat, inverse = norm_hat(x_ref[0])
    small_ref[0:1] += rows_sum(grad_normed * hat)
    small_ref[1:2] += rows_sum(grad_normed)
    small_ref[2:3] += rows_sum(dmid)
    return dmid + norm_back(hat, inverse, vec_ref[base : base + 1], grad_normed)


def attention_weights(c_ref, keep_ref, send_ref, left_s, outs_s, grads_s, lows_s, tile_s):
    tile_s[:, : 3 * D] = t_dot(left_s[...], grads_s[...]).astype(bf16)
    tile_s[:, 3 * D :] = t_dot(outs_s[...], lows_s[...]).astype(bf16)
    scatter_pieces(c_ref, keep_ref, send_ref, 0, by_columns(tile_s))


def middle_backward_kernel(
    layer_id,
    c_ref,
    dmid_ref,
    x_ref,
    h_ref,
    qkv_ref,
    lse_ref,
    o_ref,
    vec_ref,
    wa_ref,
    x1_ref,
    x0_ref,
    ws_ref,
    keep_ref,
    send_ref,
    d1_ref,
    d0_ref,
    small_ref,
    left_s,
    outs_s,
    grads_s,
    lows_s,
    dqkv_s,
    tile_s,
    both_s,
    skip_s,
    skip_tile_s,
):
    b = pl.program_id(0)
    refs = (dmid_ref, x_ref, h_ref, qkv_ref, lse_ref, o_ref, vec_ref, wa_ref, small_ref)
    grad = attention_backward(layer_id, *refs, left_s, outs_s, grads_s, lows_s, dqkv_s)
    low = grad.astype(bf16)
    small_ref[3:4] += rows_sum(grad)
    rows = rows_of(b)
    both_s[rows, :D] = x1_ref[0].astype(bf16)
    both_s[rows, D:] = x0_ref[0].astype(bf16)
    skip_s[rows] = low
    for u, dest in ((0, d1_ref), (1, d0_ref)):
        cols = slice(D * u, D * u + D)
        dest[0] = dot_t(low[:, :256], ws_ref[0, cols]) + dot_t(low[:, 256:], ws_ref[1, cols])

    @pl.when(b == pl.num_programs(0) - 1)
    def _():
        attention_weights(c_ref, keep_ref, send_ref, left_s, outs_s, grads_s, lows_s, tile_s)
        skip_tile_s[...] = t_dot(both_s[...], skip_s[...]).astype(bf16)
        for half in range(2):

            def piece(j, s, half=half):
                rows = pl.ds(pl.multiple_of(128 * s + 16 * j, 16), 16)
                return skip_tile_s[rows, 256 * half : 256 * half + 256]

            scatter_pieces(c_ref, keep_ref, send_ref, 64 + 16 * half, piece)


def embed_grads(b, label_ref, grad, latent_ref, table_s):
    table_s[:T] += grad
    patch = grad[:NP]
    last = ROW_VEC + N_VEC - 1
    table_s[last : last + 1] += rows_sum(patch)
    table_s[ROW_PATCH:ROW_CLASS] += dot(latent_ref[0], patch.astype(bf16))
    row = lax.broadcasted_iota(jnp.int32, (CLASSES, D), 0)
    table_s[ROW_CLASS:ROW_HEAD] += jnp.where(row == label_ref[b], grad[NP + 1 : NP + 2], 0.0)


def table_pieces(c_ref, loss, table, keep_ref, send_ref, at):
    x, c, z, y = coords(c_ref)
    me = (x * 2 + c) * 8 + z * 2 + y
    high = loss.astype(bf16).astype(f32)
    middle = (loss - high).astype(bf16).astype(f32)
    small = loss - high - middle
    row = lax.broadcasted_iota(jnp.int32, (ROWS, D), 0)
    kind = lax.broadcasted_iota(jnp.int32, (ROWS, D), 1) % 8
    slots = jnp.where(kind == 0, high, jnp.where(kind == 1, middle, jnp.where(kind == 2, small, 0.0)))
    turned = jnp.where(row == ROW_LOSS + me, slots, table).T
    for s in range(8):
        f, k = place_of(c_ref, s)
        for j in range(8):
            rows = slice(64 * s + 8 * j, 64 * s + 8 * j + 8)
            piece = jnp.concatenate([turned[rows, :256], turned[rows, 256:]], 0).astype(bf16)
            h, t, g = (j // 4) ^ c, j // 2 % 2, (j % 2) ^ x

            @pl.when(h == 0)
            def _(piece=piece, t=t, g=g, f=f, k=k):
                keep_ref[t, g, f, k, at : at + 16] = piece

            @pl.when(h == 1)
            def _(piece=piece, t=t, g=g, f=f, k=k):
                send_ref[t, g, f, k, at : at + 16] = piece


def per_seq(width, rows=T):
    return pl.BlockSpec((1, rows, width), lambda b: (b, 0, 0))


def fixed(shape):
    return pl.BlockSpec(shape, lambda b: (0,) * len(shape))


def shape_of(shape, dtype=f32):
    return jax.ShapeDtypeStruct(shape, dtype)


def pieces_shape(rows):
    return (2, 2, 2, 4, rows, 256)


def call_attention(order, first, n_seqs, inputs):
    shapes = [(T, D, f32), (T, D, bf16), (T, 3 * D, bf16), (LSE, NP, f32), (T, D, bf16), (T, D, f32)]
    vec_spec, wa_spec = fixed((N_VEC, D)), fixed((D, 4 * D))
    if first:
        in_specs = [SMEM, per_seq(NP, CH), per_seq(D, TAIL), fixed((ROWS, D)), vec_spec, wa_spec]
    else:
        in_specs = [per_seq(D), per_seq(D), fixed((2, 2 * D, D // 2)), vec_spec, wa_spec]
    return order(
        embed_attention_kernel if first else skip_attention_kernel,
        inputs,
        in_specs,
        [shape_of((n_seqs, r, w), d) for r, w, d in shapes],
        [per_seq(w, r) for r, w, _ in shapes],
        grid=(n_seqs,),
        name="attention_forward_%d" % (0 if first else 1),
    )


MLP_STEPS = 4


def flat(width, rows):
    return pl.BlockSpec((rows, width), lambda b: (b, 0))


def call_mlp(order, layer_id, n_seqs, mid, vec, w1, w2, head=None):
    shapes = [(D, bf16), (FF, bf16), (FF, bf16), (D, f32)]
    whole = n_seqs * T
    size = T if head else whole // MLP_STEPS
    inputs = [mid.reshape(whole, D), vec, w1, w2]
    specs = [flat(D, size), fixed((N_VEC, D)), fixed((D, FF)), fixed((2, FF, D // 2))]
    outs = [shape_of((whole, w), d) for w, d in shapes]
    out_specs = [flat(w, size) for w, _ in shapes]
    kernel = functools.partial(mlp_kernel, layer_id)
    if head:
        total, weights, noise, tab = head
        kernel = mlp_head_kernel
        inputs = [total, weights, *inputs, noise, tab]
        specs = [SMEM, SMEM, *specs, per_seq(NP, CH), fixed((ROWS, D))]
        outs += [shape_of((CH, D)), shape_of((8, D))]
        out_specs += [fixed((CH, D)), fixed((8, D))]
    out = order(kernel, inputs, specs, outs, out_specs, grid=(whole // size,), name="mlp_forward_%d" % layer_id)
    return [*out[:3], out[3].reshape(n_seqs, T, D), *out[4:]]


def call_mlp_backward(order, layer_id, n_seqs, place, dout, act, slope, normed, mid, vec, w1, w2):
    whole = n_seqs * T
    size = whole // MLP_STEPS
    pieces = pieces_shape(128)
    out = order(
        functools.partial(mlp_backward_kernel, layer_id),
        (place, dout.reshape(whole, D), act, slope, normed, mid.reshape(whole, D), vec, w1, w2),
        [SMEM, flat(D, size), flat(FF, size), flat(FF, size), flat(D, size), flat(D, size)]
        + [fixed((N_VEC, D)), fixed((D, FF)), fixed((2, FF, D // 2))],
        [shape_of((whole, D)), shape_of(pieces, bf16), shape_of(pieces, bf16), shape_of((8, D)), shape_of((1, FF))],
        [flat(D, size), fixed(pieces), fixed(pieces), fixed((8, D)), fixed((1, FF))],
        [
            pltpu.VMEM((whole, D), bf16),
            pltpu.VMEM((whole, D), bf16),
            pltpu.VMEM((whole, FF), bf16),
            pltpu.VMEM((whole, FF), bf16),
            pltpu.VMEM((D, FF), bf16),
        ],
        grid=(MLP_STEPS,),
        name="mlp_backward_%d" % layer_id,
    )
    return [out[0].reshape(n_seqs, T, D), *out[1:]]


def call_attention_backward(order, layer_id, n_seqs, place, dmid, x, normed, qkv, lse, att, vec, wa, more):
    whole = n_seqs * T
    pieces = pieces_shape(80 if layer_id == 0 else 96)
    specs = [SMEM, per_seq(D), per_seq(D), per_seq(D), per_seq(3 * D), per_seq(NP, LSE), per_seq(D)]
    specs += [fixed((N_VEC, D)), fixed((D, 4 * D))]
    scratch = [
        pltpu.VMEM((whole, D), bf16),
        pltpu.VMEM((whole, D), bf16),
        pltpu.VMEM((whole, 3 * D), bf16),
        pltpu.VMEM((whole, D), bf16),
        pltpu.VMEM((T, 3 * D), bf16),
        pltpu.VMEM((D, 4 * D), bf16),
    ]
    if layer_id == 1:
        kernel = middle_backward_kernel
        specs += [per_seq(D), per_seq(D), fixed((2, 2 * D, D // 2))]
        outs = [shape_of((n_seqs, T, D)), shape_of((n_seqs, T, D)), shape_of((8, D))]
        out_specs = [per_seq(D), per_seq(D), fixed((8, D))]
        scratch += [pltpu.VMEM((whole, 2 * D), bf16), pltpu.VMEM((whole, D), bf16), pltpu.VMEM((2 * D, D), bf16)]
    else:
        kernel = last_backward_kernel
        specs += [SMEM, per_seq(D), per_seq(NP, CH), fixed((CH, D))] + [fixed((8, D))] * 4 + [fixed((1, FF))] * 2
        scratch += [pltpu.VMEM((8, D), f32), pltpu.VMEM((ROWS, D), f32)]
        outs, out_specs = [], []
    return order(
        functools.partial(kernel, layer_id),
        [place, dmid, x, normed, qkv, lse, att, vec, wa, *more],
        specs,
        [shape_of(pieces, bf16), shape_of(pieces, bf16)] + outs,
        [fixed(pieces), fixed(pieces)] + out_specs,
        scratch,
        grid=(n_seqs,),
        name="attention_backward_%d" % layer_id,
    )


def device_id(x, c, z, y):
    return (x * 2 + c) * 8 + z * 2 + y


def pairs(move):
    every = [(x, c, z, y) for x in range(2) for c in range(2) for z in range(4) for y in range(2)]
    return [(device_id(*at), device_id(*move(*at))) for at in every]


TO_CORE = pairs(lambda x, c, z, y: (x, 1 - c, z, y))
TO_X = pairs(lambda x, c, z, y: (1 - x, c, z, y))
TO_Y = pairs(lambda x, c, z, y: (x, c, z, 1 - y))
TO_Z = [pairs(lambda x, c, z, y, k=k: (x, c, (z + k) % 4, y)) for k in range(4)]
PIECE_ROWS = {"a": 64, "m": 128, "s": 32, "t": 16}


def send(value, to):
    return lax.ppermute(value, ALL, to)


def rows_in(kinds):
    return sum(PIECE_ROWS[kind[0]] for kind in kinds)


def pack_kernel(kinds, c_ref, mats_ref, down_ref, skip_ref, tab_ref, vec_ref, weight_ref, u_ref, wide_s, narrow_s, sem):
    x, c, _, _ = coords(c_ref)
    copies, casts = [], []
    wide = narrow = row = 0
    for kind in kinds:
        l = int(kind[1:] or 0)
        if kind[0] in "am":
            for t in range(2):
                start = (2048 if kind[0] == "m" else 0) + 256 * (4 * c + 2 * t + x)
                copies.append((mats_ref.at[l, :, pl.ds(pl.multiple_of(start, 256), 256)], wide_s.at[wide]))
                casts.append((t, row, wide_s.at[wide], None))
                wide += 1
            row += 64
        if kind[0] in "ms":
            size = 32 if kind[0] == "m" else 16
            ref = down_ref.at[l] if kind[0] == "m" else skip_ref
            for t in range(2):
                start = pl.multiple_of(size * (4 * c + 2 * t + x), size)
                copies.append((ref.at[pl.ds(start, size)], narrow_s.at[narrow, :size]))
                for half in range(2):
                    cols = slice(256 * half, 256 * half + 256)
                    casts.append((t, row + size * half, narrow_s.at[narrow, :size], cols))
                narrow += 1
            row += 2 * size
        if kind[0] == "t":
            own_weight = weight_ref[0]
            for i in range(1, weight_ref.shape[0]):
                own_weight += weight_ref[i]
            turned = vec_ref[...].T
            first, last = CH + CLASSES, CH + CLASSES + SEQ_LEN
            corner = (lax.broadcasted_iota(jnp.int32, (16, 256), 0) == 8) & (
                lax.broadcasted_iota(jnp.int32, (16, 256), 1) == 255
            )
            for t in range(2):
                j = 4 * c + 2 * t + x
                table = tab_ref[pl.ds(pl.multiple_of(8 * j, 8), 8)]
                vecs = turned[0:8]
                for i in range(1, 8):
                    vecs = jnp.where(j == i, turned[8 * i : 8 * i + 8], vecs)
                rest = [
                    table[:, first : first + 2],
                    jnp.zeros((8, TAIL - 2), f32),
                    table[:, :first],
                    table[:, last:],
                    vecs,
                    jnp.zeros((8, ROWS - ROW_VEC - N_VEC), f32),
                ]
                piece = jnp.concatenate([table[:, first + 2 : last], jnp.concatenate(rest, 1)], 0)
                if t == 0:
                    piece = jnp.where(corner, own_weight.astype(f32), piece)
                u_ref[t, row : row + 16] = piece.astype(bf16)
            row += 16
    copies = [pltpu.make_async_copy(a, b, sem) for a, b in copies]
    for copy in copies:
        copy.start()
    yield
    for copy in copies:
        copy.wait()
    for t, at, ref, cols in casts:
        value = ref[...] if cols is None else ref[:, cols]
        u_ref[t, at : at + value.shape[0]] = value.astype(bf16)


def join_ring_kernel(u0, u1, u2, u3, b_ref, c_ref):
    for k, ref in enumerate((u0, u1, u2, u3)):
        b_ref[k] = ref[0]
        c_ref[k] = ref[1]


def join_pair_kernel(b0, b1, c0, c1, b_ref, c_ref):
    for i, (b, c) in enumerate(((b0, c0), (b1, c1))):
        b_ref[i] = b[...]
        c_ref[i] = c[...]


def join_own_kernel(b, c, both_ref):
    both_ref[0] = b[...]
    both_ref[1] = c[...]


def assemble_kernel(kinds, c_ref, *refs):
    x, c, z, y = coords(c_ref)
    sources, dests = refs[:7], refs[7:]
    for h in range(2):
        if h == 0:
            own_b, x_b, own_c, y_c = sources[:4]
        else:
            own_b, own_c, x_b, y_c = sources[4].at[0], sources[4].at[1], sources[5], sources[6]
        for t in range(2):
            for g in range(2):
                j = 4 * (c ^ h) + 2 * t + (g ^ x)
                cols = pl.ds(pl.multiple_of(256 * j, 256), 256)
                for f in range(2):
                    src = ((own_b, x_b)[g].at[f]) if t == 0 else ((own_c, y_c)[f].at[g])
                    for k in range(4):
                        s = 2 * ((z - k) & 3) + (y ^ f)
                        row = 0
                        at = 0
                        for kind in kinds:
                            if kind[0] in "am":
                                rows = pl.ds(pl.multiple_of(64 * s, 64), 64)
                                dests[at][rows, cols] = src[k, row : row + 64]
                                row, at = row + 64, at + 1
                            if kind[0] in "ms":
                                size = 32 if kind[0] == "m" else 16
                                rows = pl.ds(pl.multiple_of(size * (8 * s + j), size), size)
                                for half in range(2):
                                    dests[at][half, rows] = src[k, row : row + size]
                                    row += size
                                at += 1
                            if kind[0] == "t":
                                both = src[k, row : row + 16].astype(f32)
                                rows = pl.ds(pl.multiple_of(64 * s + 8 * j, 8), 8)
                                dests[-1][rows, :256] = both[:8]
                                dests[-1][rows, 256:] = both[8:]
    if "t" in kinds:
        table_ref, vec_ref, total_ref, turned_s = dests[-4:]
        table = turned_s[...].T
        table_ref[...] = table.astype(bf16)
        vec_ref[...] = table[ROW_VEC : ROW_VEC + N_VEC]
        total_ref[0, 0] = jnp.sum(table[ROW_WEIGHT : ROW_WEIGHT + 1])


class Gather:
    def __init__(self, place, kinds, sources):
        self.place, self.kinds, self.sources = place, kinds, sources
        self.rows = rows_in(kinds)

    def pack(self):
        return Part(
            functools.partial(pack_kernel, self.kinds),
            (self.place, *self.sources),
            [SMEM, ANY, ANY, ANY] + ([WHOLE, WHOLE, SMEM] if "t" in self.kinds else [ANY] * 3),
            [shape_of((2, self.rows, 256), bf16)],
            [WHOLE],
            [pltpu.VMEM((4, 64, 256), f32), pltpu.VMEM((4, 32, D), f32), pltpu.SemaphoreType.DMA],
        )

    def packed(self, results):
        (own,) = results
        self.ring = [own] + [send(own, TO_Z[k]) for k in range(1, 4)]

    def join_ring(self):
        half = shape_of((4, self.rows, 256), bf16)
        return Part(join_ring_kernel, self.ring, [WHOLE] * 4, [half] * 2, [WHOLE] * 2)

    def ring_joined(self, results):
        b, c = results
        self.halves = (b, send(b, TO_Y), c, send(c, TO_X))

    def join_pair(self):
        whole = shape_of((2, 4, self.rows, 256), bf16)
        return Part(join_pair_kernel, self.halves, [WHOLE] * 4, [whole, whole], [WHOLE] * 2)

    def pair_joined(self, results):
        b, c = results
        self.mine = [b, send(b, TO_X), c, send(c, TO_Y)]

    def join_own(self):
        both = shape_of((2, 2, 4, self.rows, 256), bf16)
        return Part(join_own_kernel, (self.mine[0], self.mine[2]), [WHOLE] * 2, [both], [WHOLE])

    def own_joined(self, results):
        self.other = [send(results[0], TO_CORE)]

    def rest_to_core(self):
        self.other += [send(self.mine[1], TO_CORE), send(self.mine[3], TO_CORE)]

    def assemble(self):
        shapes, scratch = [], []
        for kind in self.kinds:
            if kind[0] in "am":
                shapes.append(shape_of((D, 2048), bf16))
            if kind[0] == "m":
                shapes.append(shape_of((2, FF, 256), bf16))
            if kind[0] == "s":
                shapes.append(shape_of((2, 2 * D, 256), bf16))
            if kind[0] == "t":
                shapes += [shape_of((ROWS, D), bf16), shape_of((N_VEC, D)), shape_of((1, 1))]
                scratch = [pltpu.VMEM((D, ROWS), f32)]
        return Part(
            functools.partial(assemble_kernel, self.kinds),
            (self.place, *self.mine, *self.other),
            [SMEM] + [WHOLE] * 7,
            shapes,
            [SMEM if shape.shape == (1, 1) else WHOLE for shape in shapes],
            scratch,
        )


def added(*values):
    total = values[0].astype(f32)
    for value in values[1:]:
        total += value.astype(f32)
    return total.astype(bf16)


def add_core_kernel(n, *refs):
    keeps, gots, (b0_ref, b1_ref, c0_ref, c1_ref) = refs[:n], refs[n : 2 * n], refs[2 * n :]
    row = 0
    for keep, got in zip(keeps, gots):
        rows = slice(row, row + keep.shape[4])
        row = rows.stop
        for i in range(2):
            for dest, at in ((b0_ref, (0, 0, i)), (b1_ref, (0, 1, i)), (c0_ref, (1, i, 0)), (c1_ref, (1, i, 1))):
                dest[i, :, rows] = added(keep[at], got[at])


def add_both_kernel(b0_ref, gb_ref, c0_ref, gc_ref, b_ref, sb_ref, c_ref, sc_ref):
    for keep, got, dests in ((b0_ref, gb_ref, (b_ref, sb_ref)), (c0_ref, gc_ref, (c_ref, sc_ref))):
        for i, dest in enumerate(dests):
            dest[...] = added(keep[i], got[i])


def add_ring_kernel(b_ref, gb_ref, c_ref, gc_ref, *dests):
    for t, (keep, got) in enumerate(((b_ref, gb_ref), (c_ref, gc_ref))):
        for k, dest in enumerate(dests):
            dest[t] = added(keep[k], got[k])


def add_last_kernel(*refs):
    row = 0
    for i in range(0, len(refs) - 1, 4):
        rows = slice(row, row + refs[i].shape[1])
        row = rows.stop
        refs[-1][:, rows] = added(*(ref[...] for ref in refs[i : i + 4]))


class Reduce:
    def __init__(self, kinds):
        self.kinds = kinds
        self.rows = rows_in(kinds)
        self.keep, self.got = [], []

    def start(self, keep, give):
        self.keep.append(keep)
        self.got.append(send(give, TO_CORE))

    def core(self):
        def six(rows):
            return pl.BlockSpec((2, 2, 2, 1, rows, 256), lambda k: (0, 0, 0, k, 0, 0))

        four = pl.BlockSpec((2, 1, self.rows, 256), lambda k: (0, k, 0, 0))
        parts = self.keep + self.got
        return Part(
            functools.partial(add_core_kernel, len(self.keep)),
            parts,
            [six(part.shape[4]) for part in parts],
            [shape_of((2, 4, self.rows, 256), bf16)] * 4,
            [four] * 4,
        )

    def core_added(self, results):
        b0, b1, c0, c1 = results
        self.parts = (b0, send(b1, TO_X), c0, send(c1, TO_Y))

    def both(self):
        four = pl.BlockSpec((2, 1, self.rows, 256), lambda k: (0, k, 0, 0))
        three = pl.BlockSpec((1, self.rows, 256), lambda k: (k, 0, 0))
        return Part(
            add_both_kernel, self.parts, [four] * 4, [shape_of((4, self.rows, 256), bf16)] * 4, [three] * 4
        )

    def both_added(self, results):
        b, sb, c, sc = results
        self.parts = (b, send(sb, TO_Y), c, send(sc, TO_X))

    def ring(self):
        small = shape_of((2, self.rows, 256), bf16)
        return Part(add_ring_kernel, self.parts, [WHOLE] * 4, [small] * 4, [WHOLE] * 4)

    def ring_added(self, results):
        self.parts = [results[0]] + [send(results[k], TO_Z[k]) for k in range(1, 4)]


class Owned:
    def __init__(self, *chunks):
        self.chunks = chunks
        self.kinds = [kind for chunk in chunks for kind in chunk.kinds]

    def last(self):
        parts = [part for chunk in self.chunks for part in chunk.parts]
        out = shape_of((2, rows_in(self.kinds), 256), bf16)
        return Part(add_last_kernel, parts, [WHOLE] * len(parts), [out], [WHOLE])

    def last_added(self, results):
        (mine,) = results
        near = send(mine, TO_X)
        self.parts = (mine, near, send(mine, TO_CORE), send(near, TO_CORE))

    def adam(self, order, place, states, bufs, name):
        inputs, in_specs, outs, out_specs, aliases = [place, *self.parts], [SMEM] + [WHOLE] * 4, [], [], {}
        targets = []
        for kind in self.kinds:
            l = int(kind[1:] or 0)
            if kind[0] == "a":
                targets.append(("mats", "a", pl.BlockSpec((1, 64, 4096), lambda i, l=l: (l, 0, 0))))
            if kind[0] == "m":
                targets.append(("down", "d", pl.BlockSpec((1, 256, D), lambda i, l=l: (l, 0, 0))))
            if kind[0] == "s":
                targets.append(("skip", "s", fixed((128, D))))
            if kind[0] == "t":
                targets.append(("tables", "t", fixed((64, SEQ_LEN + 3 * CH))))
                targets.append(("vectors", "v", fixed((N_VEC, 64))))
        held = []
        for name, _, spec in targets:
            inputs += list(states[name])
            in_specs += [spec] * 3
            weight = states[name][0]
            if bufs.get(name) is not None:
                held += [(len(outs) + i, buf) for i, buf in enumerate(bufs[name])]
            outs += [shape_of(weight.shape)] * 3 + [shape_of(weight.shape, bf16)]
            out_specs += [spec] * 4
        n_read = len(inputs)
        for at, buf in held:
            aliases[len(inputs)] = at
            inputs.append(buf)
            in_specs.append(ANY)
        scratch = []
        if any(t[1] == "d" for t in targets):
            scratch.append(pltpu.VMEM((D, 256), f32))
        if any(t[1] == "t" for t in targets):
            scratch.append(pltpu.VMEM((64, ROWS), f32))
            outs.append(shape_of((1, 1)))
            out_specs.append(SMEM)
        result = order(
            functools.partial(adam_kernel, self.kinds, [t[1] for t in targets], n_read, len(inputs)),
            inputs,
            in_specs,
            outs,
            out_specs,
            scratch,
            name=name,
            aliases=aliases,
        )
        for i, (name, _, _) in enumerate(targets):
            bufs[name] = result[4 * i : 4 * i + 4]
        return result[4 * len(targets) :]


def adam_kernel(kinds, targets, n_read, n_in, c_ref, *refs):
    x, c, _, _ = coords(c_ref)
    parts, ins, outs = refs[:4], refs[4 : n_read - 1], refs[n_in - 1 :]
    scratch = list(outs[4 * len(targets) :])
    loss_ref = scratch.pop(0) if "t" in targets else None
    offsets, row = {}, 0
    for kind in kinds:
        offsets[kind[0]] = row
        row += PIECE_ROWS[kind[0]]
    pieces = []
    for h in range(2):
        for g in range(2):
            for t in range(2):
                pieces.append((4 * (c ^ h) + 2 * t + (g ^ x), parts[2 * h + g].at[t]))
    for i, kind in enumerate(targets):
        state, dests = ins[3 * i : 3 * i + 3], outs[4 * i : 4 * i + 4]
        row = offsets[{"d": "m", "v": "t"}.get(kind, kind)]

        def update(at, grad, rate, state=state, dests=dests):
            weight, first, second = (ref[at] for ref in state)
            values = adam_update(weight, grad, first, second, rate)
            for dest, value in zip(dests, values):
                dest[at] = value

        if kind == "a":
            for at_row, start in ((row, 0), (offsets["m"], 2048)):
                for j, piece in pieces:
                    at = (0, slice(None), pl.ds(pl.multiple_of(start + 256 * j, 256), 256))
                    update(at, piece[at_row : at_row + 64], step_rates[0])
        if kind == "d":
            held = scratch[0]
            for j, piece in pieces:
                held[pl.ds(pl.multiple_of(64 * j, 64), 64)] = piece[row + 64 : row + 128].astype(f32)
            update((0,), held[...].T, step_rates[1])
        if kind == "s":
            for j, piece in pieces:
                for half in range(2):
                    at = (pl.ds(pl.multiple_of(16 * j, 16), 16), slice(256 * half, 256 * half + 256))
                    update(at, piece[row + 16 * half : row + 16 * half + 16], step_rates[2])
        if kind == "t":
            held = scratch[-1]
            for j, piece in pieces:
                both = piece[row : row + 16].astype(f32)
                rows = pl.ds(pl.multiple_of(8 * j, 8), 8)
                held[rows, :256] = both[:8]
                held[rows, 256:] = both[8:]
            grad = held[...]
            parts_of = [grad[:, ROW_PATCH:ROW_HEAD], grad[:, NP : NP + 2], grad[:, :NP], grad[:, ROW_HEAD:ROW_VEC]]
            update(slice(None), jnp.concatenate(parts_of, 1), step_rates[3])
            loss_ref[0, 0] = jnp.sum(grad[0:3, ROW_LOSS : ROW_LOSS + 32])
        if kind == "v":
            grad = scratch[-1][:, ROW_VEC : ROW_VEC + N_VEC].T
            update(slice(None), grad, step_rates[4])


def gather_any(mats, down, skip, tables, vectors):
    first, last = CH + CLASSES, CH + CLASSES + SEQ_LEN
    width = tables.shape[1]
    tab = jnp.concatenate(
        [
            tables[first + 2 : last],
            tables[first : first + 2],
            jnp.zeros((TAIL - 2, width), f32),
            tables[:first],
            tables[last:],
            vectors,
            jnp.zeros((ROWS - ROW_VEC - N_VEC, width), f32),
        ]
    )
    every = lax.all_gather(mats.astype(bf16), "shard", axis=1, tiled=True)
    downs = lax.all_gather(down.astype(bf16), "shard", axis=1, tiled=True)
    skips = lax.all_gather(skip.astype(bf16), "shard", axis=0, tiled=True)
    table = lax.all_gather(tab.astype(bf16), "shard", axis=1, tiled=True)

    def halves(m):
        return jnp.stack([m[:, : D // 2], m[:, D // 2 :]])

    mats_of = [(every[l, :, :2048], every[l, :, 2048:]) for l in range(LAYERS)]
    return (mats_of, [halves(downs[l]) for l in range(LAYERS)], halves(skips), table)


def reduce_any(grads):
    def ordered(kind):
        both = jnp.stack(grads[kind])
        return both.transpose(0, 1, 2, 4, 3, 5, 6).reshape((8, 8) + both.shape[5:])

    def shard_sum(value, axis):
        owned = lax.psum_scatter(value.astype(f32), "shard", scatter_dimension=axis, tiled=True)
        return lax.psum(owned.astype(bf16), "rep")

    mats, down = [], []
    for l in range(LAYERS):
        attn, mlp = ordered("a%d" % l), ordered("m%d" % l)
        both = [part[:, :, :64].transpose(1, 2, 0, 3).reshape(D, 2048) for part in (attn, mlp)]
        mats.append(jnp.concatenate(both, 1))
        down.append(mlp[:, :, 64:].transpose(0, 2, 1, 3).reshape(D, FF).T)
    skip = ordered("a1")[:, :, 64:].reshape(8, 8, 2, 16, 256).transpose(1, 0, 3, 2, 4).reshape(2 * D, D)
    turned = ordered("a0")[:, :, 64:].reshape(8, 8, 2, 8, 256).transpose(1, 0, 3, 2, 4).reshape(D, ROWS)
    return (shard_sum(jnp.stack(mats), 1), shard_sum(jnp.stack(down), 1), shard_sum(skip, 0), shard_sum(turned, 0))


def time_token(timesteps):
    half_width = D // 2
    freqs_row = jnp.exp(-math.log(10000.0) * jnp.arange(half_width, dtype=f32) / half_width)
    angles = timesteps.astype(f32)[:, None] * freqs_row[None, :]
    return jnp.concatenate([jnp.cos(angles), jnp.sin(angles)], -1)


def adam_update(weight, grad, moment_one, moment_two, step_rate):
    grad = grad.astype(f32)
    moment_one = beta_one * moment_one + (1.0 - beta_one) * grad
    moment_two = beta_two * moment_two + (1.0 - beta_two) * grad * grad
    first_hat = moment_one / (1.0 - beta_one**STEP)
    second_hat = moment_two / (1.0 - beta_two**STEP)
    weight = weight - step_rate * (first_hat / (jnp.sqrt(second_hat) + epsilon) + weight_decay * weight)
    return (moment_one, moment_two, weight, weight.astype(bf16))


def local(
    fast,
    latents,
    target_noise,
    labels,
    timesteps,
    loss_weight,
    layer_mats,
    layer_mats_first,
    layer_mats_second,
    down_mats,
    down_first,
    down_second,
    skip_mat,
    skip_first,
    skip_second,
    tables,
    tables_first,
    tables_second,
    vectors,
    vectors_first,
    vectors_second,
):
    n_seqs = latents.shape[0]
    if fast:
        rep, shard = lax.axis_index("rep"), lax.axis_index("shard")
        place = jnp.stack([rep // 2, rep % 2, shard // 2, shard % 2]).astype(jnp.int32)
    else:
        place = jnp.zeros((4,), jnp.int32)
    order = Order()
    time_rows = jnp.pad(time_token(timesteps)[:, None], ((0, 0), (0, TAIL - 1), (0, 0)))
    mats, downs = [None, None], [None, None]
    forward = {}

    def attention(l):
        if l == 0:
            inputs = (labels, latents, time_rows, table, vec, mats[0][0])
        else:
            inputs = (forward["x1"], forward["x0"], ws, vec, mats[1][0])
        forward["a%d" % l] = call_attention(order, l == 0, n_seqs, inputs)
        if l == 0:
            forward["x0"] = forward["a0"][0]

    def mlp(l):
        head = (weight_total, loss_weight, target_noise, table) if l == 1 else None
        out = call_mlp(order, l, n_seqs, forward["a%d" % l][5], vec, mats[l][1], downs[l], head)
        forward["m%d" % l] = out
        forward["x%d" % (l + 1)] = out[3]

    if fast:
        args = (layer_mats, down_mats, skip_mat, tables.T, vectors, loss_weight)
        one, two, three, four = (Gather(place, kinds, args) for kinds in GATHER_CHUNKS)
        one.packed(*order.fuse([one.pack()], "pack_0"))
        joined, packed = order.fuse([one.join_ring(), two.pack()], "join_ring_0")
        one.ring_joined(joined)
        two.packed(packed)
        one.pair_joined(*order.fuse([one.join_pair()], "join_pair_0"))
        joined, own = order.fuse([two.join_ring(), one.join_own()], "join_ring_1")
        two.ring_joined(joined)
        one.own_joined(own)
        one.rest_to_core()
        (wa0, table, vec, weight_total), packed = order.fuse([one.assemble(), three.pack()], "assemble_0")
        mats[0] = (wa0, None)
        three.packed(packed)
        two.pair_joined(*order.fuse([two.join_pair()], "join_pair_1"))
        attention(0)
        joined, own = order.fuse([three.join_ring(), two.join_own()], "join_ring_2")
        three.ring_joined(joined)
        two.own_joined(own)
        two.rest_to_core()
        (w10, downs[0]), packed = order.fuse([two.assemble(), four.pack()], "assemble_1")
        mats[0] = (wa0, w10)
        four.packed(packed)
        three.pair_joined(*order.fuse([three.join_pair()], "join_pair_2"))
        mlp(0)
        joined, own = order.fuse([four.join_ring(), three.join_own()], "join_ring_3")
        four.ring_joined(joined)
        three.own_joined(own)
        three.rest_to_core()
        ((wa1, ws),) = order.fuse([three.assemble()], "assemble_2")
        mats[1] = (wa1, None)
        four.pair_joined(*order.fuse([four.join_pair()], "join_pair_3"))
        four.own_joined(*order.fuse([four.join_own()], "join_own_3"))
        attention(1)
        four.rest_to_core()
        ((w11, downs[1]),) = order.fuse([four.assemble()], "assemble_3")
        mats[1] = (wa1, w11)
        mlp(1)
    else:
        mats, downs, ws, table = gather_any(layer_mats, down_mats, skip_mat, tables, vectors)
        vec = table[ROW_VEC : ROW_VEC + N_VEC].astype(f32)
        weight_total = lax.psum(jnp.sum(loss_weight.astype(f32)), ALL).reshape(1, 1)
        attention(0)
        mlp(0)
        attention(1)
        mlp(1)

    dx, dhead, small_head = forward["m1"][3:]
    grads, small = {}, {}

    def mlp_back(l, dout):
        normed, act, slope = forward["m%d" % l][:3]
        out = call_mlp_backward(
            order, l, n_seqs, place, dout, act, slope, normed, forward["a%d" % l][5], vec, mats[l][1], downs[l]
        )
        grads["m%d" % l], small["m%d" % l], small["f%d" % l] = out[1:3], out[3], out[4]
        return out[0]

    def attention_back(l, dmid, more):
        x, normed, qkv, lse, att, _ = forward["a%d" % l]
        out = call_attention_backward(order, l, n_seqs, place, dmid, x, normed, qkv, lse, att, vec, mats[l][0], more)
        grads["a%d" % l] = out[:2]
        return out[2:]

    bufs = {}
    if fast:
        first, second, third = (Reduce(kinds) for kinds in REDUCE_CHUNKS)
        states = {
            "mats": (layer_mats, layer_mats_first, layer_mats_second),
            "down": (down_mats, down_first, down_second),
            "skip": (skip_mat, skip_first, skip_second),
            "tables": (tables.T, tables_first.T, tables_second.T),
            "vectors": (vectors, vectors_first, vectors_second),
        }
    dmid = mlp_back(1, dx)
    if fast:
        first.start(*grads["m1"])
    dx, d0, small["a1"] = attention_back(1, dmid, (forward["x1"], forward["x0"], ws))
    if fast:
        first.start(*grads["a1"])
        first.core_added(*order.fuse([first.core()], "add_core_1", grid=(4,)))
    dmid = mlp_back(0, dx)
    if fast:
        second.start(*grads["m0"])
        first.both_added(*order.fuse([first.both()], "add_both_1", grid=(4,)))
        second.core_added(*order.fuse([second.core()], "add_core_2", grid=(4,)))
    last = (labels, d0, latents, dhead, small["m0"], small["m1"], small["a1"], small_head, small["f0"], small["f1"])
    attention_back(0, dmid, last)
    if fast:
        third.start(*grads["a0"])
        second.both_added(*order.fuse([second.both()], "add_both_2", grid=(4,)))
        first.ring_added(*order.fuse([first.ring()], "add_ring_1"))
        third.core_added(*order.fuse([third.core()], "add_core_3", grid=(4,)))
        second.ring_added(*order.fuse([second.ring()], "add_ring_2"))
        third.both_added(*order.fuse([third.both()], "add_both_3", grid=(4,)))
        upper, lower = Owned(first), Owned(second, third)
        upper.last_added(*order.fuse([upper.last()], "add_last_1"))
        third.ring_added(*order.fuse([third.ring()], "add_ring_3"))
        upper.adam(order, place, states, bufs, "adam_1")
        lower.last_added(*order.fuse([lower.last()], "add_last_0"))
        (loss,) = lower.adam(order, place, states, bufs, "adam_0")
        loss_sum = loss[0, 0]
        results = [bufs[name] for name in ("mats", "down", "skip", "tables", "vectors")]
        results[3] = [part.T for part in results[3]]
    else:
        loss_sum = lax.psum(small_head[2, 0], ALL)
        g_mats, g_down, g_skip, g_turned = reduce_any(grads)
        g_rows = g_turned.T
        g_tables = jnp.concatenate(
            [g_rows[ROW_PATCH:ROW_HEAD], g_rows[NP : NP + 2], g_rows[:NP], g_rows[ROW_HEAD:ROW_VEC]]
        )
        g_vectors = g_rows[ROW_VEC : ROW_VEC + N_VEC]
        results = [
            adam_update(layer_mats, g_mats, layer_mats_first, layer_mats_second, step_rates[0]),
            adam_update(down_mats, g_down, down_first, down_second, step_rates[1]),
            adam_update(skip_mat, g_skip, skip_first, skip_second, step_rates[2]),
            adam_update(tables, g_tables, tables_first, tables_second, step_rates[3]),
            adam_update(vectors, g_vectors, vectors_first, vectors_second, step_rates[4]),
        ]
    return (loss_sum, weight_total[0, 0], *(part for result in results for part in result))


GATHER_CHUNKS = (("a0", "t"), ("m0",), ("a1", "s"), ("m1",))
REDUCE_CHUNKS = (("m1", "a1", "s"), ("m0",), ("a0", "t"))


def solution(mesh):
    one, two, rows = P(None, "shard", None), P("shard", None), P(None, "shard")
    every = P(ALL, None, None)
    placed = (every, every, P(ALL), P(ALL), P(ALL), *[one] * 6, *[two] * 3, *[rows] * 6)
    fast = mesh.shape["rep"] == 4 and mesh.shape["shard"] == 8
    return jax.shard_map(
        functools.partial(local, fast),
        mesh=mesh,
        in_specs=placed,
        out_specs=(P(), P(), *[one] * 8, *[two] * 4, *[rows] * 8),
        check_vma=False,
    )
```

time: 1120 us -> 382 us (0.34)
  waiting for transfers between devices: 636 us -> 45.1 us
  Pallas kernels: 0 us -> 239 us
  matrix products: 201 us -> 0 us
  blocking collectives: 116 us -> 0 us
  other arithmetic: 93.4 us -> 0.73 us
  starting transfers between devices: 0.55 us -> 67.3 us
  local copies, waits for them, and re-layouts: 54.4 us -> 21.2 us
  between operations: 16.7 us -> 1.65 us
    reduce_scatter x3 -> x0, waiting for transfers between devices: 351 us -> none  [the longest x1 283 us: local(): lax.psum_scatter(grads[0], 'shard', scatter_dimension=1, tiled=True)]
    pallas_call x0 -> x35, Pallas kernels: none -> 239 us  [fuse(): pl.pallas_call(body, grid=grid, in_specs=[spec for part in parts for spec...]
    dot_general x46 -> x0, matrix products: 201 us -> none  [the longest x2 24.2 us: layer_backward(): jnp.einsum('bqhe,bkhe->bhqk', grad_att, values, preferred_element_type=jn...]
    all_gather x3 -> x0, waiting for transfers between devices: 128 us -> none  [the longest x1 61.8 us: local(): lax.all_gather(mats_low, 'shard', axis=1, tiled=True)]
    unnamed x11 -> x0, waiting for transfers between devices: 126 us -> none
    ppermute x0 -> x71, starting transfers between devices: none -> 67.3 us  [send(): return lax.ppermute(value, ALL, to)]
    all_gather x2 -> x0, blocking collectives: 64.9 us -> none  [the longest x1 32.8 us: local(): lax.all_gather(vectors_low, 'shard', axis=1, tiled=True)]
    psum x2 -> x0, blocking collectives: 50.9 us -> none  [the longest x1 38.5 us: local(): lax.psum((jnp.sum(seq_weight * per_seq), jnp.sum(seq_weight)), ('rep', 's...]
  transfers between devices with their start and end apart: 9 -> 71, of which waited for: 8 -> 21; matrix products, arithmetic and copies ran while one was open for 18% -> 0% of each run, Pallas kernels for 0% -> 46%
where the time goes in v1:
time: 382 us; the launch traced here: 375 us
  Pallas kernels  239 us (63%)
  starting transfers between devices  67.3 us (18%)
  waiting for transfers between devices  45.1 us (12%)
  local copies, waits for them, and re-layouts  21.2 us (6%)
    pallas_call x35, Pallas kernels, fuse(): pl.pallas_call(body, grid=grid, in_specs=[spec for part in parts for spec...  239 us
    ppermute x71, starting transfers between devices, send(): return lax.ppermute(value, ALL, to)  67.3 us
    ppermute x71, waiting for transfers between devices, send(): return lax.ppermute(value, ALL, to)  45.1 us
    unnamed x148, local copies, waits for them, and re-layouts  20.5 us
  transfers between devices with their start and end apart: 71, of which 21 were waited for; matrix products, arithmetic and copies ran while one was open for 0% of the time, Pallas kernels for 46%

profile of v1, /device:TPU:0, one launch (start us, length us, event | category | flops | bytes accessed | tf_op | source)
XLA Modules:
  0.0 375.3 jit_solution(13573942883882019801)
XLA Ops:
  1.3 2.4 pack_0.1.refs_0_.refs_11_
  3.7 5.1 %collective-permute-start.2 = (bf16[2,80,256]{2,1,0:T(8,128)(2,1)}, bf16[2,80,256]{2,1,0:T(8,128)(2,1)S(1)}, u32[]{:S(2)}, u32[]{:S(2)}) collective-permute-start(bf16[2,80,256]{2,1,0:T(8,128)(2,1)} %pack_0.1.refs_0_.refs_11_), channel_id=1, source_target_pairs={{0,6},{1,7},{2,0},{3,1},{4,2},{5,3},{6,4},{7,5},{8,14},{9,15},{10,... | collective-permute-start | bytes 245768 | tf_op jit(solution)/shard_map/ppermute | solution.py:772
  9.9 2.1 collective-permute-done.2.refs_3_
  12.0 4.6 %collective-permute-done.1.refs_2_ = bf16[2,80,256]{2,1,0:T(8,128)(2,1)S(1)} collective-permute-done((bf16[2,80,256]{2,1,0:T(8,128)(2,1)}, bf16[2,80,256]{2,1,0:T(8,128)(2,1)S(1)}, u32[]{:S(2)}, u32[]{:S(2)}) %collective-permute-start.1) | collective-permute-done | bytes 81952 | tf_op jit(solution)/shard_map/ppermute | solution.py:772
  17.8 2.7 join_ring_0.1
  23.7 2.1 collective-permute-start.9
  28.6 2.0 join_pair_0.1
  33.0 3.3 collective-permute-done.8.refs_2_
  37.6 2.4 join_ring_1.1
  44.7 4.5 %assemble_0.1 = (bf16[512,2048]{1,0:T(8,128)(2,1)}, bf16[512,512]{1,0:T(8,128)(2,1)}, f32[24,512]{1,0:T(8,128)}, f32[1,1]{1,0:T(1,128)}, bf16[2,96,256]{2,1,0:T(8,128)(2,1)}) custom-call(s32[4]{0:T(128)} %pad_add_fusion.refs_0_.refs_4_.refs_8_, bf16[2,4,80,256]{3,2,1,0:T(8,128)(2,1)} %get-tuple-element.160.refs_4_.refs_6_.refs_1_, ...), custom_call_target="tpu_custom_call" | custom-call | flops 49999998976 | bytes 100000000 | tf_op jit(solution)/shard_map/assemble_0/pallas_call | solution.py:82
  53.1 2.2 join_pair_1.1
  57.9 13.8 %attention_forward_0.1 = (f32[4,272,512]{2,1,0:T(8,128)}, bf16[4,272,512]{2,1,0:T(8,128)(2,1)}, bf16[4,272,1536]{2,1,0:T(8,128)(2,1)}, f32[4,16,256]{2,1,0:T(8,1...) custom-call(s32[4]{0:T(128)} %refs_9_.9, bf16[4,16,256]{2,1,0:T(8,128)(2,1)} %refs_11_.6, ...), custom_call_target="tpu_custom_call" | custom-call | flops 49999998976 | bytes 100000000 | tf_op jit(solution)/shard_map/attention_forward_0/pallas_call | solution.py:82
  72.4 2.5 join_ring_2.1
  80.9 5.5 %assemble_1.1 = (bf16[512,2048]{1,0:T(8,128)(2,1)}, bf16[2,2048,256]{2,1,0:T(8,128)(2,1)}, bf16[2,128,256]{2,1,0:T(8,128)(2,1)}) custom-call(s32[4]{0:T(128)} %pad_add_fusion.refs_0_.refs_4_.refs_8_, bf16[2,4,128,256]{3,2,1,0:T(8,128)(2,1)} %get-tuple-element.170.refs_6_.refs_4_.refs_1_, bf16[2,4,128,256]{3,2,1,0:T(8,128)(2,1)} %copy-done.11, ...), custom_call_target="tpu_custom_call" | custom-call | flops 49999998976 | bytes 100000000 | tf_op jit(solution)/shard_map/assemble_1/pallas_call | solution.py:82
  86.3 2.0 collective-permute-start.29
  91.2 2.1 join_pair_2.1
  94.8 13.3 %mlp_forward_0.1 = (bf16[1088,512]{1,0:T(8,128)(2,1)}, bf16[1088,2048]{1,0:T(8,128)(2,1)}, bf16[1088,2048]{1,0:T(8,128)(2,1)}, f32[1088,512]{1,0:T(8,128)}) custom-call(f32[1088,512]{1,0:T(8,128)} %bitcast.26, f32[24,512]{1,0:T(8,128)} %get-tuple-element.167.refs_4_.refs_1_.refs_3_.refs_6_.refs_7_, ...), custom_call_target="tpu_custom_call" | custom-call | flops 49999998976 | bytes 100000000 | tf_op jit(solution)/shard_map/mlp_forward_0/pallas_call | solution.py:82
  108.8 2.4 join_ring_3.1
  116.4 3.9 %assemble_2.1 = (bf16[512,2048]{1,0:T(8,128)(2,1)}, bf16[2,1024,256]{2,1,0:T(8,128)(2,1)}) custom-call(s32[4]{0:T(128)} %pad_add_fusion.refs_0_.refs_4_.refs_8_, bf16[2,4,96,256]{3,2,1,0:T(8,128)(2,1)} %get-tuple-element.180.refs_4_.refs_1_, bf16[2,4,96,256]{3,2,1,0:T(8,128)(2,1)} %copy-done.21, bf16[2,4,96,256]{3,2,1,0:T(8,128)(2,1)} %get-tuple-element.182.refs_5_.refs_3_, ...), custom_call_target="tpu_custom_call" | custom-call | flops 49999998976 | bytes 100000000 | tf_op jit(solution)/shard_map/assemble_2/pallas_call | solution.py:82
  122.4 2.2 join_pair_3.1
  126.5 2.2 join_own_3.1.refs_5_
  128.7 9.2 %collective-permute-done.35.refs_2_ = bf16[2,4,128,256]{3,2,1,0:T(8,128)(2,1)S(1)} collective-permute-done((bf16[2,4,128,256]{3,2,1,0:T(8,128)(2,1)}, bf16[2,4,128,256]{3,2,1,0:T(8,128)(2,1)S(1)}, u32[]{:S(2)}, u32[]{:S(2)}) %collective-permute-start.35) | collective-permute-done | bytes 524320 | tf_op jit(solution)/shard_map/ppermute | solution.py:772
  138.5 15.3 %attention_forward_1.1 = (f32[4,272,512]{2,1,0:T(8,128)}, bf16[4,272,512]{2,1,0:T(8,128)(2,1)}, bf16[4,272,1536]{2,1,0:T(8,128)(2,1)}, f32[4,16,256]{2,1,0:T(8,1...) custom-call(f32[4,272,512]{2,1,0:T(8,128)} %bitcast.28, ...), custom_call_target="tpu_custom_call" | custom-call | flops 49999998976 | bytes 100000000 | tf_op jit(solution)/shard_map/attention_forward_1/pallas_call | solution.py:82
  155.1 4.6 %assemble_3.1 = (bf16[512,2048]{1,0:T(8,128)(2,1)}, bf16[2,2048,256]{2,1,0:T(8,128)(2,1)}) custom-call(s32[4]{0:T(128)} %pad_add_fusion.refs_0_.refs_4_.refs_8_, bf16[2,4,128,256]{3,2,1,0:T(8,128)(2,1)} %get-tuple-element.190.refs_0_.refs_2_.refs_1_, bf16[2,4,128,256]{3,2,1,0:T(8,128)(2,1)} %copy-done.13, ...), custom_call_target="tpu_custom_call" | custom-call | flops 49999998976 | bytes 100000000 | tf_op jit(solution)/shard_map/assemble_3/pallas_call | solution.py:82
  159.6 17.2 %mlp_forward_1.1 = (bf16[1088,512]{1,0:T(8,128)(2,1)}, bf16[1088,2048]{1,0:T(8,128)(2,1)}, bf16[1088,2048]{1,0:T(8,128)(2,1)}, f32[1088,512]{1,0:T(8,128)}, f32[16,512]{1,0:T(8,128)}, /*index=5*/f32[8,512]{1,0:T(8,128)}) custom-call(f32[1,1]{1,0:T(1,128)} %get-tuple-element.165.refs_0_, s32[4]{0:T(128)} %refs_1_.5, f32[1088,512]{1,0:T(8,128)} %bitcast.32, ...), custom_call_target="tpu_custom_call" | custom-call | flops 49999998976 | bytes 100000000 | tf_op jit(solution)/shard_map/mlp_forward_1/pallas_call | solution.py:82
  176.9 19.5 %mlp_backward_1.1 = (f32[1088,512]{1,0:T(8,128)}, bf16[2,2,2,4,128,256]{5,4,3,2,1,0:T(8,128)(2,1)}, bf16[2,2,2,4,128,256]{5,4,3,2,1,0:T(8,128)(2,1)}, f32[8,512]{1,0:T(8,128)}, f32[1,2048]{1,0:T(1,128)}) custom-call(s32[4]{0:T(128)} %pad_add_fusion.refs_0_.refs_4_.refs_8_, f32[1088,512]{1,0:T(8,128)} %get-tuple-element.196.refs_1_, ...), custom_call_target="tpu_custom_call" | custom-call | flops 49999998976 | bytes 100000000 | tf_op jit(solution)/shard_map/mlp_backward_1/pallas_call | solution.py:82
  196.8 26.7 %attention_backward_1.1 = (bf16[2,2,2,4,96,256]{5,4,3,2,1,0:T(8,128)(2,1)}, bf16[2,2,2,4,96,256]{5,4,3,2,1,0:T(8,128)(2,1)}, f32[4,272,512]{2,1,0:T(8,128)}, f32[4,272,512]{2,1,0:T(8,128)}, f32[8,512]{1,0:T(8,128)}) custom-call(s32[4]{0:T(128)} %pad_add_fusion.refs_0_.refs_4_.refs_8_, f32[4,272,512]{2,1,0:T(8,128)} %bitcast.34, ...), custom_call_target="tpu_custom_call" | custom-call | flops 49999998976 | bytes 100000000 | tf_op jit(solution)/shard_map/attention_backward_1/pallas_call | solution.py:82
  223.7 3.4 collective-permute-done.41.refs_3_
  229.0 5.5 %add_core_1.1 = (bf16[2,4,224,256]{3,2,1,0:T(8,128)(2,1)}, bf16[2,4,224,256]{3,2,1,0:T(8,128)(2,1)}, bf16[2,4,224,256]{3,2,1,0:T(8,128)(2,1)}, bf16[2,4,224,256]{3,2,1,0:T(8,128)(2,1)}) custom-call(bf16[2,2,2,4,128,256]{5,4,3,2,1,0:T(8,128)(2,1)} %get-tuple-element.208.refs_0_, bf16[2,2,2,4,96,256]{5,4,3,2,1,0:T(8,128)(2,1)} %get-tuple-element.209.refs_1_.refs_4_, ...), custom_call_target="tpu_custom_call" | custom-call | flops 49999998976 | bytes 100000000 | tf_op jit(solution)/shard_map/add_core_1/pallas_call | solution.py:82
  237.1 19.3 %mlp_backward_0.1 = (f32[1088,512]{1,0:T(8,128)}, bf16[2,2,2,4,128,256]{5,4,3,2,1,0:T(8,128)(2,1)}, bf16[2,2,2,4,128,256]{5,4,3,2,1,0:T(8,128)(2,1)}, f32[8,512]{1,0:T(8,128)}, f32[1,2048]{1,0:T(1,128)}) custom-call(s32[4]{0:T(128)} %pad_add_fusion.refs_0_.refs_4_.refs_8_, f32[1088,512]{1,0:T(8,128)} %bitcast.31, ...), custom_call_target="tpu_custom_call" | custom-call | flops 49999998976 | bytes 100000000 | tf_op jit(solution)/shard_map/mlp_backward_0/pallas_call | solution.py:82
  259.0 4.1 %add_both_1.1 = (bf16[4,224,256]{2,1,0:T(8,128)(2,1)}, bf16[4,224,256]{2,1,0:T(8,128)(2,1)}, bf16[4,224,256]{2,1,0:T(8,128)(2,1)}, bf16[4,224,256]{2,1,0:T(8,128)(2,1)}) custom-call(bf16[2,4,224,256]{3,2,1,0:T(8,128)(2,1)} %get-tuple-element.212.refs_9_.refs_0_, bf16[2,4,224,256]{3,2,1,0:T(8,128)(2,1)} %copy-done.6, ...), custom_call_target="tpu_custom_call" | custom-call | flops 49999998976 | bytes 100000000 | tf_op jit(solution)/shard_map/add_both_1/pallas_call | solution.py:82
  266.6 4.3 %add_core_2.1 = (bf16[2,4,128,256]{3,2,1,0:T(8,128)(2,1)}, bf16[2,4,128,256]{3,2,1,0:T(8,128)(2,1)}, bf16[2,4,128,256]{3,2,1,0:T(8,128)(2,1)}, bf16[2,4,128,256]{3,2,1,0:T(8,128)(2,1)}) custom-call(bf16[2,2,2,4,128,256]{5,4,3,2,1,0:T(8,128)(2,1)} %get-tuple-element.213.refs_0_, bf16[2,2,2,4,128,256]{5,4,3,2,1,0:T(8,128)(2,1)} %copy-done, ...), custom_call_target="tpu_custom_call" | custom-call | flops 49999998976 | bytes 100000000 | tf_op jit(solution)/shard_map/add_core_2/pallas_call | solution.py:82
  272.8 23.6 %attention_backward_0.1 = (bf16[2,2,2,4,80,256]{5,4,3,2,1,0:T(8,128)(2,1)}, bf16[2,2,2,4,80,256]{5,4,3,2,1,0:T(8,128)(2,1)}) custom-call(s32[4]{0:T(128)} %pad_add_fusion.refs_0_.refs_4_.refs_8_, f32[4,272,512]{2,1,0:T(8,128)} %bitcast.30, f32[4,272,512]{2,1,0:T(8,128)} %get-tuple-element.174.refs_6_.refs_1_.refs_10_.refs_2_, ...), custom_call_target="tpu_custom_call" | custom-call | flops 49999998976 | bytes 100000000 | tf_op jit(solution)/shard_map/attention_backward_0/pallas_call | solution.py:82
  297.5 3.6 add_both_2.1
  301.2 2.5 add_ring_1.1
  310.5 3.8 %add_core_3.1 = (bf16[2,4,80,256]{3,2,1,0:T(8,128)(2,1)}, bf16[2,4,80,256]{3,2,1,0:T(8,128)(2,1)}, bf16[2,4,80,256]{3,2,1,0:T(8,128)(2,1)}, bf16[2,4,80,256]{3,2,1,0:T(8,128)(2,1)}) custom-call(bf16[2,2,2,4,80,256]{5,4,3,2,1,0:T(8,128)(2,1)} %get-tuple-element.236.refs_4_.refs_0_, bf16[2,2,2,4,80,256]{5,4,3,2,1,0:T(8,128)(2,1)} %copy-done.3, ...), custom_call_target="tpu_custom_call" | custom-call | flops 49999998976 | bytes 100000000 | tf_op jit(solution)/shard_map/add_core_3/pallas_call | solution.py:82
  318.6 2.0 add_ring_2.1
  320.6 4.1 %collective-permute-done.55.refs_1_ = bf16[2,4,80,256]{3,2,1,0:T(8,128)(2,1)S(1)} collective-permute-done((bf16[2,4,80,256]{3,2,1,0:T(8,128)(2,1)}, bf16[2,4,80,256]{3,2,1,0:T(8,128)(2,1)S(1)}, u32[]{:S(2)}, u32[]{:S(2)}) %collective-permute-start.55) | collective-permute-done | bytes 327712 | tf_op jit(solution)/shard_map/ppermute | solution.py:772
  326.5 3.4 add_both_3.1
  330.0 2.2 add_last_1.1.refs_4_.refs_1_
  335.7 2.0 collective-permute-start.53
  342.1 1.9 add_ring_3.1
  345.3 2.0 collective-permute-start.63
  347.3 3.0 collective-permute-start.64
  350.4 6.8 %skip.1 = (f32[2,256,512]{2,1,0:T(8,128)}, f32[2,256,512]{2,1,0:T(8,128)}, f32[2,256,512]{2,1,0:T(8,128)}, bf16[2,256,512]{2,1,0:T(8,128)(2,1)}, f32[2,64,4096]{...) custom-call(s32[4]{0:T(128)} %pad_add_fusion.refs_0_.refs_4_.refs_8_, ...), custom_call_target="tpu_custom_call" | custom-call | flops 49999998976 | bytes 100000000 | tf_op jit(solution)/shard_map/skip/pallas_call | solution.py:82
  358.0 2.0 add_last_0.1.refs_1_.refs_25_
  360.8 5.3 %collective-permute-done.68.refs_2_ = bf16[2,208,256]{2,1,0:T(8,128)(2,1)S(1)} collective-permute-done((bf16[2,208,256]{2,1,0:T(8,128)(2,1)}, bf16[2,208,256]{2,1,0:T(8,128)(2,1)S(1)}, u32[]{:S(2)}, u32[]{:S(2)}) %collective-permute-start.68) | collective-permute-done | bytes 213024 | tf_op jit(solution)/shard_map/ppermute | solution.py:772
  368.3 6.8 %vectors.1 = (f32[2,256,512]{2,1,0:T(8,128)}, f32[2,256,512]{2,1,0:T(8,128)}, f32[2,256,512]{2,1,0:T(8,128)}, bf16[2,256,512]{2,1,0:T(8,128)(2,1)}, f32[2,64,409...) custom-call(s32[4]{0:T(128)} %pad_add_fusion.refs_0_.refs_4_.refs_8_, ...), custom_call_target="tpu_custom_call", output_to_operand_aliasing={{0}: (17, {}), {1}: (18, {}), {2}: (19, {}), {3}: (20, {}),... | custom-call | flops 49999998976 | bytes 100000000 | tf_op jit(solution)/shard_map/vectors/pallas_call | solution.py:82
  (284 shorter events, 86.0 us)
Async XLA Ops:
  3.7 8.3 %collective-permute-start.2 = (bf16[2,80,256]{2,1,0:T(8,128)(2,1)}, bf16[2,80,256]{2,1,0:T(8,128)(2,1)S(1)}, u32[]{:S(2)}, u32[]{:S(2)}) collective-permute-start(bf16[2,80,256]{2,1,0:T(8,128)(2,1)} %pack_0.1.refs_0_.refs_11_), channel_id=1, source_target_pairs={{0,6},{1,7},{2,0},{3,1},{4,2},{5,3},{6,4},{7,5},{8,14},{9,15},{10,... | collective-permute-start | bytes 245768 | tf_op jit(solution)/shard_map/ppermute | solution.py:772
  23.7 9.4 %collective-permute-start.9 = (bf16[2,128,256]{2,1,0:T(8,128)(2,1)}, bf16[2,128,256]{2,1,0:T(8,128)(2,1)S(1)}, u32[]{:S(2)}, u32[]{:S(2)}) collective-permute-start(bf16[2,128,256]{2,1,0:T(8,128)(2,1)} %get-tuple-element.162.refs_0_), channel_id=1, source_target_pairs={{0,6},{1,7},{2,0},{3,1},{4,2},{5,3},{6,4},{7,5},{8,14},{9,15},{10,... | collective-permute-start | bytes 393224 | tf_op jit(solution)/shard_map/ppermute | solution.py:772
  25.8 10.6 %collective-permute-start.8 = (bf16[2,128,256]{2,1,0:T(8,128)(2,1)}, bf16[2,128,256]{2,1,0:T(8,128)(2,1)S(1)}, u32[]{:S(2)}, u32[]{:S(2)}) collective-permute-start(bf16[2,128,256]{2,1,0:T(8,128)(2,1)} %get-tuple-element.162.refs_0_), channel_id=1, source_target_pairs={{0,4},{1,5},{2,6},{3,7},{4,0},{5,1},{6,2},{7,3},{8,12},{9,13},{10,... | collective-permute-start | bytes 393224 | tf_op jit(solution)/shard_map/ppermute | solution.py:772
  25.8 10.6 %collective-permute-start.7 = (bf16[2,128,256]{2,1,0:T(8,128)(2,1)}, bf16[2,128,256]{2,1,0:T(8,128)(2,1)S(1)}, u32[]{:S(2)}, u32[]{:S(2)}) collective-permute-start(bf16[2,128,256]{2,1,0:T(8,128)(2,1)} %get-tuple-element.162.refs_0_), channel_id=1, source_target_pairs={{0,2},{1,3},{2,4},{3,5},{4,6},{5,7},{6,0},{7,1},{8,10},{9,11},{10,... | collective-permute-start | bytes 393224 | tf_op jit(solution)/shard_map/ppermute | solution.py:772
  30.6 9.5 %collective-permute-start.5 = (bf16[2,4,80,256]{3,2,1,0:T(8,128)(2,1)}, bf16[2,4,80,256]{3,2,1,0:T(8,128)(2,1)S(1)}, u32[]{:S(2)}, u32[]{:S(2)}) collective-permute-start(bf16[2,4,80,256]{3,2,1,0:T(8,128)(2,1)} %get-tuple-element.160.refs_4_.refs_6_.refs_1_), channel_id=1, source_target_pairs={{0,16},{1,17},{2,18},{3,19},{4,20},{5,21},{6,22},{7,23},{8,24},{9,... | collective-permute-start | bytes 983048 | tf_op jit(solution)/shard_map/ppermute | solution.py:772
  32.1 8.5 %collective-permute-start.6 = (bf16[2,4,80,256]{3,2,1,0:T(8,128)(2,1)}, bf16[2,4,80,256]{3,2,1,0:T(8,128)(2,1)S(1)}, u32[]{:S(2)}, u32[]{:S(2)}) collective-permute-start(bf16[2,4,80,256]{3,2,1,0:T(8,128)(2,1)} %get-tuple-element.161.refs_5_.refs_3_), channel_id=1, source_target_pairs={{0,1},{1,0},{2,3},{3,2},{4,5},{5,4},{6,7},{7,6},{8,9},{9,8},{10,11... | collective-permute-start | bytes 983048 | tf_op jit(solution)/shard_map/ppermute | solution.py:772
  41.5 10.7 %collective-permute-start.14 = (bf16[4,128,256]{2,1,0:T(8,128)(2,1)}, bf16[4,128,256]{2,1,0:T(8,128)(2,1)S(1)}, u32[]{:S(2)}, u32[]{:S(2)}) collective-permute-start(bf16[4,128,256]{2,1,0:T(8,128)(2,1)} %get-tuple-element.169.refs_2_), channel_id=1, source_target_pairs={{0,16},{1,17},{2,18},{3,19},{4,20},{5,21},{6,22},{7,23},{8,24},{9,... | collective-permute-start | bytes 786440 | tf_op jit(solution)/shard_map/ppermute | solution.py:772
  42.1 10.2 %collective-permute-start.13 = (bf16[4,128,256]{2,1,0:T(8,128)(2,1)}, bf16[4,128,256]{2,1,0:T(8,128)(2,1)S(1)}, u32[]{:S(2)}, u32[]{:S(2)}) collective-permute-start(bf16[4,128,256]{2,1,0:T(8,128)(2,1)} %get-tuple-element.164.refs_15_.refs_0_), channel_id=1, source_target_pairs={{0,1},{1,0},{2,3},{3,2},{4,5},{5,4},{6,7},{7,6},{8,9},{9,8},{10,11... | collective-permute-start | bytes 786440 | tf_op jit(solution)/shard_map/ppermute | solution.py:772
  49.2 22.5 %collective-permute-start.19 = (bf16[2,96,256]{2,1,0:T(8,128)(2,1)}, bf16[2,96,256]{2,1,0:T(8,128)(2,1)S(1)}, u32[]{:S(2)}, u32[]{:S(2)}) collective-permute-start(bf16[2,96,256]{2,1,0:T(8,128)(2,1)} %get-tuple-element.173.refs_0_), channel_id=1, source_target_pairs={{0,6},{1,7},{2,0},{3,1},{4,2},{5,3},{6,4},{7,5},{8,14},{9,15},{10,... | collective-permute-start | bytes 294920 | tf_op jit(solution)/shard_map/ppermute | solution.py:772
  49.8 21.9 %collective-permute-start.18 = (bf16[2,96,256]{2,1,0:T(8,128)(2,1)}, bf16[2,96,256]{2,1,0:T(8,128)(2,1)S(1)}, u32[]{:S(2)}, u32[]{:S(2)}) collective-permute-start(bf16[2,96,256]{2,1,0:T(8,128)(2,1)} %get-tuple-element.173.refs_0_), channel_id=1, source_target_pairs={{0,4},{1,5},{2,6},{3,7},{4,0},{5,1},{6,2},{7,3},{8,12},{9,13},{10,... | collective-permute-start | bytes 294920 | tf_op jit(solution)/shard_map/ppermute | solution.py:772
  51.0 20.8 %collective-permute-start.17 = (bf16[2,96,256]{2,1,0:T(8,128)(2,1)}, bf16[2,96,256]{2,1,0:T(8,128)(2,1)S(1)}, u32[]{:S(2)}, u32[]{:S(2)}) collective-permute-start(bf16[2,96,256]{2,1,0:T(8,128)(2,1)} %get-tuple-element.173.refs_0_), channel_id=1, source_target_pairs={{0,2},{1,3},{2,4},{3,5},{4,6},{5,7},{6,0},{7,1},{8,10},{9,11},{10,... | collective-permute-start | bytes 294920 | tf_op jit(solution)/shard_map/ppermute | solution.py:772
  55.3 19.7 %collective-permute-start.16 = (bf16[2,4,128,256]{3,2,1,0:T(8,128)(2,1)}, bf16[2,4,128,256]{3,2,1,0:T(8,128)(2,1)S(1)}, u32[]{:S(2)}, u32[]{:S(2)}) collective-permute-start(bf16[2,4,128,256]{3,2,1,0:T(8,128)(2,1)} %get-tuple-element.172.refs_5_.refs_3_), channel_id=1, source_target_pairs={{0,1},{1,0},{2,3},{3,2},{4,5},{5,4},{6,7},{7,6},{8,9},{9,8},{10,11... | collective-permute-start | bytes 1572872 | tf_op jit(solution)/shard_map/ppermute | solution.py:772
  56.4 19.0 %collective-permute-start.15 = (bf16[2,4,128,256]{3,2,1,0:T(8,128)(2,1)}, bf16[2,4,128,256]{3,2,1,0:T(8,128)(2,1)S(1)}, u32[]{:S(2)}, u32[]{:S(2)}) collective-permute-start(bf16[2,4,128,256]{3,2,1,0:T(8,128)(2,1)} %get-tuple-element.170.refs_6_.refs_4_.refs_1_), channel_id=1, source_target_pairs={{0,16},{1,17},{2,18},{3,19},{4,20},{5,21},{6,22},{7,23},{8,24},{9,... | collective-permute-start | bytes 1572872 | tf_op jit(solution)/shard_map/ppermute | solution.py:772
  75.6 14.9 %collective-permute-start.24 = (bf16[4,96,256]{2,1,0:T(8,128)(2,1)}, bf16[4,96,256]{2,1,0:T(8,128)(2,1)S(1)}, u32[]{:S(2)}, u32[]{:S(2)}) collective-permute-start(bf16[4,96,256]{2,1,0:T(8,128)(2,1)} %get-tuple-element.179.refs_2_), channel_id=1, source_target_pairs={{0,16},{1,17},{2,18},{3,19},{4,20},{5,21},{6,22},{7,23},{8,24},{9,... | collective-permute-start | bytes 589832 | tf_op jit(solution)/shard_map/ppermute | solution.py:772
  76.1 14.4 %collective-permute-start.23 = (bf16[4,96,256]{2,1,0:T(8,128)(2,1)}, bf16[4,96,256]{2,1,0:T(8,128)(2,1)S(1)}, u32[]{:S(2)}, u32[]{:S(2)}) collective-permute-start(bf16[4,96,256]{2,1,0:T(8,128)(2,1)} %get-tuple-element.176.refs_15_.refs_0_), channel_id=1, source_target_pairs={{0,1},{1,0},{2,3},{3,2},{4,5},{5,4},{6,7},{7,6},{8,9},{9,8},{10,11... | collective-permute-start | bytes 589832 | tf_op jit(solution)/shard_map/ppermute | solution.py:772
  86.3 21.7 %collective-permute-start.29 = (bf16[2,128,256]{2,1,0:T(8,128)(2,1)}, bf16[2,128,256]{2,1,0:T(8,128)(2,1)S(1)}, u32[]{:S(2)}, u32[]{:S(2)}) collective-permute-start(bf16[2,128,256]{2,1,0:T(8,128)(2,1)} %get-tuple-element.183.refs_0_), channel_id=1, source_target_pairs={{0,6},{1,7},{2,0},{3,1},{4,2},{5,3},{6,4},{7,5},{8,14},{9,15},{10,... | collective-permute-start | bytes 393224 | tf_op jit(solution)/shard_map/ppermute | solution.py:772
  88.3 19.8 %collective-permute-start.28 = (bf16[2,128,256]{2,1,0:T(8,128)(2,1)}, bf16[2,128,256]{2,1,0:T(8,128)(2,1)S(1)}, u32[]{:S(2)}, u32[]{:S(2)}) collective-permute-start(bf16[2,128,256]{2,1,0:T(8,128)(2,1)} %get-tuple-element.183.refs_0_), channel_id=1, source_target_pairs={{0,4},{1,5},{2,6},{3,7},{4,0},{5,1},{6,2},{7,3},{8,12},{9,13},{10,... | collective-permute-start | bytes 393224 | tf_op jit(solution)/shard_map/ppermute | solution.py:772
  88.9 19.2 %collective-permute-start.27 = (bf16[2,128,256]{2,1,0:T(8,128)(2,1)}, bf16[2,128,256]{2,1,0:T(8,128)(2,1)S(1)}, u32[]{:S(2)}, u32[]{:S(2)}) collective-permute-start(bf16[2,128,256]{2,1,0:T(8,128)(2,1)} %get-tuple-element.183.refs_0_), channel_id=1, source_target_pairs={{0,2},{1,3},{2,4},{3,5},{4,6},{5,7},{6,0},{7,1},{8,10},{9,11},{10,... | collective-permute-start | bytes 393224 | tf_op jit(solution)/shard_map/ppermute | solution.py:772
  93.3 18.0 %collective-permute-start.26 = (bf16[2,4,96,256]{3,2,1,0:T(8,128)(2,1)}, bf16[2,4,96,256]{3,2,1,0:T(8,128)(2,1)S(1)}, u32[]{:S(2)}, u32[]{:S(2)}) collective-permute-start(bf16[2,4,96,256]{3,2,1,0:T(8,128)(2,1)} %get-tuple-element.182.refs_5_.refs_3_), channel_id=1, source_target_pairs={{0,1},{1,0},{2,3},{3,2},{4,5},{5,4},{6,7},{7,6},{8,9},{9,8},{10,11... | collective-permute-start | bytes 1179656 | tf_op jit(solution)/shard_map/ppermute | solution.py:772
  94.0 17.8 %collective-permute-start.25 = (bf16[2,4,96,256]{3,2,1,0:T(8,128)(2,1)}, bf16[2,4,96,256]{3,2,1,0:T(8,128)(2,1)S(1)}, u32[]{:S(2)}, u32[]{:S(2)}) collective-permute-start(bf16[2,4,96,256]{3,2,1,0:T(8,128)(2,1)} %get-tuple-element.180.refs_4_.refs_1_), channel_id=1, source_target_pairs={{0,16},{1,17},{2,18},{3,19},{4,20},{5,21},{6,22},{7,23},{8,24},{9,... | collective-permute-start | bytes 1179656 | tf_op jit(solution)/shard_map/ppermute | solution.py:772
  111.9 8.9 %collective-permute-start.34 = (bf16[4,128,256]{2,1,0:T(8,128)(2,1)}, bf16[4,128,256]{2,1,0:T(8,128)(2,1)S(1)}, u32[]{:S(2)}, u32[]{:S(2)}) collective-permute-start(bf16[4,128,256]{2,1,0:T(8,128)(2,1)} %get-tuple-element.189.refs_2_), channel_id=1, source_target_pairs={{0,16},{1,17},{2,18},{3,19},{4,20},{5,21},{6,22},{7,23},{8,24},{9,... | collective-permute-start | bytes 786440 | tf_op jit(solution)/shard_map/ppermute | solution.py:772
  113.1 8.6 %collective-permute-start.33 = (bf16[4,128,256]{2,1,0:T(8,128)(2,1)}, bf16[4,128,256]{2,1,0:T(8,128)(2,1)S(1)}, u32[]{:S(2)}, u32[]{:S(2)}) collective-permute-start(bf16[4,128,256]{2,1,0:T(8,128)(2,1)} %get-tuple-element.186.refs_8_.refs_0_), channel_id=1, source_target_pairs={{0,1},{1,0},{2,3},{3,2},{4,5},{5,4},{6,7},{7,6},{8,9},{9,8},{10,11... | collective-permute-start | bytes 786440 | tf_op jit(solution)/shard_map/ppermute | solution.py:772
  124.6 13.4 %collective-permute-start.35 = (bf16[2,4,128,256]{3,2,1,0:T(8,128)(2,1)}, bf16[2,4,128,256]{3,2,1,0:T(8,128)(2,1)S(1)}, u32[]{:S(2)}, u32[]{:S(2)}) collective-permute-start(bf16[2,4,128,256]{3,2,1,0:T(8,128)(2,1)} %get-tuple-element.190.refs_0_.refs_2_.refs_1_), channel_id=1, source_target_pairs={{0,16},{1,17},{2,18},{3,19},{4,20},{5,21},{6,22},{7,23},{8,24},{9,... | collective-permute-start | bytes 1572872 | tf_op jit(solution)/shard_map/ppermute | solution.py:772
  125.4 13.1 %collective-permute-start.36 = (bf16[2,4,128,256]{3,2,1,0:T(8,128)(2,1)}, bf16[2,4,128,256]{3,2,1,0:T(8,128)(2,1)S(1)}, u32[]{:S(2)}, u32[]{:S(2)}) collective-permute-start(bf16[2,4,128,256]{3,2,1,0:T(8,128)(2,1)} %get-tuple-element.191.refs_1_.refs_3_), channel_id=1, source_target_pairs={{0,1},{1,0},{2,3},{3,2},{4,5},{5,4},{6,7},{7,6},{8,9},{9,8},{10,11... | collective-permute-start | bytes 1572872 | tf_op jit(solution)/shard_map/ppermute | solution.py:772
  128.7 25.1 %collective-permute-start.37 = (bf16[2,2,4,128,256]{4,3,2,1,0:T(8,128)(2,1)}, bf16[2,2,4,128,256]{4,3,2,1,0:T(8,128)(2,1)S(1)}, u32[]{:S(2)}, u32[]{:S(2)}) collective-permute-start(bf16[2,2,4,128,256]{4,3,2,1,0:T(8,128)(2,1)} %join_own_3.1.refs_5_), channel_id=1, source_target_pairs={{0,8},{1,9},{2,10},{3,11},{4,12},{5,13},{6,14},{7,15},{8,0},{9,1},... | collective-permute-start | bytes 3145736 | tf_op jit(solution)/shard_map/ppermute | solution.py:772
  138.0 15.8 %collective-permute-start.38 = (bf16[2,4,128,256]{3,2,1,0:T(8,128)(2,1)S(1)}, bf16[2,4,128,256]{3,2,1,0:T(8,128)(2,1)S(1)}, u32[]{:S(2)}, u32[]{:S(2)}) collective-permute-start(bf16[2,4,128,256]{3,2,1,0:T(8,128)(2,1)S(1)} %collective-permute-done.35.refs_2_), channel_id=1, source_target_pairs={{0,8},{1,9},{2,10},{3,11},{4,12},{5,13},{6,14},{7,15},{8,0},{9,1},... | collective-permute-start | bytes 1572872 | tf_op jit(solution)/shard_map/ppermute | solution.py:772
  138.5 15.3 %collective-permute-start.39 = (bf16[2,4,128,256]{3,2,1,0:T(8,128)(2,1)S(1)}, bf16[2,4,128,256]{3,2,1,0:T(8,128)(2,1)S(1)}, u32[]{:S(2)}, u32[]{:S(2)}) collective-permute-start(bf16[2,4,128,256]{3,2,1,0:T(8,128)(2,1)S(1)} %collective-permute-done.36.refs_4_), channel_id=1, source_target_pairs={{0,8},{1,9},{2,10},{3,11},{4,12},{5,13},{6,14},{7,15},{8,0},{9,1},... | collective-permute-start | bytes 1572872 | tf_op jit(solution)/shard_map/ppermute | solution.py:772
  196.4 30.8 %collective-permute-start.40 = (bf16[2,2,2,4,128,256]{5,4,3,2,1,0:T(8,128)(2,1)}, bf16[2,2,2,4,128,256]{5,4,3,2,1,0:T(8,128)(2,1)S(1)}, u32[]{:S(2)}, u32[]{:S(2)}) collective-permute-start(bf16[2,2,2,4,128,256]{5,4,3,2,1,0:T(8,128)(2,1)} %get-tuple-element.210), channel_id=1, source_target_pairs={{0,8},{1,9},{2,10},{3,11},{4,12},{5,13},{6,14},{7,15},{8,0},{9,1},... | collective-permute-start | bytes 6291464 | tf_op jit(solution)/shard_map/ppermute | solution.py:772
  234.5 22.6 %collective-permute-start.43 = (bf16[2,4,224,256]{3,2,1,0:T(8,128)(2,1)}, bf16[2,4,224,256]{3,2,1,0:T(8,128)(2,1)S(1)}, u32[]{:S(2)}, u32[]{:S(2)}) collective-permute-start(bf16[2,4,224,256]{3,2,1,0:T(8,128)(2,1)} %get-tuple-element.215), channel_id=1, source_target_pairs={{0,16},{1,17},{2,18},{3,19},{4,20},{5,21},{6,22},{7,23},{8,24},{9,... | collective-permute-start | bytes 2752520 | tf_op jit(solution)/shard_map/ppermute | solution.py:772
  235.7 22.4 %collective-permute-start.44 = (bf16[2,4,224,256]{3,2,1,0:T(8,128)(2,1)}, bf16[2,4,224,256]{3,2,1,0:T(8,128)(2,1)S(1)}, u32[]{:S(2)}, u32[]{:S(2)}) collective-permute-start(bf16[2,4,224,256]{3,2,1,0:T(8,128)(2,1)} %get-tuple-element.217), channel_id=1, source_target_pairs={{0,1},{1,0},{2,3},{3,2},{4,5},{5,4},{6,7},{7,6},{8,9},{9,8},{10,11... | collective-permute-start | bytes 2752520 | tf_op jit(solution)/shard_map/ppermute | solution.py:772
  256.4 8.9 %collective-permute-start.42 = (bf16[2,2,2,4,128,256]{5,4,3,2,1,0:T(8,128)(2,1)}, bf16[2,2,2,4,128,256]{5,4,3,2,1,0:T(8,128)(2,1)S(1)}, u32[]{:S(2)}, u32[]{:S(2)}) collective-permute-start(bf16[2,2,2,4,128,256]{5,4,3,2,1,0:T(8,128)(2,1)} %get-tuple-element.214), channel_id=1, source_target_pairs={{0,8},{1,9},{2,10},{3,11},{4,12},{5,13},{6,14},{7,15},{8,0},{9,1},... | collective-permute-start | bytes 6291464 | tf_op jit(solution)/shard_map/ppermute | solution.py:772
  263.2 37.9 %collective-permute-start.50 = (bf16[4,224,256]{2,1,0:T(8,128)(2,1)}, bf16[4,224,256]{2,1,0:T(8,128)(2,1)}, u32[]{:S(2)}, u32[]{:S(2)}) collective-permute-start(bf16[4,224,256]{2,1,0:T(8,128)(2,1)} %get-tuple-element.242), channel_id=1, source_target_pairs={{0,1},{1,0},{2,3},{3,2},{4,5},{5,4},{6,7},{7,6},{8,9},{9,8},{10,11... | collective-permute-start | bytes 1376264 | tf_op jit(solution)/shard_map/ppermute | solution.py:772
  264.5 36.6 %collective-permute-start.51 = (bf16[4,224,256]{2,1,0:T(8,128)(2,1)}, bf16[4,224,256]{2,1,0:T(8,128)(2,1)}, u32[]{:S(2)}, u32[]{:S(2)}) collective-permute-start(bf16[4,224,256]{2,1,0:T(8,128)(2,1)} %get-tuple-element.244), channel_id=1, source_target_pairs={{0,16},{1,17},{2,18},{3,19},{4,20},{5,21},{6,22},{7,23},{8,24},{9,... | collective-permute-start | bytes 1376264 | tf_op jit(solution)/shard_map/ppermute | solution.py:772
  270.8 25.7 %collective-permute-start.45 = (bf16[2,4,128,256]{3,2,1,0:T(8,128)(2,1)}, bf16[2,4,128,256]{3,2,1,0:T(8,128)(2,1)S(1)}, u32[]{:S(2)}, u32[]{:S(2)}) collective-permute-start(bf16[2,4,128,256]{3,2,1,0:T(8,128)(2,1)} %get-tuple-element.221), channel_id=1, source_target_pairs={{0,16},{1,17},{2,18},{3,19},{4,20},{5,21},{6,22},{7,23},{8,24},{9,... | collective-permute-start | bytes 1572872 | tf_op jit(solution)/shard_map/ppermute | solution.py:772
  272.2 24.4 %collective-permute-start.46 = (bf16[2,4,128,256]{3,2,1,0:T(8,128)(2,1)}, bf16[2,4,128,256]{3,2,1,0:T(8,128)(2,1)S(1)}, u32[]{:S(2)}, u32[]{:S(2)}) collective-permute-start(bf16[2,4,128,256]{3,2,1,0:T(8,128)(2,1)} %get-tuple-element.223), channel_id=1, source_target_pairs={{0,1},{1,0},{2,3},{3,2},{4,5},{5,4},{6,7},{7,6},{8,9},{9,8},{10,11... | collective-permute-start | bytes 1572872 | tf_op jit(solution)/shard_map/ppermute | solution.py:772
  296.5 12.6 %collective-permute-start.49 = (bf16[2,2,2,4,80,256]{5,4,3,2,1,0:T(8,128)(2,1)}, bf16[2,2,2,4,80,256]{5,4,3,2,1,0:T(8,128)(2,1)S(1)}, u32[]{:S(2)}, u32[]{:S(2)}) collective-permute-start(bf16[2,2,2,4,80,256]{5,4,3,2,1,0:T(8,128)(2,1)} %get-tuple-element.241), channel_id=1, source_target_pairs={{0,8},{1,9},{2,10},{3,11},{4,12},{5,13},{6,14},{7,15},{8,0},{9,1},... | collective-permute-start | bytes 3932168 | tf_op jit(solution)/shard_map/ppermute | solution.py:772
  303.7 26.2 %collective-permute-start.59 = (bf16[2,224,256]{2,1,0:T(8,128)(2,1)}, bf16[2,224,256]{2,1,0:T(8,128)(2,1)}, u32[]{:S(2)}, u32[]{:S(2)}) collective-permute-start(bf16[2,224,256]{2,1,0:T(8,128)(2,1)} %get-tuple-element.258), channel_id=1, source_target_pairs={{0,2},{1,3},{2,4},{3,5},{4,6},{5,7},{6,0},{7,1},{8,10},{9,11},{10,... | collective-permute-start | bytes 688136 | tf_op jit(solution)/shard_map/ppermute | solution.py:772
  305.2 24.7 %collective-permute-start.60 = (bf16[2,224,256]{2,1,0:T(8,128)(2,1)}, bf16[2,224,256]{2,1,0:T(8,128)(2,1)}, u32[]{:S(2)}, u32[]{:S(2)}) collective-permute-start(bf16[2,224,256]{2,1,0:T(8,128)(2,1)} %get-tuple-element.259), channel_id=1, source_target_pairs={{0,4},{1,5},{2,6},{3,7},{4,0},{5,1},{6,2},{7,3},{8,12},{9,13},{10,... | collective-permute-start | bytes 688136 | tf_op jit(solution)/shard_map/ppermute | solution.py:772
  306.6 23.3 %collective-permute-start.61 = (bf16[2,224,256]{2,1,0:T(8,128)(2,1)}, bf16[2,224,256]{2,1,0:T(8,128)(2,1)}, u32[]{:S(2)}, u32[]{:S(2)}) collective-permute-start(bf16[2,224,256]{2,1,0:T(8,128)(2,1)} %get-tuple-element.260), channel_id=1, source_target_pairs={{0,6},{1,7},{2,0},{3,1},{4,2},{5,3},{6,4},{7,5},{8,14},{9,15},{10,... | collective-permute-start | bytes 688136 | tf_op jit(solution)/shard_map/ppermute | solution.py:772
  315.7 9.0 %collective-permute-start.55 = (bf16[2,4,80,256]{3,2,1,0:T(8,128)(2,1)}, bf16[2,4,80,256]{3,2,1,0:T(8,128)(2,1)S(1)}, u32[]{:S(2)}, u32[]{:S(2)}) collective-permute-start(bf16[2,4,80,256]{3,2,1,0:T(8,128)(2,1)} %get-tuple-element.251), channel_id=1, source_target_pairs={{0,16},{1,17},{2,18},{3,19},{4,20},{5,21},{6,22},{7,23},{8,24},{9,... | collective-permute-start | bytes 983048 | tf_op jit(solution)/shard_map/ppermute | solution.py:772
  317.1 8.7 %collective-permute-start.56 = (bf16[2,4,80,256]{3,2,1,0:T(8,128)(2,1)}, bf16[2,4,80,256]{3,2,1,0:T(8,128)(2,1)S(1)}, u32[]{:S(2)}, u32[]{:S(2)}) collective-permute-start(bf16[2,4,80,256]{3,2,1,0:T(8,128)(2,1)} %get-tuple-element.253), channel_id=1, source_target_pairs={{0,1},{1,0},{2,3},{3,2},{4,5},{5,4},{6,7},{7,6},{8,9},{9,8},{10,11... | collective-permute-start | bytes 983048 | tf_op jit(solution)/shard_map/ppermute | solution.py:772
  332.2 9.3 %collective-permute-start.65 = (bf16[2,224,256]{2,1,0:T(8,128)(2,1)}, bf16[2,224,256]{2,1,0:T(8,128)(2,1)S(1)}, u32[]{:S(2)}, u32[]{:S(2)}) collective-permute-start(bf16[2,224,256]{2,1,0:T(8,128)(2,1)} %add_last_1.1.refs_4_.refs_1_), channel_id=1, source_target_pairs={{0,16},{1,17},{2,18},{3,19},{4,20},{5,21},{6,22},{7,23},{8,24},{9,... | collective-permute-start | bytes 688136 | tf_op jit(solution)/shard_map/ppermute | solution.py:772
  335.7 8.3 %collective-permute-start.52 = (bf16[2,128,256]{2,1,0:T(8,128)(2,1)S(1)}, bf16[2,128,256]{2,1,0:T(8,128)(2,1)S(1)}, u32[]{:S(2)}, u32[]{:S(2)}) collective-permute-start(bf16[2,128,256]{2,1,0:T(8,128)(2,1)S(1)} %copy-done.56), channel_id=1, source_target_pairs={{0,2},{1,3},{2,4},{3,5},{4,6},{5,7},{6,0},{7,1},{8,10},{9,11},{10,... | collective-permute-start | bytes 393224 | tf_op jit(solution)/shard_map/ppermute | solution.py:772
  335.7 21.5 %collective-permute-start.53 = (bf16[2,128,256]{2,1,0:T(8,128)(2,1)S(1)}, bf16[2,128,256]{2,1,0:T(8,128)(2,1)S(1)}, u32[]{:S(2)}, u32[]{:S(2)}) collective-permute-start(bf16[2,128,256]{2,1,0:T(8,128)(2,1)S(1)} %copy-done.53), channel_id=1, source_target_pairs={{0,4},{1,5},{2,6},{3,7},{4,0},{5,1},{6,2},{7,3},{8,12},{9,13},{10,... | collective-permute-start | bytes 393224 | tf_op jit(solution)/shard_map/ppermute | solution.py:772
  338.8 18.5 %collective-permute-start.54 = (bf16[2,128,256]{2,1,0:T(8,128)(2,1)S(1)}, bf16[2,128,256]{2,1,0:T(8,128)(2,1)S(1)}, u32[]{:S(2)}, u32[]{:S(2)}) collective-permute-start(bf16[2,128,256]{2,1,0:T(8,128)(2,1)S(1)} %copy-done.52), channel_id=1, source_target_pairs={{0,6},{1,7},{2,0},{3,1},{4,2},{5,3},{6,4},{7,5},{8,14},{9,15},{10,... | collective-permute-start | bytes 393224 | tf_op jit(solution)/shard_map/ppermute | solution.py:772
  344.0 13.2 %collective-permute-start.62 = (bf16[2,80,256]{2,1,0:T(8,128)(2,1)}, bf16[2,80,256]{2,1,0:T(8,128)(2,1)S(1)}, u32[]{:S(2)}, u32[]{:S(2)}) collective-permute-start(bf16[2,80,256]{2,1,0:T(8,128)(2,1)} %get-tuple-element.262), channel_id=1, source_target_pairs={{0,2},{1,3},{2,4},{3,5},{4,6},{5,7},{6,0},{7,1},{8,10},{9,11},{10,... | collective-permute-start | bytes 245768 | tf_op jit(solution)/shard_map/ppermute | solution.py:772
  345.3 12.0 %collective-permute-start.63 = (bf16[2,80,256]{2,1,0:T(8,128)(2,1)}, bf16[2,80,256]{2,1,0:T(8,128)(2,1)S(1)}, u32[]{:S(2)}, u32[]{:S(2)}) collective-permute-start(bf16[2,80,256]{2,1,0:T(8,128)(2,1)} %get-tuple-element.263), channel_id=1, source_target_pairs={{0,4},{1,5},{2,6},{3,7},{4,0},{5,1},{6,2},{7,3},{8,12},{9,13},{10,... | collective-permute-start | bytes 245768 | tf_op jit(solution)/shard_map/ppermute | solution.py:772
  347.3 10.0 %collective-permute-start.64 = (bf16[2,80,256]{2,1,0:T(8,128)(2,1)}, bf16[2,80,256]{2,1,0:T(8,128)(2,1)S(1)}, u32[]{:S(2)}, u32[]{:S(2)}) collective-permute-start(bf16[2,80,256]{2,1,0:T(8,128)(2,1)} %get-tuple-element.264), channel_id=1, source_target_pairs={{0,6},{1,7},{2,0},{3,1},{4,2},{5,3},{6,4},{7,5},{8,14},{9,15},{10,... | collective-permute-start | bytes 245768 | tf_op jit(solution)/shard_map/ppermute | solution.py:772
  (97 other events, 294.2 us)

commit v2 on v1

--- a/solution.py
+++ b/solution.py
@@ -38,10 +38,19 @@
 bf16 = jnp.bfloat16
 f32 = jnp.float32
 ALL = ("rep", "shard")
-VMEM = pltpu.CompilerParams(vmem_limit_bytes=56 * 1024 * 1024)
+MIB = 1024 * 1024
+MARGIN = 6 * MIB
+WIDE = ("pack_0", "join_ring_0")
 ANY = pl.BlockSpec(memory_space=pl.ANY)
 SMEM = pl.BlockSpec(memory_space=pltpu.SMEM)
 WHOLE = pl.BlockSpec(memory_space=pltpu.VMEM)
+
+
+def room(shape, dtype):
+    size = jnp.dtype(dtype).itemsize
+    rows, columns = ((1,) + tuple(shape))[-2:]
+    rows, columns = -(-rows * size // 32) * 32 // size, -(-columns // 128) * 128
+    return math.prod(shape[:-2]) * rows * columns * size
 
 
 class Part:
@@ -79,6 +88,12 @@
             for more in rest:
                 next(more, None)
 
+        need = 0
+        for part in parts:
+            for spec, value in (*zip(part.in_specs, part.inputs), *zip(part.out_specs, part.outs)):
+                if spec is not ANY and spec is not SMEM:
+                    need += 2 * room(spec.block_shape or value.shape, value.dtype)
+            need += sum(room(item.shape, item.dtype) for item in part.scratch if hasattr(item, "inner_aval") or hasattr(item, "shape"))
         result = pl.pallas_call(
             body,
             grid=grid,
@@ -88,7 +103,7 @@
             scratch_shapes=[item for part in parts for item in part.scratch],
             input_output_aliases=aliases or {},
             cost_estimate=pl.CostEstimate(flops=50_000_000_000, bytes_accessed=100_000_000, transcendentals=0),
-            compiler_params=VMEM,
+            compiler_params=pltpu.CompilerParams(vmem_limit_bytes=56 * MIB if name in WIDE else min(need + MARGIN, 56 * MIB)),
             name=name,
         )(*inputs, *extra)
         self.last = result[0]
@@ -858,12 +873,12 @@
 
 def assemble_kernel(kinds, c_ref, *refs):
     x, c, z, y = coords(c_ref)
-    sources, dests = refs[:7], refs[7:]
+    sources, dests = refs[:6], refs[6:]
     for h in range(2):
         if h == 0:
             own_b, x_b, own_c, y_c = sources[:4]
         else:
-            own_b, own_c, x_b, y_c = sources[4].at[0], sources[4].at[1], sources[5], sources[6]
+            own_b, own_c, x_b, y_c = (sources[4 + i].at[k] for i in range(2) for k in range(2))
         for t in range(2):
             for g in range(2):
                 j = 4 * (c ^ h) + 2 * t + (g ^ x)
@@ -899,6 +914,27 @@
         total_ref[0, 0] = jnp.sum(table[ROW_WEIGHT : ROW_WEIGHT + 1])
 
 
+def assemble_all_kernel(kinds, source, *dests):
+    for x in range(2):
+        for c in range(2):
+            for s in range(8):
+                for t in range(2):
+                    j = 4 * c + 2 * t + x
+                    src = source.at[8 * (2 * x + c) + s, t]
+                    row = at = 0
+                    for kind in kinds:
+                        if kind[0] in "am":
+                            dests[at][64 * s : 64 * s + 64, 256 * j : 256 * j + 256] = src[row : row + 64]
+                            row, at = row + 64, at + 1
+                        if kind[0] in "ms":
+                            size = 32 if kind[0] == "m" else 16
+                            for half in range(2):
+                                start = size * (8 * s + j)
+                                dests[at][half, start : start + size] = src[row : row + size]
+                                row += size
+                            at += 1
+
+
 class Gather:
     def __init__(self, place, kinds, sources):
         self.place, self.kinds, self.sources = place, kinds, sources
@@ -914,6 +950,15 @@
             [pltpu.VMEM((4, 64, 256), f32), pltpu.VMEM((4, 32, D), f32), pltpu.SemaphoreType.DMA],
         )
 
+    def packed_for_all(self, results):
+        self.every = lax.all_gather(results[0], ALL)
+
+    def assemble_all(self):
+        shapes = self.shapes()
+        return Part(
+            functools.partial(assemble_all_kernel, self.kinds), [self.every], [WHOLE], shapes, [WHOLE] * len(shapes)
+        )
+
     def packed(self, results):
         (own,) = results
         self.ring = [own] + [send(own, TO_Z[k]) for k in range(1, 4)]
@@ -941,11 +986,15 @@
     def own_joined(self, results):
         self.other = [send(results[0], TO_CORE)]
 
-    def rest_to_core(self):
-        self.other += [send(self.mine[1], TO_CORE), send(self.mine[3], TO_CORE)]
-
-    def assemble(self):
-        shapes, scratch = [], []
+    def join_rest(self):
+        both = shape_of((2, 2, 4, self.rows, 256), bf16)
+        return Part(join_own_kernel, (self.mine[1], self.mine[3]), [WHOLE] * 2, [both], [WHOLE])
+
+    def rest_joined(self, results):
+        self.other.append(send(results[0], TO_CORE))
+
+    def shapes(self):
+        shapes = []
         for kind in self.kinds:
             if kind[0] in "am":
                 shapes.append(shape_of((D, 2048), bf16))
@@ -955,11 +1004,15 @@
                 shapes.append(shape_of((2, 2 * D, 256), bf16))
             if kind[0] == "t":
                 shapes += [shape_of((ROWS, D), bf16), shape_of((N_VEC, D)), shape_of((1, 1))]
-                scratch = [pltpu.VMEM((D, ROWS), f32)]
+        return shapes
+
+    def assemble(self):
+        shapes = self.shapes()
+        scratch = [pltpu.VMEM((D, ROWS), f32)] if "t" in self.kinds else []
         return Part(
             functools.partial(assemble_kernel, self.kinds),
             (self.place, *self.mine, *self.other),
-            [SMEM] + [WHOLE] * 7,
+            [SMEM] + [WHOLE] * 6,
             shapes,
             [SMEM if shape.shape == (1, 1) else WHOLE for shape in shapes],
             scratch,
@@ -1285,7 +1338,7 @@
 
     if fast:
         args = (layer_mats, down_mats, skip_mat, tables.T, vectors, loss_weight)
-        one, two, three, four = (Gather(place, kinds, args) for kinds in GATHER_CHUNKS)
+        one, two, three = (Gather(place, kinds, args) for kinds in GATHER_CHUNKS)
         one.packed(*order.fuse([one.pack()], "pack_0"))
         joined, packed = order.fuse([one.join_ring(), two.pack()], "join_ring_0")
         one.ring_joined(joined)
@@ -1294,7 +1347,7 @@
         joined, own = order.fuse([two.join_ring(), one.join_own()], "join_ring_1")
         two.ring_joined(joined)
         one.own_joined(own)
-        one.rest_to_core()
+        one.rest_joined(*order.fuse([one.join_rest()], "join_rest_0"))
         (wa0, table, vec, weight_total), packed = order.fuse([one.assemble(), three.pack()], "assemble_0")
         mats[0] = (wa0, None)
         three.packed(packed)
@@ -1303,24 +1356,16 @@
         joined, own = order.fuse([three.join_ring(), two.join_own()], "join_ring_2")
         three.ring_joined(joined)
         two.own_joined(own)
-        two.rest_to_core()
-        (w10, downs[0]), packed = order.fuse([two.assemble(), four.pack()], "assemble_1")
+        two.rest_joined(*order.fuse([two.join_rest()], "join_rest_1"))
+        ((w10, downs[0]),) = order.fuse([two.assemble()], "assemble_1")
         mats[0] = (wa0, w10)
-        four.packed(packed)
         three.pair_joined(*order.fuse([three.join_pair()], "join_pair_2"))
         mlp(0)
-        joined, own = order.fuse([four.join_ring(), three.join_own()], "join_ring_3")
-        four.ring_joined(joined)
-        three.own_joined(own)
-        three.rest_to_core()
-        ((wa1, ws),) = order.fuse([three.assemble()], "assemble_2")
-        mats[1] = (wa1, None)
-        four.pair_joined(*order.fuse([four.join_pair()], "join_pair_3"))
-        four.own_joined(*order.fuse([four.join_own()], "join_own_3"))
+        three.own_joined(*order.fuse([three.join_own()], "join_own_2"))
+        three.rest_joined(*order.fuse([three.join_rest()], "join_rest_2"))
+        ((wa1, ws, w11, downs[1]),) = order.fuse([three.assemble()], "assemble_2")
+        mats[1] = (wa1, w11)
         attention(1)
-        four.rest_to_core()
-        ((w11, downs[1]),) = order.fuse([four.assemble()], "assemble_3")
-        mats[1] = (wa1, w11)
         mlp(1)
     else:
         mats, downs, ws, table = gather_any(layer_mats, down_mats, skip_mat, tables, vectors)
@@ -1373,14 +1418,14 @@
     last = (labels, d0, latents, dhead, small["m0"], small["m1"], small["a1"], small_head, small["f0"], small["f1"])
     attention_back(0, dmid, last)
     if fast:
+        upper, lower = Owned(first), Owned(second, third)
         third.start(*grads["a0"])
+        first.ring_added(*order.fuse([first.ring()], "add_ring_1"))
         second.both_added(*order.fuse([second.both()], "add_both_2", grid=(4,)))
-        first.ring_added(*order.fuse([first.ring()], "add_ring_1"))
         third.core_added(*order.fuse([third.core()], "add_core_3", grid=(4,)))
         second.ring_added(*order.fuse([second.ring()], "add_ring_2"))
+        upper.last_added(*order.fuse([upper.last()], "add_last_1"))
         third.both_added(*order.fuse([third.both()], "add_both_3", grid=(4,)))
-        upper, lower = Owned(first), Owned(second, third)
-        upper.last_added(*order.fuse([upper.last()], "add_last_1"))
         third.ring_added(*order.fuse([third.ring()], "add_ring_3"))
         upper.adam(order, place, states, bufs, "adam_1")
         lower.last_added(*order.fuse([lower.last()], "add_last_0"))
@@ -1406,7 +1451,7 @@
     return (loss_sum, weight_total[0, 0], *(part for result in results for part in result))
 
 
-GATHER_CHUNKS = (("a0", "t"), ("m0",), ("a1", "s"), ("m1",))
+GATHER_CHUNKS = (("a0", "t"), ("m0",), ("a1", "s", "m1"))
 REDUCE_CHUNKS = (("m1", "a1", "s"), ("m0",), ("a0", "t"))
 
 

time: 382 us -> 314 us (0.82)
  Pallas kernels: 239 us -> 150 us
  waiting for transfers between devices: 45.1 us -> 66.5 us
  local copies, waits for them, and re-layouts: 21.2 us -> 28.3 us
  starting transfers between devices: 67.3 us -> 62.5 us
    pallas_call x35, Pallas kernels: 239 us -> 150 us  [fuse(): pl.pallas_call(body, grid=grid, in_specs=[spec for part in parts for spec...]
    ppermute x71 -> x58, waiting for transfers between devices: 45.1 us -> 66.5 us  [send(): return lax.ppermute(value, ALL, to)]
    unnamed x148 -> x186, local copies, waits for them, and re-layouts: 20.5 us -> 28.3 us
    ppermute x71 -> x58, starting transfers between devices: 67.3 us -> 62.5 us  [send(): return lax.ppermute(value, ALL, to)]
  transfers between devices with their start and end apart: 71 -> 58, of which waited for: 21 -> 28; matrix products, arithmetic and copies ran while one was open for 0% -> 0% of each run, Pallas kernels for 46% -> 31%
where the time goes in v2:
time: 314 us; the launch traced here: 310 us
  Pallas kernels  150 us (48%)
  waiting for transfers between devices  66.5 us (21%)
  starting transfers between devices  62.5 us (20%)
  local copies, waits for them, and re-layouts  28.3 us (9%)
    pallas_call x35, Pallas kernels, fuse(): pl.pallas_call(body, grid=grid, in_specs=[spec for part in parts for spec...  150 us
    ppermute x58, waiting for transfers between devices, send(): return lax.ppermute(value, ALL, to)  66.5 us
    ppermute x58, starting transfers between devices, send(): return lax.ppermute(value, ALL, to)  62.5 us
    unnamed x186, local copies, waits for them, and re-layouts  28.3 us
  transfers between devices with their start and end apart: 58, of which 28 were waited for; matrix products, arithmetic and copies ran while one was open for 0% of the time, Pallas kernels for 31%

profile of v2, /device:TPU:0, one launch (start us, length us, event | category | flops | bytes accessed | tf_op | source)
XLA Modules:
  0.0 310.4 jit_solution(16817055039875950359)
XLA Ops:
  1.3 2.4 pack_0.1.refs_0_.refs_11_
  3.7 5.1 %collective-permute-start.2 = (bf16[2,80,256]{2,1,0:T(8,128)(2,1)}, bf16[2,80,256]{2,1,0:T(8,128)(2,1)S(1)}, u32[]{:S(2)}, u32[]{:S(2)}) collective-permute-start(bf16[2,80,256]{2,1,0:T(8,128)(2,1)} %pack_0.1.refs_0_.refs_11_), channel_id=1, source_target_pairs={{0,6},{1,7},{2,0},{3,1},{4,2},{5,3},{6,4},{7,5},{8,14},{9,15},{10,... | collective-permute-start | bytes 245768 | tf_op jit(solution)/shard_map/ppermute | solution.py:787
  9.8 2.1 collective-permute-done.2.refs_3_
  12.0 4.6 %collective-permute-done.1.refs_2_ = bf16[2,80,256]{2,1,0:T(8,128)(2,1)S(1)} collective-permute-done((bf16[2,80,256]{2,1,0:T(8,128)(2,1)}, bf16[2,80,256]{2,1,0:T(8,128)(2,1)S(1)}, u32[]{:S(2)}, u32[]{:S(2)}) %collective-permute-start.1) | collective-permute-done | bytes 81952 | tf_op jit(solution)/shard_map/ppermute | solution.py:787
  17.8 2.7 join_ring_0.1
  20.6 1.6 collective-permute-start.3
  23.6 2.1 collective-permute-start.9
  29.8 1.6 collective-permute-start.5
  31.8 4.5 %collective-permute-done.8.refs_2_ = bf16[2,128,256]{2,1,0:T(8,128)(2,1)S(1)} collective-permute-done((bf16[2,128,256]{2,1,0:T(8,128)(2,1)}, bf16[2,128,256]{2,1,0:T(8,128)(2,1)S(1)}, u32[]{:S(2)}, u32[]{:S(2)}) %collective-permute-start.8) | collective-permute-done | bytes 131104 | tf_op jit(solution)/shard_map/ppermute | solution.py:787
  41.5 2.2 assemble_0.1
  46.5 2.2 collective-permute-done.13.refs_3_
  50.8 11.5 %attention_forward_0.1 = (f32[4,272,512]{2,1,0:T(8,128)S(1)}, bf16[4,272,512]{2,1,0:T(8,128)(2,1)S(1)}, bf16[4,272,1536]{2,1,0:T(8,128)(2,1)S(1)}, f32[4,16,256]...) custom-call(s32[4]{0:T(128)S(1)} %copy-done.31, bf16[4,16,256]{2,1,0:T(8,128)(2,1)S(1)} %copy-done.23, ...), custom_call_target="tpu_custom_call" | custom-call | flops 49999998976 | bytes 100000000 | tf_op jit(solution)/shard_map/attention_forward_0/pallas_call | solution.py:97
  63.3 1.9 collective-permute-done.17.refs_2_
  71.3 8.6 %collective-permute-done.22.refs_3_ = bf16[4,224,256]{2,1,0:T(8,128)(2,1)S(1)} collective-permute-done((bf16[4,224,256]{2,1,0:T(8,128)(2,1)S(1)}, bf16[4,224,256]{2,1,0:T(8,128)(2,1)S(1)}, u32[]{:S(2)}, u32[]{:S(2)}) %collective-permute-start.22) | collective-permute-done | bytes 458784 | tf_op jit(solution)/shard_map/ppermute | solution.py:787
  81.2 1.5 collective-permute-start.23
  82.7 9.8 %mlp_forward_0.1 = (bf16[1088,512]{1,0:T(8,128)(2,1)S(1)}, bf16[1088,2048]{1,0:T(8,128)(2,1)S(1)}, bf16[1088,2048]{1,0:T(8,128)(2,1)S(1)}, f32[1088,512]{1,0:T(8,128)S(1)}) custom-call(f32[1088,512]{1,0:T(8,128)S(1)} %bitcast.25, f32[24,512]{1,0:T(8,128)S(1)} %copy-done.83, bf16[512,2048]{1,0:T(8,128)(2,1)S(1)} %get-tuple-element.171.refs_4_.refs_2_.refs_7_, ...), custom_call_target="tpu_custom_call" | custom-call | flops 49999998976 | bytes 100000000 | tf_op jit(solution)/shard_map/mlp_forward_0/pallas_call | solution.py:97
  92.6 1.9 copy-done.42
  96.4 4.9 %collective-permute-done.24.refs_1_.refs_4_ = bf16[2,4,224,256]{3,2,1,0:T(8,128)(2,1)S(1)} collective-permute-done((bf16[2,4,224,256]{3,2,1,0:T(8,128)(2,1)S(1)}, bf16[2,4,224,256]{3,2,1,0:T(8,128)(2,1)S(1)}, u32[]{:S(2)}, u32[]{:S(2)}) %collective-permute-start.24) | collective-permute-done | bytes 917536 | tf_op jit(solution)/shard_map/ppermute | solution.py:787
  102.3 3.8 %collective-permute-done.26.refs_6_ = bf16[2,2,4,224,256]{4,3,2,1,0:T(8,128)(2,1)S(1)} collective-permute-done((bf16[2,2,4,224,256]{4,3,2,1,0:T(8,128)(2,1)S(1)}, bf16[2,2,4,224,256]{4,3,2,1,0:T(8,128)(2,1)S(1)}, u32[]{:S(2)}, u32[]{:S(2)}) %collective-permute-start.26) | collective-permute-done | bytes 1835040 | tf_op jit(solution)/shard_map/ppermute | solution.py:787
  107.4 11.8 %attention_forward_1.1 = (f32[4,272,512]{2,1,0:T(8,128)S(1)}, bf16[4,272,512]{2,1,0:T(8,128)(2,1)S(1)}, bf16[4,272,1536]{2,1,0:T(8,128)(2,1)S(1)}, f32[4,16,256]...) custom-call(f32[4,272,512]{2,1,0:T(8,128)S(1)} %bitcast.27, ...), custom_call_target="tpu_custom_call" | custom-call | flops 49999998976 | bytes 100000000 | tf_op jit(solution)/shard_map/attention_forward_1/pallas_call | solution.py:97
  119.3 1.8 copy-done.44
  121.1 14.2 %mlp_forward_1.1 = (bf16[1088,512]{1,0:T(8,128)(2,1)S(1)}, bf16[1088,2048]{1,0:T(8,128)(2,1)S(1)}, bf16[1088,2048]{1,0:T(8,128)(2,1)S(1)}, f32[1088,512]{1,0:T(8...) custom-call(f32[1,1]{1,0:T(1,128)} %get-tuple-element.159.refs_0_, s32[4]{0:T(128)S(1)} %copy-done.30, ...), custom_call_target="tpu_custom_call" | custom-call | flops 49999998976 | bytes 100000000 | tf_op jit(solution)/shard_map/mlp_forward_1/pallas_call | solution.py:97
  135.3 2.0 copy-done.40
  137.4 2.0 copy-done.41
  142.0 1.6 copy-done.57
  143.6 1.6 copy-done.59
  145.2 16.6 %mlp_backward_1.1 = (f32[1088,512]{1,0:T(8,128)}, bf16[2,2,2,4,128,256]{5,4,3,2,1,0:T(8,128)(2,1)S(1)}, bf16[2,2,2,4,128,256]{5,4,3,2,1,0:T(8,128)(2,1)S(1)}, f32[8,512]{1,0:T(8,128)S(1)}, f32[1,2048]{1,0:T(1,128)S(1)}) custom-call(s32[4]{0:T(128)S(1)} %copy-done.2, f32[1088,512]{1,0:T(8,128)} %copy-done.51, bf16[1088,2048]{1,0:T(8,128)(2,1)} %copy-done.40, ...), custom_call_target="tpu_custom_call" | custom-call | flops 49999998976 | bytes 100000000 | tf_op jit(solution)/shard_map/mlp_backward_1/pallas_call | solution.py:97
  165.7 23.4 %attention_backward_1.1 = (bf16[2,2,2,4,96,256]{5,4,3,2,1,0:T(8,128)(2,1)S(1)}, bf16[2,2,2,4,96,256]{5,4,3,2,1,0:T(8,128)(2,1)S(1)}, f32[4,272,512]{2,1,0:T(8,12...) custom-call(s32[4]{0:T(128)S(1)} %copy-done.2, f32[4,272,512]{2,1,0:T(8,128)} %bitcast.33, f32[4,272,512]{2,1,0:T(8,128)} %copy-done.50, ...), custom_call_target="tpu_custom_call" | custom-call | flops 49999998976 | bytes 100000000 | tf_op jit(solution)/shard_map/attention_backward_1/pallas_call | solution.py:97
  189.5 3.1 collective-permute-done.28.refs_3_
  192.6 1.7 add_core_1.1
  194.3 1.5 collective-permute-start.30
  196.4 16.2 %mlp_backward_0.1 = (f32[1088,512]{1,0:T(8,128)}, bf16[2,2,2,4,128,256]{5,4,3,2,1,0:T(8,128)(2,1)S(1)}, bf16[2,2,2,4,128,256]{5,4,3,2,1,0:T(8,128)(2,1)S(1)}, f32[8,512]{1,0:T(8,128)S(1)}, f32[1,2048]{1,0:T(1,128)S(1)}) custom-call(s32[4]{0:T(128)S(1)} %copy-done.2, f32[1088,512]{1,0:T(8,128)} %bitcast.30, bf16[1088,2048]{1,0:T(8,128)(2,1)} %copy-done.42, ...), custom_call_target="tpu_custom_call" | custom-call | flops 49999998976 | bytes 100000000 | tf_op jit(solution)/shard_map/mlp_backward_0/pallas_call | solution.py:97
  212.6 4.3 %collective-permute-done.30.refs_1_ = bf16[2,4,224,256]{3,2,1,0:T(8,128)(2,1)S(1)} collective-permute-done((bf16[2,4,224,256]{3,2,1,0:T(8,128)(2,1)S(1)}, bf16[2,4,224,256]{3,2,1,0:T(8,128)(2,1)S(1)}, u32[]{:S(2)}, u32[]{:S(2)}) %collective-permute-start.30) | collective-permute-done | bytes 917536 | tf_op jit(solution)/shard_map/ppermute | solution.py:787
  218.2 1.6 copy-done.35
  226.6 20.1 %attention_backward_0.1 = (bf16[2,2,2,4,80,256]{5,4,3,2,1,0:T(8,128)(2,1)S(1)}, bf16[2,2,2,4,80,256]{5,4,3,2,1,0:T(8,128)(2,1)S(1)}) custom-call(s32[4]{0:T(128)S(1)} %copy-done.2, f32[4,272,512]{2,1,0:T(8,128)S(1)} %bitcast.29, f32[4,272,512]{2,1,0:T(8,128)S(1)} %copy-done.49, bf16[4,272,512]{2,1,0:T(8,128)(2,1)S(1)} %copy-done.73, ...), custom_call_target="tpu_custom_call" | custom-call | flops 49999998976 | bytes 100000000 | tf_op jit(solution)/shard_map/attention_backward_0/pallas_call | solution.py:97
  249.4 2.9 collective-permute-start.46
  252.9 1.5 collective-permute-start.36
  257.5 4.1 %collective-permute-done.36.refs_1_ = bf16[4,128,256]{2,1,0:T(8,128)(2,1)S(1)} collective-permute-done((bf16[4,128,256]{2,1,0:T(8,128)(2,1)S(1)}, bf16[4,128,256]{2,1,0:T(8,128)(2,1)S(1)}, u32[]{:S(2)}, u32[]{:S(2)}) %collective-permute-start.36) | collective-permute-done | bytes 262176 | tf_op jit(solution)/shard_map/ppermute | solution.py:787
  268.5 3.8 %collective-permute-done.42.refs_1_ = bf16[2,4,80,256]{3,2,1,0:T(8,128)(2,1)S(1)} collective-permute-done((bf16[2,4,80,256]{3,2,1,0:T(8,128)(2,1)S(1)}, bf16[2,4,80,256]{3,2,1,0:T(8,128)(2,1)S(1)}, u32[]{:S(2)}, u32[]{:S(2)}) %collective-permute-start.42) | collective-permute-done | bytes 327712 | tf_op jit(solution)/shard_map/ppermute | solution.py:787
  273.1 1.5 collective-permute-start.47
  276.4 2.0 collective-permute-start.40
  278.5 4.0 %collective-permute-start.41 = (bf16[2,128,256]{2,1,0:T(8,128)(2,1)S(1)}, bf16[2,128,256]{2,1,0:T(8,128)(2,1)S(1)}, u32[]{:S(2)}, u32[]{:S(2)}) collective-permute-start(bf16[2,128,256]{2,1,0:T(8,128)(2,1)S(1)} %get-tuple-element.238), channel_id=1, source_target_pairs={{0,6},{1,7},{2,0},{3,1},{4,2},{5,3},{6,4},{7,5},{8,14},{9,15},{10,... | collective-permute-start | bytes 393224 | tf_op jit(solution)/shard_map/ppermute | solution.py:787
  283.5 2.1 collective-permute-start.49
  285.5 2.4 collective-permute-start.50
  287.9 3.1 %collective-permute-start.51 = (bf16[2,80,256]{2,1,0:T(8,128)(2,1)S(1)}, bf16[2,80,256]{2,1,0:T(8,128)(2,1)S(1)}, u32[]{:S(2)}, u32[]{:S(2)}) collective-permute-start(bf16[2,80,256]{2,1,0:T(8,128)(2,1)S(1)} %get-tuple-element.252), channel_id=1, source_target_pairs={{0,6},{1,7},{2,0},{3,1},{4,2},{5,3},{6,4},{7,5},{8,14},{9,15},{10,... | collective-permute-start | bytes 245768 | tf_op jit(solution)/shard_map/ppermute | solution.py:787
  291.1 4.5 %skip.1 = (f32[2,256,512]{2,1,0:T(8,128)}, f32[2,256,512]{2,1,0:T(8,128)}, f32[2,256,512]{2,1,0:T(8,128)}, bf16[2,256,512]{2,1,0:T(8,128)(2,1)}, f32[2,64,4096]{...) custom-call(s32[4]{0:T(128)S(1)} %copy-done.2, ...), custom_call_target="tpu_custom_call" | custom-call | flops 49999998976 | bytes 100000000 | tf_op jit(solution)/shard_map/skip/pallas_call | solution.py:97
  299.5 4.6 %collective-permute-done.55.refs_2_ = bf16[2,208,256]{2,1,0:T(8,128)(2,1)S(1)} collective-permute-done((bf16[2,208,256]{2,1,0:T(8,128)(2,1)S(1)}, bf16[2,208,256]{2,1,0:T(8,128)(2,1)S(1)}, u32[]{:S(2)}, u32[]{:S(2)}) %collective-permute-start.55) | collective-permute-done | bytes 213024 | tf_op jit(solution)/shard_map/ppermute | solution.py:787
  305.6 4.5 %vectors.1 = (f32[2,256,512]{2,1,0:T(8,128)}, f32[2,256,512]{2,1,0:T(8,128)}, f32[2,256,512]{2,1,0:T(8,128)}, bf16[2,256,512]{2,1,0:T(8,128)(2,1)}, f32[2,64,409...) custom-call(s32[4]{0:T(128)S(1)} %copy-done.2, ...), custom_call_target="tpu_custom_call", output_to_operand_aliasing={{0}: (17, {}), {1}: (18, {}), {2}: (19, {}), {3}: (20, {}),... | custom-call | flops 49999998976 | bytes 100000000 | tf_op jit(solution)/shard_map/vectors/pallas_call | solution.py:97
  (296 shorter events, 69.0 us)
Async XLA Ops:
  3.7 8.3 %collective-permute-start.2 = (bf16[2,80,256]{2,1,0:T(8,128)(2,1)}, bf16[2,80,256]{2,1,0:T(8,128)(2,1)S(1)}, u32[]{:S(2)}, u32[]{:S(2)}) collective-permute-start(bf16[2,80,256]{2,1,0:T(8,128)(2,1)} %pack_0.1.refs_0_.refs_11_), channel_id=1, source_target_pairs={{0,6},{1,7},{2,0},{3,1},{4,2},{5,3},{6,4},{7,5},{8,14},{9,15},{10,... | collective-permute-start | bytes 245768 | tf_op jit(solution)/shard_map/ppermute | solution.py:787
  8.8 7.7 %collective-permute-start.1 = (bf16[2,80,256]{2,1,0:T(8,128)(2,1)}, bf16[2,80,256]{2,1,0:T(8,128)(2,1)S(1)}, u32[]{:S(2)}, u32[]{:S(2)}) collective-permute-start(bf16[2,80,256]{2,1,0:T(8,128)(2,1)} %pack_0.1.refs_0_.refs_11_), channel_id=1, source_target_pairs={{0,4},{1,5},{2,6},{3,7},{4,0},{5,1},{6,2},{7,3},{8,12},{9,13},{10,... | collective-permute-start | bytes 245768 | tf_op jit(solution)/shard_map/ppermute | solution.py:787
  8.8 7.7 %collective-permute-start = (bf16[2,80,256]{2,1,0:T(8,128)(2,1)}, bf16[2,80,256]{2,1,0:T(8,128)(2,1)S(1)}, u32[]{:S(2)}, u32[]{:S(2)}) collective-permute-start(bf16[2,80,256]{2,1,0:T(8,128)(2,1)} %pack_0.1.refs_0_.refs_11_), channel_id=1, source_target_pairs={{0,2},{1,3},{2,4},{3,5},{4,6},{5,7},{6,0},{7,1},{8,10},{9,11},{10,... | collective-permute-start | bytes 245768 | tf_op jit(solution)/shard_map/ppermute | solution.py:787
  20.6 6.6 %collective-permute-start.3 = (bf16[4,80,256]{2,1,0:T(8,128)(2,1)}, bf16[4,80,256]{2,1,0:T(8,128)(2,1)S(1)}, u32[]{:S(2)}, u32[]{:S(2)}) collective-permute-start(bf16[4,80,256]{2,1,0:T(8,128)(2,1)} %get-tuple-element.152.refs_0_.refs_4_), channel_id=1, source_target_pairs={{0,1},{1,0},{2,3},{3,2},{4,5},{5,4},{6,7},{7,6},{8,9},{9,8},{10,11... | collective-permute-start | bytes 491528 | tf_op jit(solution)/shard_map/ppermute | solution.py:787
  22.2 5.7 %collective-permute-start.4 = (bf16[4,80,256]{2,1,0:T(8,128)(2,1)}, bf16[4,80,256]{2,1,0:T(8,128)(2,1)S(1)}, u32[]{:S(2)}, u32[]{:S(2)}) collective-permute-start(bf16[4,80,256]{2,1,0:T(8,128)(2,1)} %get-tuple-element.153.refs_2_), channel_id=1, source_target_pairs={{0,16},{1,17},{2,18},{3,19},{4,20},{5,21},{6,22},{7,23},{8,24},{9,... | collective-permute-start | bytes 491528 | tf_op jit(solution)/shard_map/ppermute | solution.py:787
  23.6 8.2 %collective-permute-start.9 = (bf16[2,128,256]{2,1,0:T(8,128)(2,1)}, bf16[2,128,256]{2,1,0:T(8,128)(2,1)S(1)}, u32[]{:S(2)}, u32[]{:S(2)}) collective-permute-start(bf16[2,128,256]{2,1,0:T(8,128)(2,1)} %get-tuple-element.156.refs_0_), channel_id=1, source_target_pairs={{0,6},{1,7},{2,0},{3,1},{4,2},{5,3},{6,4},{7,5},{8,14},{9,15},{10,... | collective-permute-start | bytes 393224 | tf_op jit(solution)/shard_map/ppermute | solution.py:787
  25.8 10.6 %collective-permute-start.8 = (bf16[2,128,256]{2,1,0:T(8,128)(2,1)}, bf16[2,128,256]{2,1,0:T(8,128)(2,1)S(1)}, u32[]{:S(2)}, u32[]{:S(2)}) collective-permute-start(bf16[2,128,256]{2,1,0:T(8,128)(2,1)} %get-tuple-element.156.refs_0_), channel_id=1, source_target_pairs={{0,4},{1,5},{2,6},{3,7},{4,0},{5,1},{6,2},{7,3},{8,12},{9,13},{10,... | collective-permute-start | bytes 393224 | tf_op jit(solution)/shard_map/ppermute | solution.py:787
  25.8 10.6 %collective-permute-start.7 = (bf16[2,128,256]{2,1,0:T(8,128)(2,1)}, bf16[2,128,256]{2,1,0:T(8,128)(2,1)S(1)}, u32[]{:S(2)}, u32[]{:S(2)}) collective-permute-start(bf16[2,128,256]{2,1,0:T(8,128)(2,1)} %get-tuple-element.156.refs_0_), channel_id=1, source_target_pairs={{0,2},{1,3},{2,4},{3,5},{4,6},{5,7},{6,0},{7,1},{8,10},{9,11},{10,... | collective-permute-start | bytes 393224 | tf_op jit(solution)/shard_map/ppermute | solution.py:787
  29.8 8.2 %collective-permute-start.5 = (bf16[2,4,80,256]{3,2,1,0:T(8,128)(2,1)S(1)}, bf16[2,4,80,256]{3,2,1,0:T(8,128)(2,1)S(1)}, u32[]{:S(2)}, u32[]{:S(2)}) collective-permute-start(bf16[2,4,80,256]{3,2,1,0:T(8,128)(2,1)S(1)} %get-tuple-element.154.refs_4_.refs_6_.refs_1_), channel_id=1, source_target_pairs={{0,16},{1,17},{2,18},{3,19},{4,20},{5,21},{6,22},{7,23},{8,24},{9,... | collective-permute-start | bytes 983048 | tf_op jit(solution)/shard_map/ppermute | solution.py:787
  31.3 7.8 %collective-permute-start.6 = (bf16[2,4,80,256]{3,2,1,0:T(8,128)(2,1)S(1)}, bf16[2,4,80,256]{3,2,1,0:T(8,128)(2,1)S(1)}, u32[]{:S(2)}, u32[]{:S(2)}) collective-permute-start(bf16[2,4,80,256]{3,2,1,0:T(8,128)(2,1)S(1)} %get-tuple-element.155.refs_5_.refs_3_), channel_id=1, source_target_pairs={{0,1},{1,0},{2,3},{3,2},{4,5},{5,4},{6,7},{7,6},{8,9},{9,8},{10,11... | collective-permute-start | bytes 983048 | tf_op jit(solution)/shard_map/ppermute | solution.py:787
  40.0 8.6 %collective-permute-start.12 = (bf16[4,128,256]{2,1,0:T(8,128)(2,1)S(1)}, bf16[4,128,256]{2,1,0:T(8,128)(2,1)S(1)}, u32[]{:S(2)}, u32[]{:S(2)}) collective-permute-start(bf16[4,128,256]{2,1,0:T(8,128)(2,1)S(1)} %get-tuple-element.158.refs_2_.refs_0_), channel_id=1, source_target_pairs={{0,1},{1,0},{2,3},{3,2},{4,5},{5,4},{6,7},{7,6},{8,9},{9,8},{10,11... | collective-permute-start | bytes 786440 | tf_op jit(solution)/shard_map/ppermute | solution.py:787
  40.7 8.0 %collective-permute-start.13 = (bf16[4,128,256]{2,1,0:T(8,128)(2,1)S(1)}, bf16[4,128,256]{2,1,0:T(8,128)(2,1)S(1)}, u32[]{:S(2)}, u32[]{:S(2)}) collective-permute-start(bf16[4,128,256]{2,1,0:T(8,128)(2,1)S(1)} %get-tuple-element.163.refs_2_), channel_id=1, source_target_pairs={{0,16},{1,17},{2,18},{3,19},{4,20},{5,21},{6,22},{7,23},{8,24},{9,... | collective-permute-start | bytes 786440 | tf_op jit(solution)/shard_map/ppermute | solution.py:787
  43.7 19.6 %collective-permute-start.18 = (bf16[2,224,256]{2,1,0:T(8,128)(2,1)S(1)}, bf16[2,224,256]{2,1,0:T(8,128)(2,1)S(1)}, u32[]{:S(2)}, u32[]{:S(2)}) collective-permute-start(bf16[2,224,256]{2,1,0:T(8,128)(2,1)S(1)} %get-tuple-element.167.refs_0_), channel_id=1, source_target_pairs={{0,6},{1,7},{2,0},{3,1},{4,2},{5,3},{6,4},{7,5},{8,14},{9,15},{10,... | collective-permute-start | bytes 688136 | tf_op jit(solution)/shard_map/ppermute | solution.py:787
  44.9 20.3 %collective-permute-start.17 = (bf16[2,224,256]{2,1,0:T(8,128)(2,1)S(1)}, bf16[2,224,256]{2,1,0:T(8,128)(2,1)S(1)}, u32[]{:S(2)}, u32[]{:S(2)}) collective-permute-start(bf16[2,224,256]{2,1,0:T(8,128)(2,1)S(1)} %get-tuple-element.167.refs_0_), channel_id=1, source_target_pairs={{0,4},{1,5},{2,6},{3,7},{4,0},{5,1},{6,2},{7,3},{8,12},{9,13},{10,... | collective-permute-start | bytes 688136 | tf_op jit(solution)/shard_map/ppermute | solution.py:787
  45.5 19.7 %collective-permute-start.16 = (bf16[2,224,256]{2,1,0:T(8,128)(2,1)S(1)}, bf16[2,224,256]{2,1,0:T(8,128)(2,1)S(1)}, u32[]{:S(2)}, u32[]{:S(2)}) collective-permute-start(bf16[2,224,256]{2,1,0:T(8,128)(2,1)S(1)} %get-tuple-element.167.refs_0_), channel_id=1, source_target_pairs={{0,2},{1,3},{2,4},{3,5},{4,6},{5,7},{6,0},{7,1},{8,10},{9,11},{10,... | collective-permute-start | bytes 688136 | tf_op jit(solution)/shard_map/ppermute | solution.py:787
  48.7 17.3 %collective-permute-start.15 = (bf16[2,4,128,256]{3,2,1,0:T(8,128)(2,1)S(1)}, bf16[2,4,128,256]{3,2,1,0:T(8,128)(2,1)S(1)}, u32[]{:S(2)}, u32[]{:S(2)}) collective-permute-start(bf16[2,4,128,256]{3,2,1,0:T(8,128)(2,1)S(1)} %get-tuple-element.166.refs_5_.refs_3_), channel_id=1, source_target_pairs={{0,1},{1,0},{2,3},{3,2},{4,5},{5,4},{6,7},{7,6},{8,9},{9,8},{10,11... | collective-permute-start | bytes 1572872 | tf_op jit(solution)/shard_map/ppermute | solution.py:787
  50.2 15.8 %collective-permute-start.14 = (bf16[2,4,128,256]{3,2,1,0:T(8,128)(2,1)S(1)}, bf16[2,4,128,256]{3,2,1,0:T(8,128)(2,1)S(1)}, u32[]{:S(2)}, u32[]{:S(2)}) collective-permute-start(bf16[2,4,128,256]{3,2,1,0:T(8,128)(2,1)S(1)} %get-tuple-element.164.refs_6_.refs_4_.refs_1_), channel_id=1, source_target_pairs={{0,16},{1,17},{2,18},{3,19},{4,20},{5,21},{6,22},{7,23},{8,24},{9,... | collective-permute-start | bytes 1572872 | tf_op jit(solution)/shard_map/ppermute | solution.py:787
  66.7 13.1 %collective-permute-start.21 = (bf16[4,224,256]{2,1,0:T(8,128)(2,1)S(1)}, bf16[4,224,256]{2,1,0:T(8,128)(2,1)S(1)}, u32[]{:S(2)}, u32[]{:S(2)}) collective-permute-start(bf16[4,224,256]{2,1,0:T(8,128)(2,1)S(1)} %get-tuple-element.170.refs_2_.refs_0_), channel_id=1, source_target_pairs={{0,1},{1,0},{2,3},{3,2},{4,5},{5,4},{6,7},{7,6},{8,9},{9,8},{10,11... | collective-permute-start | bytes 1376264 | tf_op jit(solution)/shard_map/ppermute | solution.py:787
  67.6 12.2 %collective-permute-start.22 = (bf16[4,224,256]{2,1,0:T(8,128)(2,1)S(1)}, bf16[4,224,256]{2,1,0:T(8,128)(2,1)S(1)}, u32[]{:S(2)}, u32[]{:S(2)}) collective-permute-start(bf16[4,224,256]{2,1,0:T(8,128)(2,1)S(1)} %get-tuple-element.173.refs_2_), channel_id=1, source_target_pairs={{0,16},{1,17},{2,18},{3,19},{4,20},{5,21},{6,22},{7,23},{8,24},{9,... | collective-permute-start | bytes 1376264 | tf_op jit(solution)/shard_map/ppermute | solution.py:787
  80.0 21.2 %collective-permute-start.24 = (bf16[2,4,224,256]{3,2,1,0:T(8,128)(2,1)S(1)}, bf16[2,4,224,256]{3,2,1,0:T(8,128)(2,1)S(1)}, u32[]{:S(2)}, u32[]{:S(2)}) collective-permute-start(bf16[2,4,224,256]{3,2,1,0:T(8,128)(2,1)S(1)} %get-tuple-element.176.refs_1_.refs_3_), channel_id=1, source_target_pairs={{0,1},{1,0},{2,3},{3,2},{4,5},{5,4},{6,7},{7,6},{8,9},{9,8},{10,11... | collective-permute-start | bytes 2752520 | tf_op jit(solution)/shard_map/ppermute | solution.py:787
  81.2 20.9 %collective-permute-start.23 = (bf16[2,4,224,256]{3,2,1,0:T(8,128)(2,1)S(1)}, bf16[2,4,224,256]{3,2,1,0:T(8,128)(2,1)S(1)}, u32[]{:S(2)}, u32[]{:S(2)}) collective-permute-start(bf16[2,4,224,256]{3,2,1,0:T(8,128)(2,1)S(1)} %get-tuple-element.174.refs_4_.refs_0_.refs_1_), channel_id=1, source_target_pairs={{0,16},{1,17},{2,18},{3,19},{4,20},{5,21},{6,22},{7,23},{8,24},{9,... | collective-permute-start | bytes 2752520 | tf_op jit(solution)/shard_map/ppermute | solution.py:787
  96.4 5.9 %collective-permute-start.25 = (bf16[2,2,4,224,256]{4,3,2,1,0:T(8,128)(2,1)S(1)}, bf16[2,2,4,224,256]{4,3,2,1,0:T(8,128)(2,1)S(1)}, u32[]{:S(2)}, u32[]{:S(2)}) collective-permute-start(bf16[2,2,4,224,256]{4,3,2,1,0:T(8,128)(2,1)S(1)} %join_own_2.1.refs_2_), channel_id=1, source_target_pairs={{0,8},{1,9},{2,10},{3,11},{4,12},{5,13},{6,14},{7,15},{8,0},{9,1},... | collective-permute-start | bytes 5505032 | tf_op jit(solution)/shard_map/ppermute | solution.py:787
  163.1 29.5 %collective-permute-start.27 = (bf16[2,2,2,4,128,256]{5,4,3,2,1,0:T(8,128)(2,1)S(1)}, bf16[2,2,2,4,128,256]{5,4,3,2,1,0:T(8,128)(2,1)S(1)}, u32[]{:S(2)}, u32[]{:S(2)}) collective-permute-start(bf16[2,2,2,4,128,256]{5,4,3,2,1,0:T(8,128)(2,1)S(1)} %get-tuple-element.198), channel_id=1, source_target_pairs={{0,8},{1,9},{2,10},{3,11},{4,12},{5,13},{6,14},{7,15},{8,0},{9,1},... | collective-permute-start | bytes 6291464 | tf_op jit(solution)/shard_map/ppermute | solution.py:787
  194.3 22.7 %collective-permute-start.30 = (bf16[2,4,224,256]{3,2,1,0:T(8,128)(2,1)S(1)}, bf16[2,4,224,256]{3,2,1,0:T(8,128)(2,1)S(1)}, u32[]{:S(2)}, u32[]{:S(2)}) collective-permute-start(bf16[2,4,224,256]{3,2,1,0:T(8,128)(2,1)S(1)} %get-tuple-element.203), channel_id=1, source_target_pairs={{0,16},{1,17},{2,18},{3,19},{4,20},{5,21},{6,22},{7,23},{8,24},{9,... | collective-permute-start | bytes 2752520 | tf_op jit(solution)/shard_map/ppermute | solution.py:787
  195.8 22.3 %collective-permute-start.31 = (bf16[2,4,224,256]{3,2,1,0:T(8,128)(2,1)S(1)}, bf16[2,4,224,256]{3,2,1,0:T(8,128)(2,1)S(1)}, u32[]{:S(2)}, u32[]{:S(2)}) collective-permute-start(bf16[2,4,224,256]{3,2,1,0:T(8,128)(2,1)S(1)} %get-tuple-element.205), channel_id=1, source_target_pairs={{0,1},{1,0},{2,3},{3,2},{4,5},{5,4},{6,7},{7,6},{8,9},{9,8},{10,11... | collective-permute-start | bytes 2752520 | tf_op jit(solution)/shard_map/ppermute | solution.py:787
  212.6 9.5 %collective-permute-start.29 = (bf16[2,2,2,4,128,256]{5,4,3,2,1,0:T(8,128)(2,1)S(1)}, bf16[2,2,2,4,128,256]{5,4,3,2,1,0:T(8,128)(2,1)S(1)}, u32[]{:S(2)}, u32[]{:S(2)}) collective-permute-start(bf16[2,2,2,4,128,256]{5,4,3,2,1,0:T(8,128)(2,1)S(1)} %get-tuple-element.202), channel_id=1, source_target_pairs={{0,8},{1,9},{2,10},{3,11},{4,12},{5,13},{6,14},{7,15},{8,0},{9,1},... | collective-permute-start | bytes 6291464 | tf_op jit(solution)/shard_map/ppermute | solution.py:787
  220.6 26.1 %collective-permute-start.34 = (bf16[4,224,256]{2,1,0:T(8,128)(2,1)S(1)}, bf16[4,224,256]{2,1,0:T(8,128)(2,1)S(1)}, u32[]{:S(2)}, u32[]{:S(2)}) collective-permute-start(bf16[4,224,256]{2,1,0:T(8,128)(2,1)S(1)} %get-tuple-element.212), channel_id=1, source_target_pairs={{0,1},{1,0},{2,3},{3,2},{4,5},{5,4},{6,7},{7,6},{8,9},{9,8},{10,11... | collective-permute-start | bytes 1376264 | tf_op jit(solution)/shard_map/ppermute | solution.py:787
  221.2 25.5 %collective-permute-start.35 = (bf16[4,224,256]{2,1,0:T(8,128)(2,1)S(1)}, bf16[4,224,256]{2,1,0:T(8,128)(2,1)S(1)}, u32[]{:S(2)}, u32[]{:S(2)}) collective-permute-start(bf16[4,224,256]{2,1,0:T(8,128)(2,1)S(1)} %get-tuple-element.214), channel_id=1, source_target_pairs={{0,16},{1,17},{2,18},{3,19},{4,20},{5,21},{6,22},{7,23},{8,24},{9,... | collective-permute-start | bytes 1376264 | tf_op jit(solution)/shard_map/ppermute | solution.py:787
  223.2 29.1 %collective-permute-start.32 = (bf16[2,4,128,256]{3,2,1,0:T(8,128)(2,1)S(1)}, bf16[2,4,128,256]{3,2,1,0:T(8,128)(2,1)S(1)}, u32[]{:S(2)}, u32[]{:S(2)}) collective-permute-start(bf16[2,4,128,256]{3,2,1,0:T(8,128)(2,1)S(1)} %get-tuple-element.209), channel_id=1, source_target_pairs={{0,16},{1,17},{2,18},{3,19},{4,20},{5,21},{6,22},{7,23},{8,24},{9,... | collective-permute-start | bytes 1572872 | tf_op jit(solution)/shard_map/ppermute | solution.py:787
  224.4 27.9 %collective-permute-start.33 = (bf16[2,4,128,256]{3,2,1,0:T(8,128)(2,1)S(1)}, bf16[2,4,128,256]{3,2,1,0:T(8,128)(2,1)S(1)}, u32[]{:S(2)}, u32[]{:S(2)}) collective-permute-start(bf16[2,4,128,256]{3,2,1,0:T(8,128)(2,1)S(1)} %get-tuple-element.211), channel_id=1, source_target_pairs={{0,1},{1,0},{2,3},{3,2},{4,5},{5,4},{6,7},{7,6},{8,9},{9,8},{10,11... | collective-permute-start | bytes 1572872 | tf_op jit(solution)/shard_map/ppermute | solution.py:787
  247.6 17.7 %collective-permute-start.44 = (bf16[2,224,256]{2,1,0:T(8,128)(2,1)}, bf16[2,224,256]{2,1,0:T(8,128)(2,1)}, u32[]{:S(2)}, u32[]{:S(2)}) collective-permute-start(bf16[2,224,256]{2,1,0:T(8,128)(2,1)} %get-tuple-element.242), channel_id=1, source_target_pairs={{0,2},{1,3},{2,4},{3,5},{4,6},{5,7},{6,0},{7,1},{8,10},{9,11},{10,... | collective-permute-start | bytes 688136 | tf_op jit(solution)/shard_map/ppermute | solution.py:787
  248.0 18.0 %collective-permute-start.45 = (bf16[2,224,256]{2,1,0:T(8,128)(2,1)}, bf16[2,224,256]{2,1,0:T(8,128)(2,1)}, u32[]{:S(2)}, u32[]{:S(2)}) collective-permute-start(bf16[2,224,256]{2,1,0:T(8,128)(2,1)} %get-tuple-element.243), channel_id=1, source_target_pairs={{0,4},{1,5},{2,6},{3,7},{4,0},{5,1},{6,2},{7,3},{8,12},{9,13},{10,... | collective-permute-start | bytes 688136 | tf_op jit(solution)/shard_map/ppermute | solution.py:787
  249.4 16.5 %collective-permute-start.46 = (bf16[2,224,256]{2,1,0:T(8,128)(2,1)}, bf16[2,224,256]{2,1,0:T(8,128)(2,1)}, u32[]{:S(2)}, u32[]{:S(2)}) collective-permute-start(bf16[2,224,256]{2,1,0:T(8,128)(2,1)} %get-tuple-element.244), channel_id=1, source_target_pairs={{0,6},{1,7},{2,0},{3,1},{4,2},{5,3},{6,4},{7,5},{8,14},{9,15},{10,... | collective-permute-start | bytes 688136 | tf_op jit(solution)/shard_map/ppermute | solution.py:787
  252.9 8.8 %collective-permute-start.36 = (bf16[4,128,256]{2,1,0:T(8,128)(2,1)S(1)}, bf16[4,128,256]{2,1,0:T(8,128)(2,1)S(1)}, u32[]{:S(2)}, u32[]{:S(2)}) collective-permute-start(bf16[4,128,256]{2,1,0:T(8,128)(2,1)S(1)} %get-tuple-element.230), channel_id=1, source_target_pairs={{0,1},{1,0},{2,3},{3,2},{4,5},{5,4},{6,7},{7,6},{8,9},{9,8},{10,11... | collective-permute-start | bytes 786440 | tf_op jit(solution)/shard_map/ppermute | solution.py:787
  255.4 8.3 %collective-permute-start.37 = (bf16[4,128,256]{2,1,0:T(8,128)(2,1)S(1)}, bf16[4,128,256]{2,1,0:T(8,128)(2,1)S(1)}, u32[]{:S(2)}, u32[]{:S(2)}) collective-permute-start(bf16[4,128,256]{2,1,0:T(8,128)(2,1)S(1)} %get-tuple-element.232), channel_id=1, source_target_pairs={{0,16},{1,17},{2,18},{3,19},{4,20},{5,21},{6,22},{7,23},{8,24},{9,... | collective-permute-start | bytes 786440 | tf_op jit(solution)/shard_map/ppermute | solution.py:787
  261.6 10.6 %collective-permute-start.42 = (bf16[2,4,80,256]{3,2,1,0:T(8,128)(2,1)S(1)}, bf16[2,4,80,256]{3,2,1,0:T(8,128)(2,1)S(1)}, u32[]{:S(2)}, u32[]{:S(2)}) collective-permute-start(bf16[2,4,80,256]{3,2,1,0:T(8,128)(2,1)S(1)} %get-tuple-element.239), channel_id=1, source_target_pairs={{0,16},{1,17},{2,18},{3,19},{4,20},{5,21},{6,22},{7,23},{8,24},{9,... | collective-permute-start | bytes 983048 | tf_op jit(solution)/shard_map/ppermute | solution.py:787
  263.7 9.0 %collective-permute-start.43 = (bf16[2,4,80,256]{3,2,1,0:T(8,128)(2,1)S(1)}, bf16[2,4,80,256]{3,2,1,0:T(8,128)(2,1)S(1)}, u32[]{:S(2)}, u32[]{:S(2)}) collective-permute-start(bf16[2,4,80,256]{3,2,1,0:T(8,128)(2,1)S(1)} %get-tuple-element.241), channel_id=1, source_target_pairs={{0,1},{1,0},{2,3},{3,2},{4,5},{5,4},{6,7},{7,6},{8,9},{9,8},{10,11... | collective-permute-start | bytes 983048 | tf_op jit(solution)/shard_map/ppermute | solution.py:787
  267.2 9.2 %collective-permute-start.52 = (bf16[2,224,256]{2,1,0:T(8,128)(2,1)S(1)}, bf16[2,224,256]{2,1,0:T(8,128)(2,1)S(1)}, u32[]{:S(2)}, u32[]{:S(2)}) collective-permute-start(bf16[2,224,256]{2,1,0:T(8,128)(2,1)S(1)} %add_last_1.1.refs_4_.refs_1_), channel_id=1, source_target_pairs={{0,16},{1,17},{2,18},{3,19},{4,20},{5,21},{6,22},{7,23},{8,24},{9,... | collective-permute-start | bytes 688136 | tf_op jit(solution)/shard_map/ppermute | solution.py:787
  274.6 7.9 %collective-permute-start.48 = (bf16[4,80,256]{2,1,0:T(8,128)(2,1)S(1)}, bf16[4,80,256]{2,1,0:T(8,128)(2,1)S(1)}, u32[]{:S(2)}, u32[]{:S(2)}) collective-permute-start(bf16[4,80,256]{2,1,0:T(8,128)(2,1)S(1)} %get-tuple-element.248), channel_id=1, source_target_pairs={{0,16},{1,17},{2,18},{3,19},{4,20},{5,21},{6,22},{7,23},{8,24},{9,... | collective-permute-start | bytes 491528 | tf_op jit(solution)/shard_map/ppermute | solution.py:787
  275.2 10.3 %collective-permute-start.53 = (bf16[2,224,256]{2,1,0:T(8,128)(2,1)S(1)}, bf16[2,224,256]{2,1,0:T(8,128)(2,1)S(1)}, u32[]{:S(2)}, u32[]{:S(2)}) collective-permute-start(bf16[2,224,256]{2,1,0:T(8,128)(2,1)S(1)} %add_last_1.1.refs_4_.refs_1_), channel_id=1, source_target_pairs={{0,8},{1,9},{2,10},{3,11},{4,12},{5,13},{6,14},{7,15},{8,0},{9,1},... | collective-permute-start | bytes 688136 | tf_op jit(solution)/shard_map/ppermute | solution.py:787
  275.2 8.2 %collective-permute-start.39 = (bf16[2,128,256]{2,1,0:T(8,128)(2,1)S(1)}, bf16[2,128,256]{2,1,0:T(8,128)(2,1)S(1)}, u32[]{:S(2)}, u32[]{:S(2)}) collective-permute-start(bf16[2,128,256]{2,1,0:T(8,128)(2,1)S(1)} %get-tuple-element.236), channel_id=1, source_target_pairs={{0,2},{1,3},{2,4},{3,5},{4,6},{5,7},{6,0},{7,1},{8,10},{9,11},{10,... | collective-permute-start | bytes 393224 | tf_op jit(solution)/shard_map/ppermute | solution.py:787
  276.4 19.2 %collective-permute-start.40 = (bf16[2,128,256]{2,1,0:T(8,128)(2,1)S(1)}, bf16[2,128,256]{2,1,0:T(8,128)(2,1)S(1)}, u32[]{:S(2)}, u32[]{:S(2)}) collective-permute-start(bf16[2,128,256]{2,1,0:T(8,128)(2,1)S(1)} %get-tuple-element.237), channel_id=1, source_target_pairs={{0,4},{1,5},{2,6},{3,7},{4,0},{5,1},{6,2},{7,3},{8,12},{9,13},{10,... | collective-permute-start | bytes 393224 | tf_op jit(solution)/shard_map/ppermute | solution.py:787
  278.5 17.1 %collective-permute-start.41 = (bf16[2,128,256]{2,1,0:T(8,128)(2,1)S(1)}, bf16[2,128,256]{2,1,0:T(8,128)(2,1)S(1)}, u32[]{:S(2)}, u32[]{:S(2)}) collective-permute-start(bf16[2,128,256]{2,1,0:T(8,128)(2,1)S(1)} %get-tuple-element.238), channel_id=1, source_target_pairs={{0,6},{1,7},{2,0},{3,1},{4,2},{5,3},{6,4},{7,5},{8,14},{9,15},{10,... | collective-permute-start | bytes 393224 | tf_op jit(solution)/shard_map/ppermute | solution.py:787
  282.5 5.4 %collective-permute-start.54 = (bf16[2,224,256]{2,1,0:T(8,128)(2,1)S(1)}, bf16[2,224,256]{2,1,0:T(8,128)(2,1)S(1)}, u32[]{:S(2)}, u32[]{:S(2)}) collective-permute-start(bf16[2,224,256]{2,1,0:T(8,128)(2,1)S(1)} %collective-permute-done.52.refs_2_), channel_id=1, source_target_pairs={{0,8},{1,9},{2,10},{3,11},{4,12},{5,13},{6,14},{7,15},{8,0},{9,1},... | collective-permute-start | bytes 688136 | tf_op jit(solution)/shard_map/ppermute | solution.py:787
  283.5 12.2 %collective-permute-start.49 = (bf16[2,80,256]{2,1,0:T(8,128)(2,1)S(1)}, bf16[2,80,256]{2,1,0:T(8,128)(2,1)S(1)}, u32[]{:S(2)}, u32[]{:S(2)}) collective-permute-start(bf16[2,80,256]{2,1,0:T(8,128)(2,1)S(1)} %get-tuple-element.250), channel_id=1, source_target_pairs={{0,2},{1,3},{2,4},{3,5},{4,6},{5,7},{6,0},{7,1},{8,10},{9,11},{10,... | collective-permute-start | bytes 245768 | tf_op jit(solution)/shard_map/ppermute | solution.py:787
  285.5 11.3 %collective-permute-start.50 = (bf16[2,80,256]{2,1,0:T(8,128)(2,1)S(1)}, bf16[2,80,256]{2,1,0:T(8,128)(2,1)S(1)}, u32[]{:S(2)}, u32[]{:S(2)}) collective-permute-start(bf16[2,80,256]{2,1,0:T(8,128)(2,1)S(1)} %get-tuple-element.251), channel_id=1, source_target_pairs={{0,4},{1,5},{2,6},{3,7},{4,0},{5,1},{6,2},{7,3},{8,12},{9,13},{10,... | collective-permute-start | bytes 245768 | tf_op jit(solution)/shard_map/ppermute | solution.py:787
  287.9 8.9 %collective-permute-start.51 = (bf16[2,80,256]{2,1,0:T(8,128)(2,1)S(1)}, bf16[2,80,256]{2,1,0:T(8,128)(2,1)S(1)}, u32[]{:S(2)}, u32[]{:S(2)}) collective-permute-start(bf16[2,80,256]{2,1,0:T(8,128)(2,1)S(1)} %get-tuple-element.252), channel_id=1, source_target_pairs={{0,6},{1,7},{2,0},{3,1},{4,2},{5,3},{6,4},{7,5},{8,14},{9,15},{10,... | collective-permute-start | bytes 245768 | tf_op jit(solution)/shard_map/ppermute | solution.py:787
  298.2 5.9 %collective-permute-start.55 = (bf16[2,208,256]{2,1,0:T(8,128)(2,1)S(1)}, bf16[2,208,256]{2,1,0:T(8,128)(2,1)S(1)}, u32[]{:S(2)}, u32[]{:S(2)}) collective-permute-start(bf16[2,208,256]{2,1,0:T(8,128)(2,1)S(1)} %add_last_0.1.refs_1_.refs_25_), channel_id=1, source_target_pairs={{0,16},{1,17},{2,18},{3,19},{4,20},{5,21},{6,22},{7,23},{8,24},{9,... | collective-permute-start | bytes 638984 | tf_op jit(solution)/shard_map/ppermute | solution.py:787
  (103 other events, 610.6 us)
